TPU v7x, 32 devices: a whole 2x2x4 slice. The times are simulated.
32 devices in a mesh: row: 8 (over y, x, core), col: 4 (over z).
Axes of the slice: x: 2, y: 2, z: 4, core: 2. Of those that a mesh axis runs over, the one named last changes fastest.
Arguments:
- amplitudes: float32 [32, 4, 512, 512], P('row', None, 'col'), may hold values from -6 to 6
- integrals: float32 [4, 512, 32, 512], P(None, 'row', 'col'), may hold values from -0.125 to 0.125
- occ_energy: float32 [32], replicated, may hold values from -1.5 to -0.3
- vir_energy: float32 [512], replicated, may hold values from 0.2 to 3
Outputs:
- update: float32 [32, 32, 512, 512], P('row', None, 'col')
All inputs are finite; a program needn't handle non-finite values.
Results may differ from a plain program's by a relative error of at most 0.00007.
Values sent between devices are 32-bit elements; how exact they have to be, the bound alone decides.
No kernel may reach another device: no remote copies, remote signals or barrier semaphores. Data moves between devices by JAX's collectives and lax.ppermute only.
A program may use at most 192 MiB of HBM per device.

v0:
```python
import jax
import jax.numpy as jnp
from jax import lax
from jax.sharding import PartitionSpec as P


def body(amplitudes, integrals, occ_energy, vir_energy):
    moved = lax.all_to_all(amplitudes, "col", split_axis=3, concat_axis=2, tiled=True)
    panel = lax.all_gather(moved, "col", axis=3, tiled=True)
    rows_i = panel.shape[0]
    cycle = jnp.einsum(
        "ikac,kcjb->ijab",
        panel,
        lax.all_gather(integrals, "row", axis=1, tiled=True),
        precision=lax.Precision.HIGHEST,
    )
    back = lax.all_to_all(cycle, "col", split_axis=2, concat_axis=1, tiled=True)
    a_local = back.shape[2]
    occ_local = lax.dynamic_slice_in_dim(occ_energy, lax.axis_index("row") * rows_i, rows_i, 0)
    vir_local = lax.dynamic_slice_in_dim(vir_energy, lax.axis_index("col") * a_local, a_local, 0)
    denom = (
        occ_local[:, None, None, None]
        + occ_energy[None, :, None, None]
        - vir_local[None, None, :, None]
        - vir_energy[None, None, None, :]
    )
    return back / denom


def solution(mesh):
    return jax.shard_map(
        body,
        mesh=mesh,
        in_specs=(P("row", None, "col", None), P(None, "row", "col", None), P(), P()),
        out_specs=P("row", None, "col", None),
        check_vma=False,
    )
```

profile of v0, /device:TPU:0, one launch (start us, length us, event | category | flops | bytes accessed | tf_op | source)
XLA Modules:
  0.0 1811.6 jit_solution(18370049312721297832)
XLA Ops:
  6.5 0.0 all-gather.5.cloned.1.call-start
  6.5 5.4 copy.9
  12.0 100.5 %all_to_all.36 = f32[4,4,128,512]{2,1,0,3:T(4,128)} all-to-all(f32[4,4,128,512]{2,1,0,3:T(4,128)} %copy.9), channel_id=1, replica_groups=mesh['row'=8,'col'=4] {'col'}, dimensions={3} | all-to-all | bytes 8388608 | tf_op jit(solution)/shard_map/all_to_all | solution.py:8
  112.5 5.2 copy.10
  117.7 0.0 all-gather.5.cloned.1.call-update
  117.7 0.0 all-gather.3.cloned.1.call-start
  117.8 6.7 copy.8
  124.5 0.0 all-gather.3.cloned.1.call-update
  124.6 278.7 %all-gather.5.cloned.1.call-done = f32[4,4,512,512]{3,2,1,0:T(8,128)} async-done(((f32[4,4,512,128]{3,2,1,0:T(8,128)}), f32[4,4,512,512]{3,2,1,0:T(8,128)}) %all-gather.5.cloned.1.call-update) | async-done | bytes 16777232 | tf_op jit(solution)/shard_map/all_gather | solution.py:9
  403.3 160.9 %all-gather.3.cloned.1.call-done = f32[4,512,8,512]{3,1,0,2:T(8,128)} async-done(((f32[4,64,8,512]{3,1,0,2:T(8,128)}), f32[4,512,8,512]{3,1,0,2:T(8,128)}) %all-gather.3.cloned.1.call-update) | async-done | bytes 33554448 | tf_op jit(solution)/shard_map/all_gather | solution.py:14
  564.2 428.2 %fusion.3 = f32[4,8,512,512]{2,3,0,1:T(8,128)} fusion(f32[4,4,512,512]{3,2,1,0:T(8,128)} %all-gather.5.cloned.1.call-done, f32[4,512,8,512]{3,1,0,2:T(8,128)} %all-gather.3.cloned.1.call-done), kind=kOutput, calls=%fused_computation.4 | convolution fusion | flops 206158430208 | bytes 83886080 | tf_op jit(solution)/shard_map/ikac,kcjb->ijab/dot_general | solution.py:11
  992.4 39.1 %copy.11 = f32[4,8,512,512]{3,0,1,2:T(4,128)} copy(f32[4,8,512,512]{2,3,0,1:T(8,128)} %fusion.3) | data formatting | bytes 67108864 | tf_op jit(solution)/shard_map/ikac,kcjb->ijab/transpose | solution.py:11
  1031.5 0.0 copy-start
  1031.5 0.0 copy-start.1
  1031.5 9.9 all-to-all-start.1
  1041.4 0.0 copy-done
  1041.4 0.1 dynamic_slice.7
  1041.5 0.0 copy-done.1
  1041.5 0.1 dynamic_slice.6
  1041.5 0.1 broadcast_add_fusion
  1041.6 0.1 broadcast_subtract_fusion
  1041.7 722.7 %all-to-all-done.1 = f32[4,8,512,512]{3,0,1,2:T(4,128)} async-done(((f32[4,8,512,512]{3,0,1,2:T(4,128)}), f32[4,8,512,512]{3,0,1,2:T(4,128)}, u32[]{:S(2)}, u32[]{:S(2)}) %all-to-all-start.1) | async-done | bytes 33554464 | tf_op jit(solution)/shard_map/all_to_all | solution.py:17
  1764.5 28.3 %copy.12 = f32[4,4,8,128,512]{4,3,2,1,0:T(8,128)S(1)} copy(f32[4,4,8,128,512]{4,0,2,3,1:T(4,128)} %bitcast.10) | data formatting | bytes 67108864 | tf_op jit(solution)/shard_map/all_to_all | solution.py:17
  1792.8 12.0 subtract_divide_fusion
Async XLA Ops:
  6.5 396.8 %all-gather.5.cloned.1.call-start = ((), (), s32[]{:S(2)}) async-start(), calls=%async_computation.3 | async-start | bytes 20971520 | tf_op jit(solution)/shard_map/all_gather | solution.py:9
  117.7 446.5 %all-gather.3.cloned.1.call-start = ((), (), s32[]{:S(2)}) async-start(), calls=%async_computation.2 | async-start | bytes 37748736 | tf_op jit(solution)/shard_map/all_gather | solution.py:14
  1031.5 9.9 copy-start
  1031.5 10.0 copy-start.1
  1031.5 732.9 %all-to-all-start.1 = ((f32[4,8,512,512]{3,0,1,2:T(4,128)}), f32[4,8,512,512]{3,0,1,2:T(4,128)}, u32[]{:S(2)}, u32[]{:S(2)}) async-start(f32[4,8,512,512]{3,0,1,2:T(4,128)} %copy.11), calls=%async_computation.1 | async-start | bytes 67108864 | tf_op jit(solution)/shard_map/all_to_all | solution.py:17
Sparse Core Ops, SparseCore 0:
  117.9 285.3 all-gather.4
  405.2 158.9 all-gather.2
where the time goes:
time: 1810 us
  waiting for transfers between devices  1160 us (64%)
  matrix products  428 us (24%)
  blocking collectives  101 us (6%)
  local copies, waits for them, and re-layouts  85 us (5%)
    all_to_all x1, waiting for transfers between devices, body(): back = lax.all_to_all(cycle, 'col', split_axis=2, concat_axis=1, tiled=True)  723 us
    dot_general x1, matrix products, body(): jnp.einsum('ikac,kcjb->ijab', panel, lax.all_gather(integrals, 'row', axi...  428 us
    all_gather x1, waiting for transfers between devices, body(): panel = lax.all_gather(moved, 'col', axis=3, tiled=True)  279 us
    all_gather x1, waiting for transfers between devices, body(): lax.all_gather(integrals, 'row', axis=1, tiled=True)  161 us
    all_to_all x1, blocking collectives, body(): lax.all_to_all(amplitudes, 'col', split_axis=3, concat_axis=2, tiled=True)  101 us
    transpose x1, local copies, waits for them, and re-layouts, body(): jnp.einsum('ikac,kcjb->ijab', panel, lax.all_gather(integrals, 'row', axi...  39.1 us
  transfers between devices with their start and end apart: 3, of which 3 were waited for; matrix products, arithmetic and copies ran while one was open for 0% of the time, Pallas kernels for 0%

commit v1 on v0

v1 whole, which is shorter than its diff:
```python
import functools

import jax
import jax.numpy as jnp
from jax import lax
from jax.experimental import pallas as pl
from jax.experimental.pallas import tpu as pltpu
from jax.sharding import PartitionSpec as P

AXES = ("row", "col")

HBM = pl.BlockSpec(memory_space=pl.ANY)
VMEM = 58 * 2**20


def streamed(amplitudes, integrals, occ_energy, vir_energy):
    planes = lax.axis_size("col")
    plane = lax.axis_index("col")
    rows_i, _, rows_a, _ = amplitudes.shape
    cols_j, cols_b = integrals.shape[2:]
    occ_i = lax.dynamic_slice_in_dim(occ_energy, lax.axis_index("row") * rows_i, rows_i, 0)
    vir_a = lax.dynamic_slice_in_dim(vir_energy, plane * rows_a, rows_a, 0)
    ring = [(z, (z + 1) % planes) for z in range(planes)]

    def step(s, carry):
        block, out = carry
        q = lax.rem(plane - s + planes, planes)
        panel = lax.all_gather(block, "row", axis=1, tiled=True)
        cycle = jnp.einsum("ikac,kcjb->ijab", amplitudes, panel, precision=lax.Precision.HIGHEST)
        occ_j = lax.dynamic_slice_in_dim(occ_energy, q * cols_j, cols_j, 0)
        denom = (
            occ_i[:, None, None, None]
            + occ_j[None, :, None, None]
            - vir_a[None, None, :, None]
            - vir_energy[None, None, None, :]
        )
        out = lax.dynamic_update_slice_in_dim(out, cycle / denom, q * cols_j, 1)
        return lax.ppermute(block, "col", ring), out

    out = jnp.zeros((rows_i, occ_energy.shape[0], rows_a, cols_b), jnp.float32)
    return lax.fori_loop(0, planes, step, (integrals, out))[1]


def split(value):
    high = value.astype(jnp.bfloat16)
    return high, (value - high.astype(jnp.float32)).astype(jnp.bfloat16)


def columns_kernel(core_ref, block, out):
    for j in range(block.shape[2]):
        to = j ^ (core_ref[0] * (block.shape[2] // 2))
        out[pl.ds(to, 1), 0] = block[0, :, j, :][None]


def columns(integrals, core):
    ks, cs, js, width = integrals.shape
    return pl.pallas_call(
        columns_kernel,
        grid_spec=pltpu.PrefetchScalarGridSpec(
            num_scalar_prefetch=1,
            grid=(ks,),
            in_specs=[pl.BlockSpec((1, cs, js, width), lambda k, _: (k, 0, 0, 0))],
            out_specs=pl.BlockSpec((js, 1, cs, width), lambda k, _: (0, k, 0, 0)),
        ),
        out_shape=jax.ShapeDtypeStruct((js, ks, cs, width), jnp.float32),
        compiler_params=pltpu.CompilerParams(vmem_limit_bytes=VMEM),
    )(core.reshape(1), integrals)


def merge_kernel(core_ref, mine, other, *refs):
    outs = refs[:-1]
    t, cs, per = pl.program_id(0), mine.shape[2], 2
    for n, out in enumerate(outs):

        @pl.when((t >= n * per) & (t < (n + 1) * per))
        def _(out=out):
            for source, at in ((mine, core_ref[0]), (other, 1 - core_ref[0])):
                out[0, :, pl.ds(pl.multiple_of(at * cs, cs), cs), :] = source[0]


def merge(ordered, other, core, room):
    parts, ks, cs, width = other.shape
    block = (1, ks, cs, width)
    pairs = parts // 2
    return pl.pallas_call(
        merge_kernel,
        grid_spec=pltpu.PrefetchScalarGridSpec(
            num_scalar_prefetch=1,
            grid=(parts,),
            in_specs=[pl.BlockSpec(block, lambda t, _: (t, 0, 0, 0))] * 2,
            out_specs=[
                pl.BlockSpec((1, ks, 2 * cs, width), lambda t, _, n=n: (jnp.clip(t - 2 * n, 0, 1), 0, 0, 0))
                for n in range(pairs)
            ]
            + [HBM],
        ),
        out_shape=[jax.ShapeDtypeStruct((2, ks, 2 * cs, width), jnp.float32)] * pairs
        + [jax.ShapeDtypeStruct(room, jnp.float32)],
        compiler_params=pltpu.CompilerParams(vmem_limit_bytes=VMEM),
    )(core.reshape(1), ordered, other)


def rows_kernel(starts, chip_ref, *refs):
    sources, (high, low) = refs[:-2], refs[-2:]
    step = pl.program_id(0)
    for source, (first, count) in zip(sources, starts):

        @pl.when((step >= first) & (step < first + count))
        def _(source=source):
            ks = source.shape[1]
            n = source.shape[3] // 4
            for m in range(4):
                at = pl.ds(pl.multiple_of((chip_ref[0] ^ m) * n, n), n)
                for k in range(ks):
                    to = pl.ds((m * ks + k) * n, n)
                    high[:, to], low[:, to] = split(source[0, k, :, at])


def rows(values, chip):
    starts, first = [], 0
    for v in values:
        starts.append((first, v.shape[0]))
        first += v.shape[0]
    _, ks, rows_a, depth = values[0].shape
    shape = jax.ShapeDtypeStruct((first * rows_a, ks * depth), jnp.bfloat16)
    return pl.pallas_call(
        functools.partial(rows_kernel, starts),
        grid_spec=pltpu.PrefetchScalarGridSpec(
            num_scalar_prefetch=1,
            grid=(first,),
            in_specs=[
                pl.BlockSpec((1, ks, rows_a, depth), lambda s, _, a=a, n=n: (jnp.clip(s - a, 0, n - 1), 0, 0, 0))
                for a, n in starts
            ],
            out_specs=[pl.BlockSpec((rows_a, ks * depth), lambda s, _: (s, 0))] * 2,
        ),
        out_shape=[shape, shape],
        compiler_params=pltpu.CompilerParams(vmem_limit_bytes=VMEM),
    )(chip.reshape(1), *values)


def product_kernel(chunks, places, mode, added, meta, occ, a_hi, a_lo, rowd, vir, *refs):
    pieces, refs = refs[: len(chunks)], refs[len(chunks) :]
    if added:
        start, refs = refs[0], refs[1:]
    if mode == "own":
        gots, refs = refs[:places], refs[places + 1 :]
        out, send, b_hi, b_lo, own, own_sem, got_sem = refs
    elif mode == "lent":
        own, send, b_hi, b_lo = refs
    else:
        part, b_hi, b_lo = refs
    block, step, tiles = pl.program_id(0), pl.program_id(1), pl.num_programs(1)
    half = tiles // 2
    ks, n = pieces[0].shape[1:3]
    tile_i = a_hi.shape[0] // 128

    def got_copy(m):
        return pltpu.make_async_copy(gots[m].at[0], out.at[:, meta[2 + 2 * m] + block], got_sem.at[m])

    def own_copy(s):
        rows_at = pl.ds(s * tile_i, tile_i)
        return pltpu.make_async_copy(own.at[rows_at], out.at[rows_at, meta[1] + block], own_sem.at[s])

    if mode == "own":

        @pl.when(step == 0)
        def _():
            for m in range(places):
                pl.when(meta[3 + 2 * m] == 1)(lambda m=m: got_copy(m).start())

    @pl.when(meta[0] == 1)
    def _():
        @pl.when(step == 0)
        def _():
            for m, piece in enumerate(pieces):
                for k in range(ks):
                    at = pl.ds((m * ks + k) * n, n)
                    b_hi[at, :], b_lo[at, :] = split(piece[0, k])

        cols = slice(0, len(chunks) * ks * n)
        dot = functools.partial(jnp.dot, preferred_element_type=jnp.float32)
        high, low = a_hi[:, cols], a_lo[:, cols]
        value = dot(low, b_hi[...]) + dot(high, b_lo[...]) + dot(high, b_hi[...])
        if added:
            value = value + start[0]
        if mode == "part":
            part[0] = value
        else:
            wide = jnp.concatenate([rowd[...]] * (value.shape[1] // 128), axis=1)
            value = value / (wide + occ[meta[1] + block] - vir[...])
            value = value.reshape(tile_i, 128, value.shape[1])

            @pl.when(step < half)
            def _():
                if mode == "lent":
                    own[0] = value
                else:
                    own[pl.ds(step * tile_i, tile_i)] = value
                    own_copy(step).start()

            @pl.when(step >= half)
            def _():
                send[0] = value

        if mode == "own":

            @pl.when(step == tiles - 1)
            def _():
                for s in range(2):
                    own_copy(s).wait()

    if mode == "own":

        @pl.when(step == tiles - 1)
        def _():
            for m in range(places):
                pl.when(meta[3 + 2 * m] == 1)(lambda m=m: got_copy(m).wait())


def product(rows_in, pieces, run, j, occ, vir, mode="own", chunks=(0, 1, 2, 3), added=None, out=None, gots=()):
    a_hi, a_lo, rowd = rows_in
    size = a_hi.shape[0]
    _, ks, n, width = pieces[0].shape
    depth = len(chunks) * ks * n
    whole = a_hi.shape[1]
    tiles, i_own = 4, size // 256
    tall = size // tiles
    tile_i = tall // 128
    assert tiles == 4 and i_own == 2 * tile_i
    block = jax.ShapeDtypeStruct((2, i_own, 128, width), jnp.float32)
    meta = jnp.stack([jnp.asarray(v, jnp.int32) for v in (run, j, *[v for _, at, keep in gots for v in (at, keep)])])
    args = [meta, occ, a_hi, a_lo, rowd, vir, *pieces]
    if chunks[0] == 0:
        a_spec = pl.BlockSpec((tall, whole), lambda b, s, *_: (s, 0))
    else:
        a_spec = pl.BlockSpec((tall, depth), lambda b, s, *_: (s, chunks[0]))
    specs = [a_spec, a_spec, pl.BlockSpec((tall, 128), lambda b, s, *_: (s, 0))]
    specs += [pl.BlockSpec(vir.shape, lambda b, s, *_: (0, 0))]
    specs += [pl.BlockSpec((1, ks, n, width), lambda b, s, *_: (b, 0, 0, 0))] * len(pieces)
    part_spec = pl.BlockSpec((1, tall, width), lambda b, s, *_: (b, s, 0))
    if added is not None:
        args.append(added)
        specs.append(part_spec)
    own_spec = pl.BlockSpec((1, tile_i, 128, width), lambda b, s, *_: (b, jnp.minimum(s, 1), 0, 0))
    send_spec = pl.BlockSpec((1, tile_i, 128, width), lambda b, s, *_: (b, jnp.maximum(s - 2, 0), 0, 0))
    scratch = [pltpu.VMEM((depth, width), jnp.bfloat16)] * 2
    alias = {}
    if mode == "own":
        args += [*[g for g, _, _ in gots], out]
        specs += [pl.BlockSpec((1, i_own, 128, width), lambda b, s, *_: (b, 0, 0, 0))] * len(gots) + [HBM]
        alias = {len(args) - 1: 0}
        scratch += [pltpu.VMEM(block.shape[1:], jnp.float32)]
        scratch += [pltpu.SemaphoreType.DMA((2,)), pltpu.SemaphoreType.DMA((max(len(gots), 1),))]
        out_specs, out_shape = [HBM, send_spec], [jax.ShapeDtypeStruct(out.shape, out.dtype), block]
    elif mode == "lent":
        out_specs, out_shape = [own_spec, send_spec], [block, block]
    else:
        out_specs, out_shape = part_spec, jax.ShapeDtypeStruct((2, size, width), jnp.float32)
    return pl.pallas_call(
        functools.partial(product_kernel, chunks, len(gots), mode, added is not None),
        grid_spec=pltpu.PrefetchScalarGridSpec(
            num_scalar_prefetch=2, grid=(2, tiles), in_specs=specs, out_specs=out_specs, scratch_shapes=scratch
        ),
        out_shape=out_shape,
        input_output_aliases=alias,
        compiler_params=pltpu.CompilerParams(vmem_limit_bytes=VMEM),
        cost_estimate=pl.CostEstimate(
            flops=12 * size * depth * width, bytes_accessed=8 * size * (depth + width) + 8 * depth * width, transcendentals=0
        ),
    )(*args)


def place_kernel(count, meta, *refs):
    gots, out, sem = refs[:count], refs[count + 1], refs[count + 2]
    for act in ("start", "wait"):
        for n in range(count):
            copy = pltpu.make_async_copy(gots[n].at[0], out.at[:, meta[2 * n] + pl.program_id(0)], sem.at[n])
            pl.when(meta[2 * n + 1] == 1)(getattr(copy, act))


def place(out, gots):
    meta = jnp.stack([jnp.asarray(v, jnp.int32) for _, at, keep in gots for v in (at, keep)])
    return pl.pallas_call(
        functools.partial(place_kernel, len(gots)),
        grid_spec=pltpu.PrefetchScalarGridSpec(
            num_scalar_prefetch=1,
            grid=(2,),
            in_specs=[pl.BlockSpec((1, *g.shape[1:]), lambda b, _: (b, 0, 0, 0)) for g, _, _ in gots] + [HBM],
            out_specs=HBM,
            scratch_shapes=[pltpu.SemaphoreType.DMA((len(gots),))],
        ),
        out_shape=jax.ShapeDtypeStruct(out.shape, out.dtype),
        input_output_aliases={len(gots) + 1: 0},
        compiler_params=pltpu.CompilerParams(vmem_limit_bytes=VMEM),
    )(meta, *[g for g, _, _ in gots], out)


def hop(value, mask=0, planes=None, core=0):
    planes = {z: z for z in range(4)} if planes is None else planes
    flip = 2 * mask + core
    pairs = [(r * 4 + z, (r ^ flip) * 4 + w) for r in range(8) for z, w in planes.items()]
    return lax.ppermute(value, AXES, pairs)


def together(values):
    return lax.optimization_barrier(values)


def body(amplitudes, integrals, occ_energy, vir_energy):
    row, plane = lax.axis_index("row"), lax.axis_index("col")
    core, chip = lax.rem(row, 2), lax.div(row, 2)
    rows_i, ks, rows_a, depth = amplitudes.shape
    cols_j, cols_b = integrals.shape[2:]
    parts = cols_j // 2
    swap, cross = {0: 1, 1: 0, 2: 3, 3: 2}, {1: 2, 2: 1}
    is_end = (plane == 0) | (plane == 3)
    is_mid = ~is_end
    vir = vir_energy.reshape(1, -1)

    def share(plane_of):
        occ = [lax.dynamic_slice_in_dim(occ_energy, r * rows_i, rows_i, 0) for r in (row, row ^ 1)]
        part = lax.dynamic_slice_in_dim(vir_energy, plane_of * rows_a, rows_a, 0)
        rowd = (jnp.concatenate(occ)[:, None] - part[None, :]).reshape(-1, 1)
        return jnp.broadcast_to(rowd, (rowd.shape[0], 128))

    def column(w, pair, of_core):
        return (plane ^ w) * cols_j + of_core * parts + 2 * pair

    def either(at_end, at_mid):
        return jnp.where(is_end, at_end, at_mid)

    def along(x, y, z, mid=None, flip=0):
        got = [hop(x, mask=1), hop(y, mask=2), hop(z, planes=swap, core=flip)]
        return got + [hop(mid, planes=cross)] if mid is not None else got

    ordered = columns(integrals, core)
    room = (rows_i, occ_energy.shape[0], rows_a, cols_b)
    a0, b0, out = merge(ordered, hop(ordered[parts:], core=1), core, room)
    state = dict(out=out, gots=[], sends=[])

    def work(name, rows_in, pieces, w, pair, run=1, **how):
        state["out"], send = product(
            rows_in, pieces, run, column(w, pair, core), occ_energy, vir, out=state["out"], gots=state["gots"], **how
        )
        state["gots"] = []
        state["sends"].append((send, column(w, pair, 1 - core), run))

    def exchange(count=2):
        now, state["sends"] = state["sends"][:count], state["sends"][count:]
        return [(hop(v, core=1), at, keep) for v, at, keep in now]

    def end_round(values, moved=()):
        gots, sends = state["gots"] + list(moved), state["sends"]
        values, new_gots, new_sends, state["out"] = together(
            (values, [g[0] for g in gots], [s[0] for s in sends], state["out"])
        )
        state["gots"] = [(v, *g[1:]) for v, g in zip(new_gots, gots)]
        state["sends"] = [(v, *s[1:]) for v, s in zip(new_sends, sends)]
        return values

    a_other = hop(amplitudes, core=1)
    a0x, b0y, a1, a3m = along(a0, b0, a0, a0)
    v = end_round((amplitudes, a_other, a0, b0, a0x, b0y, a1, a3m))
    amplitudes, a_other, a0, b0, a0x, b0y, a1, a3m = v
    b0x, a0y, ab, a2m = along(b0, a0, either(b0, a3m), a1)
    here = rows([amplitudes, a_other], chip)
    v = end_round((amplitudes, here, a0, b0, a0x, b0y, a1, a3m, b0x, a0y, ab, a2m))
    amplitudes, here, a0, b0, a0x, b0y, a1, a3m, b0x, a0y, ab, a2m = v
    here = (*here, share(plane))
    b0d, a0d, first, b3m = along(b0y, a0x, either(amplitudes[:2], a2m), b0)
    first_other = hop(first, core=1)
    v = end_round((amplitudes, here, a0, b0, a0x, b0y, a1, a3m, b0x, a0y, ab, a2m, b0d, a0d, first, first_other, b3m))
    amplitudes, here, a0, b0, a0x, b0y, a1, a3m, b0x, a0y, ab, a2m, b0d, a0d, first, first_other, b3m = v
    e3, e6 = either(ab, a2m), either(first, ab)
    e3x, e6y, second, b2m = along(e3, e6, either(amplitudes[2:], b3m), ab)
    work("k1", here, (a0, a0x, a0y, a0d), 0, 0)
    work("k2", here, (b0, b0x, b0y, b0d), 0, 1)
    second, state["out"] = together((second, state["out"]))
    second_other = hop(second, core=1)
    v = end_round((here, a0, b0, a0x, b0y, a1, a3m, b0x, a0y, b2m, b0d, a0d, first, first_other, second, second_other, b3m, e3, e6, e3x, e6y))
    here, a0, b0, a0x, b0y, a1, a3m, b0x, a0y, b2m, b0d, a0d, first, first_other, second, second_other, b3m, e3, e6, e3x, e6y = v
    near = (*rows([first, second, first_other, second_other], chip), share(plane ^ 1))
    e4 = either(second, b2m)
    moved = exchange(1)
    e6x, e3y, third, g3x = along(e6, e3, either(a0x, b2m), a0x)
    s_a, l_a = product(near, (a0, a0x, a0y, a0d), is_mid, column(0, 0, core), occ_energy, vir, mode="lent")
    v = end_round((here, near, b0, b0y, a1, a3m, b0x, a0y, b0d, a0d, b3m, e3, e6, e3x, e6y, e4, e6x, e3y, third, g3x, s_a, l_a), moved)
    here, near, b0, b0y, a1, a3m, b0x, a0y, b0d, a0d, b3m, e3, e6, e3x, e6y, e4, e6x, e3y, third, g3x, s_a, l_a = v
    e5 = either(third, b3m)
    moved = exchange(1)
    e6d, e3d, fourth, g3y = along(e6y, e3x, either(a0y, s_a), a0y)
    s_b, l_b = product(near, (b0, b0x, b0y, b0d), is_mid, column(0, 1, core), occ_energy, vir, mode="lent")
    v = end_round((here, a1, a3m, a0d, e3, e6, e3x, e6y, e4, e5, e6x, e3y, third, g3x, e6d, e3d, fourth, g3y, l_a, s_b, l_b), moved)
    here, a1, a3m, a0d, e3, e6, e3x, e6y, e4, e5, e6x, e3y, third, g3x, e6d, e3d, fourth, g3y, l_a, s_b, l_b = v
    state["gots"].append((fourth, column(1, 0, core), is_end))
    e4x, e5y, fifth, g3d = along(e4, e5, either(a0d, s_b), a0d)
    work("k3", here, (e3, e3x, e3y, e3d), 2, 0)
    work("k6", here, (e6, e6x, e6y, e6d), either(3, 1), either(0, 1))
    v = end_round((here, a1, a3m, e4, e5, third, fourth, fifth, g3x, g3y, g3d, l_a, l_b, e4x, e5y))
    here, a1, a3m, e4, e5, third, fourth, fifth, g3x, g3y, g3d, l_a, l_b, e4x, e5y = v
    state["gots"].append((fifth, column(1, 1, core), is_end))
    moved = exchange()
    e5x, e4y, sixth = along(e5, e4, l_a, flip=1)
    work("g1", here, (a1, third, fourth, fifth), 1, 0, is_mid)
    work("g3", here, (a3m, g3x, g3y, g3d), 3, 0, is_mid)
    moved.append((sixth, column(1, 0, 1 - core), is_end))
    v = end_round((here, e4, e5, l_b, e4x, e5y, e5x, e4y), moved)
    here, e4, e5, l_b, e4x, e5y, e5x, e4y = v
    moved = exchange()
    e5d, e4d, seventh = along(e5y, e4x, l_b, flip=1)
    p4 = product(here, (e4, e4x, e4y), 1, column(2, 1, core), occ_energy, vir, mode="part", chunks=(0, 1, 2))
    p5 = product(here, (e5, e5x, e5y), 1, column(3, 1, core), occ_energy, vir, mode="part", chunks=(0, 1, 2))
    moved.append((seventh, column(1, 1, 1 - core), is_end))
    here, e4d, e5d, p4, p5 = end_round((here, e4d, e5d, p4, p5), moved)
    work("k4", here, (e4d,), 2, 1, chunks=(3,), added=p4)
    moved = exchange()
    work("k5", here, (e5d,), 3, 1, chunks=(3,), added=p5)
    return place(state["out"], state["gots"] + moved + exchange())


def solution(mesh):
    planned = mesh.shape["row"] == 8 and mesh.shape["col"] == 4
    return jax.shard_map(
        body if planned else streamed,
        mesh=mesh,
        in_specs=(P("row", None, "col", None), P(None, "row", "col", None), P(), P()),
        out_specs=P("row", None, "col", None),
        check_vma=False,
    )
```

time: 1810 us -> 555 us (0.31)
  waiting for transfers between devices: 1160 us -> 214 us
  matrix products: 428 us -> 0 us
  Pallas kernels: 0 us -> 244 us
  blocking collectives: 101 us -> 0 us
  local copies, waits for them, and re-layouts: 85 us -> 9.38 us
  starting transfers between devices: 9.9 us -> 54.6 us
  other arithmetic: 12.1 us -> 31.2 us
    all_to_all x1 -> x0, waiting for transfers between devices: 723 us -> none  [body(): back = lax.all_to_all(cycle, 'col', split_axis=2, concat_axis=1, tiled=True)]
    all_gather x2 -> x0, waiting for transfers between devices: 440 us -> none  [the longest x1 279 us: body(): panel = lax.all_gather(moved, 'col', axis=3, tiled=True)]
    dot_general x1 -> x0, matrix products: 428 us -> none  [body(): jnp.einsum('ikac,kcjb->ijab', panel, lax.all_gather(integrals, 'row', axi...]
    pallas_call x0 -> x17, Pallas kernels: none -> 244 us  [the longest x12 209 us: product(): pl.pallas_call(functools.partial(product_kernel, chunks, len(gots), mode,...]
    ppermute x0 -> x46, waiting for transfers between devices: none -> 214 us  [hop(): return lax.ppermute(value, AXES, pairs)]
    all_to_all x1 -> x0, blocking collectives: 101 us -> none  [body(): lax.all_to_all(amplitudes, 'col', split_axis=3, concat_axis=2, tiled=True)]
    ppermute x0 -> x46, starting transfers between devices: none -> 54.6 us  [hop(): return lax.ppermute(value, AXES, pairs)]
    transpose x1 -> x0, local copies, waits for them, and re-layouts: 39.1 us -> none  [body(): jnp.einsum('ikac,kcjb->ijab', panel, lax.all_gather(integrals, 'row', axi...]
  transfers between devices with their start and end apart: 3 -> 46, of which waited for: 3 -> 26; matrix products, arithmetic and copies ran while one was open for 0% -> 6% of each run, Pallas kernels for 0% -> 37%
where the time goes in v1:
time: 555 us; the launch traced here: 554 us
  Pallas kernels  244 us (44%)
  waiting for transfers between devices  214 us (39%)
  starting transfers between devices  54.6 us (10%)
  other arithmetic  31.2 us (6%)
  local copies, waits for them, and re-layouts  9.38 us (2%)
    ppermute x46, waiting for transfers between devices, hop(): return lax.ppermute(value, AXES, pairs)  214 us
    pallas_call x12, Pallas kernels, product(): pl.pallas_call(functools.partial(product_kernel, chunks, len(gots), mode,...  209 us
    ppermute x46, starting transfers between devices, hop(): return lax.ppermute(value, AXES, pairs)  54.6 us
    select_n x8, other arithmetic, either(): return jnp.where(is_end, at_end, at_mid)  26.7 us
    pallas_call x2, Pallas kernels, rows(): pl.pallas_call(functools.partial(rows_kernel, starts), grid_spec=pltpu.Pr...  20.2 us
  transfers between devices with their start and end apart: 46, of which 26 were waited for; matrix products, arithmetic and copies ran while one was open for 6% of the time, Pallas kernels for 37%

profile of v1, /device:TPU:0, one launch (start us, length us, event | category | flops | bytes accessed | tf_op | source)
XLA Modules:
  0.0 553.6 jit_solution(6345030295180892939)
XLA Ops:
  7.4 5.9 %collective-permute-done.1.other = f32[4,4,64,512]{3,2,1,0:T(8,128)S(1)} collective-permute-done((f32[4,4,64,512]{3,2,1,0:T(8,128)S(1)}, f32[4,4,64,512]{3,2,1,0:T(8,128)S(1)}, u32[]{:S(2)}, u32[]{:S(2)}) %collective-permute-start.1) | collective-permute-done | bytes 2097184 | tf_op jit(solution)/shard_map/ppermute | solution.py:303
  26.5 42.3 %collective-permute-done.2.refs_1_ = f32[2,4,128,512]{3,2,1,0:T(8,128)} collective-permute-done((f32[2,4,128,512]{3,2,1,0:T(8,128)}, f32[2,4,128,512]{3,2,1,0:T(8,128)}, u32[]{:S(2)}, u32[]{:S(2)}) %collective-permute-start.2) | collective-permute-done | bytes 2097184 | tf_op jit(solution)/shard_map/ppermute | solution.py:303
  82.3 9.6 %shard_map.48 = (bf16[1024,2048]{1,0:T(8,128)(2,1)}, bf16[1024,2048]{1,0:T(8,128)(2,1)}) custom-call(s32[1]{0:T(128)} %bitcast.11.chip_ref, f32[4,4,128,512]{3,2,1,0:T(8,128)} %refs_0_, f32[4,4,128,512]{3,2,1,0:T(8,128)} %collective-permute-done.refs_1_), custom_call_target="tpu_custom_call" | custom-call | tf_op jit(solution)/shard_map/pallas_call | solution.py:126
  91.9 31.1 %collective-permute-done.8 = f32[2,4,128,512]{3,2,1,0:T(8,128)} collective-permute-done((f32[2,4,128,512]{3,2,1,0:T(8,128)}, f32[2,4,128,512]{3,2,1,0:T(8,128)}, u32[]{:S(2)}, u32[]{:S(2)}) %collective-permute-start.8) | collective-permute-done | bytes 2097184 | tf_op jit(solution)/shard_map/ppermute | solution.py:303
  134.8 38.8 %collective-permute-done.12.refs_0_ = f32[2,4,128,512]{3,2,1,0:T(8,128)} collective-permute-done((f32[2,4,128,512]{3,2,1,0:T(8,128)S(1)}, f32[2,4,128,512]{3,2,1,0:T(8,128)}, u32[]{:S(2)}, u32[]{:S(2)}) %collective-permute-start.12) | collective-permute-done | bytes 2097184 | tf_op jit(solution)/shard_map/ppermute | solution.py:303
  181.1 5.1 broadcast_select_fusion.5
  194.0 22.4 %shard_map.49 = (f32[4,32,128,512]{3,2,1,0:T(8,128)}, f32[2,4,128,512]{3,2,1,0:T(8,128)}) custom-call(s32[2]{0:T(128)} %get-tuple-element.424.meta, f32[32]{0:T(128)} %occ.23, bf16[1024,2048]{1,0:T(8,128)(2,1)} %get-tuple-element.393.a_hi, bf16[1024,2048]{1,0:T(8,128)(2,1)} %get-tuple-element.394.a_lo, ...), custom_call_target="tpu_custom_call", output_to_operand_aliasing={{0}: (10, {})} | custom-call | flops 12884901888 | bytes 29360128 | tf_op jit(solution)/shard_map/pallas_call | solution.py:260
  216.3 22.4 %shard_map.50 = (f32[4,32,128,512]{3,2,1,0:T(8,128)}, f32[2,4,128,512]{3,2,1,0:T(8,128)}) custom-call(s32[2]{0:T(128)} %pad_add_fusion.4.meta, f32[32]{0:T(128)} %occ.23, bf16[1024,2048]{1,0:T(8,128)(2,1)} %get-tuple-element.393.a_hi, bf16[1024,2048]{1,0:T(8,128)(2,1)} %get-tuple-element.394.a_lo, ...), custom_call_target="tpu_custom_call", output_to_operand_aliasing={{0}: (10, {})} | custom-call | flops 12884901888 | bytes 29360128 | tf_op jit(solution)/shard_map/pallas_call | solution.py:260
  256.4 10.6 %shard_map.51 = (bf16[1024,2048]{1,0:T(8,128)(2,1)}, bf16[1024,2048]{1,0:T(8,128)(2,1)}) custom-call(s32[1]{0:T(128)} %bitcast.11.chip_ref, f32[2,4,128,512]{3,2,1,0:T(8,128)} %collective-permute-done.12.refs_0_, f32[2,4,128,512]{3,2,1,0:T(8,128)} %copy-done.5, f32[2,4,128,512]{3,2,1,0:T(8,128)} %collective-permute-done.13.refs_2_, f32[2,4,128,512]{3,2,1,0:T(8,128)} %copy-done.9), custom_call_target="tpu_custom_call" | custom-call | tf_op jit(solution)/shard_map/pallas_call | solution.py:126
  268.0 12.9 %shard_map.52 = (f32[2,4,128,512]{3,2,1,0:T(8,128)}, f32[2,4,128,512]{3,2,1,0:T(8,128)}) custom-call(s32[2]{0:T(128)} %pad_add_fusion.9.meta, f32[32]{0:T(128)} %occ.23, bf16[1024,2048]{1,0:T(8,128)(2,1)} %get-tuple-element.311.a_hi, bf16[1024,2048]{1,0:T(8,128)(2,1)} %get-tuple-element.312.a_lo, f32[1024,128]{1,0:T(8,128)} %broadcast_in_dim.5.rowd, ...), custom_call_target="tpu_custom_call" | custom-call | flops 12884901888 | bytes 29360128 | tf_op jit(solution)/shard_map/pallas_call | solution.py:260
  280.8 18.9 %collective-permute-done.22.refs_1_ = f32[2,4,128,512]{3,2,1,0:T(8,128)} collective-permute-done((f32[2,4,128,512]{3,2,1,0:T(8,128)}, f32[2,4,128,512]{3,2,1,0:T(8,128)}, u32[]{:S(2)}, u32[]{:S(2)}) %collective-permute-start.22) | collective-permute-done | bytes 2097184 | tf_op jit(solution)/shard_map/ppermute | solution.py:303
  316.5 12.7 %shard_map.53 = (f32[2,4,128,512]{3,2,1,0:T(8,128)}, f32[2,4,128,512]{3,2,1,0:T(8,128)}) custom-call(s32[2]{0:T(128)} %get-tuple-element.426.meta, f32[32]{0:T(128)} %occ.23, bf16[1024,2048]{1,0:T(8,128)(2,1)} %get-tuple-element.311.a_hi, bf16[1024,2048]{1,0:T(8,128)(2,1)} %get-tuple-element.312.a_lo, f32[1024,128]{1,0:T(8,128)} %broadcast_in_dim.5.rowd, ...), custom_call_target="tpu_custom_call" | custom-call | flops 12884901888 | bytes 29360128 | tf_op jit(solution)/shard_map/pallas_call | solution.py:260
  329.3 23.6 %collective-permute-done.27.refs_6_.refs_2_ = f32[2,4,128,512]{3,2,1,0:T(8,128)} collective-permute-done((f32[2,4,128,512]{3,2,1,0:T(8,128)}, f32[2,4,128,512]{3,2,1,0:T(8,128)}, u32[]{:S(2)}, u32[]{:S(2)}) %collective-permute-start.27) | collective-permute-done | bytes 2097184 | tf_op jit(solution)/shard_map/ppermute | solution.py:303
  364.2 24.6 %shard_map.54 = (f32[4,32,128,512]{3,2,1,0:T(8,128)}, f32[2,4,128,512]{3,2,1,0:T(8,128)}) custom-call(s32[8]{0:T(128)} %stack.141.meta, f32[32]{0:T(128)} %occ.23, bf16[1024,2048]{1,0:T(8,128)(2,1)} %get-tuple-element.393.a_hi, bf16[1024,2048]{1,0:T(8,128)(2,1)} %get-tuple-element.394.a_lo, ...), custom_call_target="tpu_custom_call", output_to_operand_aliasing={{0}: (13, {})} | custom-call | flops 12884901888 | bytes 29360128 | tf_op jit(solution)/shard_map/pallas_call | solution.py:260
  388.8 22.4 %shard_map.55 = (f32[4,32,128,512]{3,2,1,0:T(8,128)}, f32[2,4,128,512]{3,2,1,0:T(8,128)}) custom-call(s32[2]{0:T(128)} %get-tuple-element.423.meta, f32[32]{0:T(128)} %occ.23, bf16[1024,2048]{1,0:T(8,128)(2,1)} %get-tuple-element.393.a_hi, bf16[1024,2048]{1,0:T(8,128)(2,1)} %get-tuple-element.394.a_lo, ...), custom_call_target="tpu_custom_call", output_to_operand_aliasing={{0}: (10, {})} | custom-call | flops 12884901888 | bytes 29360128 | tf_op jit(solution)/shard_map/pallas_call | solution.py:260
  414.4 13.7 %shard_map.56 = (f32[4,32,128,512]{3,2,1,0:T(8,128)}, f32[2,4,128,512]{3,2,1,0:T(8,128)}) custom-call(s32[4]{0:T(128)} %pad_add_fusion.6.meta, f32[32]{0:T(128)} %occ.23, bf16[1024,2048]{1,0:T(8,128)(2,1)} %get-tuple-element.393.a_hi, bf16[1024,2048]{1,0:T(8,128)(2,1)} %get-tuple-element.394.a_lo, ...), custom_call_target="tpu_custom_call", output_to_operand_aliasing={{0}: (11, {})} | custom-call | flops 12884901888 | bytes 29360128 | tf_op jit(solution)/shard_map/pallas_call | solution.py:260
  428.1 12.0 %shard_map.57 = (f32[4,32,128,512]{3,2,1,0:T(8,128)}, f32[2,4,128,512]{3,2,1,0:T(8,128)}) custom-call(s32[2]{0:T(128)} %get-tuple-element.425.meta, f32[32]{0:T(128)} %occ.23, bf16[1024,2048]{1,0:T(8,128)(2,1)} %get-tuple-element.393.a_hi, bf16[1024,2048]{1,0:T(8,128)(2,1)} %get-tuple-element.394.a_lo, ...), custom_call_target="tpu_custom_call", output_to_operand_aliasing={{0}: (10, {})} | custom-call | flops 12884901888 | bytes 29360128 | tf_op jit(solution)/shard_map/pallas_call | solution.py:260
  440.1 15.1 %collective-permute-done.34.refs_1_ = f32[2,4,128,512]{3,2,1,0:T(8,128)} collective-permute-done((f32[2,4,128,512]{3,2,1,0:T(8,128)S(1)}, f32[2,4,128,512]{3,2,1,0:T(8,128)}, u32[]{:S(2)}, u32[]{:S(2)}) %collective-permute-start.34) | collective-permute-done | bytes 2097184 | tf_op jit(solution)/shard_map/ppermute | solution.py:303
  456.4 5.4 collective-permute-done.38.refs_4_
  466.3 18.8 %shard_map.59.refs_1_ = f32[2,1024,512]{2,1,0:T(8,128)} custom-call(s32[2]{0:T(128)} %get-tuple-element.421.meta, f32[32]{0:T(128)} %occ.23, bf16[1024,2048]{1,0:T(8,128)(2,1)} %get-tuple-element.393.a_hi, bf16[1024,2048]{1,0:T(8,128)(2,1)} %get-tuple-element.394.a_lo, f32[1024,128]{1,0:T(8,128)} %broadcast_in_dim.4.rowd, f32[1,512]{1,0:T(1,128)} %bitcast.35, ...), custom_call_target="tpu_custom_call" | custom-call | flops 9663676416 | bytes 23068672 | tf_op jit(solution)/shard_map/pallas_call | solution.py:260
  485.2 18.8 %shard_map.58.refs_1_ = f32[2,1024,512]{2,1,0:T(8,128)} custom-call(s32[2]{0:T(128)} %get-tuple-element.422.meta, f32[32]{0:T(128)} %occ.23, bf16[1024,2048]{1,0:T(8,128)(2,1)} %get-tuple-element.393.a_hi, bf16[1024,2048]{1,0:T(8,128)(2,1)} %get-tuple-element.394.a_lo, f32[1024,128]{1,0:T(8,128)} %broadcast_in_dim.4.rowd, f32[1,512]{1,0:T(1,128)} %bitcast.36, ...), custom_call_target="tpu_custom_call" | custom-call | flops 9663676416 | bytes 23068672 | tf_op jit(solution)/shard_map/pallas_call | solution.py:260
  504.0 5.7 %collective-permute-done.39.refs_0_ = f32[2,4,128,512]{3,2,1,0:T(8,128)S(1)} collective-permute-done((f32[2,4,128,512]{3,2,1,0:T(8,128)}, f32[2,4,128,512]{3,2,1,0:T(8,128)S(1)}, u32[]{:S(2)}, u32[]{:S(2)}) %collective-permute-start.39) | collective-permute-done | bytes 2097184 | tf_op jit(solution)/shard_map/ppermute | solution.py:303
  512.6 16.8 %shard_map.60 = (f32[4,32,128,512]{3,2,1,0:T(8,128)}, f32[2,4,128,512]{3,2,1,0:T(8,128)}) custom-call(s32[14]{0:T(128)} %stack.130.meta, f32[32]{0:T(128)} %occ.23, bf16[1024,2048]{1,0:T(8,128)(2,1)} %get-tuple-element.393.a_hi, bf16[1024,2048]{1,0:T(8,128)(2,1)} %get-tuple-element.394.a_lo, ...), custom_call_target="tpu_custom_call", output_to_operand_aliasing={{0}: (14, {})} | custom-call | flops 3221225472 | bytes 10485760 | tf_op jit(solution)/shard_map/pallas_call | solution.py:260
  529.4 11.5 %shard_map.61 = (f32[4,32,128,512]{3,2,1,0:T(8,128)}, f32[2,4,128,512]{3,2,1,0:T(8,128)}) custom-call(s32[2]{0:T(128)} %get-tuple-element.421.meta, f32[32]{0:T(128)} %occ.23, bf16[1024,2048]{1,0:T(8,128)(2,1)} %get-tuple-element.393.a_hi, bf16[1024,2048]{1,0:T(8,128)(2,1)} %get-tuple-element.394.a_lo, ...), custom_call_target="tpu_custom_call", output_to_operand_aliasing={{0}: (8, {})} | custom-call | flops 3221225472 | bytes 10485760 | tf_op jit(solution)/shard_map/pallas_call | solution.py:260
  (135 shorter events, 132.1 us)
Async XLA Ops:
  7.4 65.1 %collective-permute-start = (f32[4,4,128,512]{3,2,1,0:T(8,128)}, f32[4,4,128,512]{3,2,1,0:T(8,128)}, u32[]{:S(2)}, u32[]{:S(2)}) collective-permute-start(f32[4,4,128,512]{3,2,1,0:T(8,128)} %refs_0_), channel_id=1, source_target_pairs={{0,4},{1,5},{2,6},{3,7},{4,0},{5,1},{6,2},{7,3},{8,12},{9,13},{10,... | collective-permute-start | bytes 12582920 | tf_op jit(solution)/shard_map/ppermute | solution.py:303
  19.7 49.1 %collective-permute-start.2 = (f32[2,4,128,512]{3,2,1,0:T(8,128)}, f32[2,4,128,512]{3,2,1,0:T(8,128)}, u32[]{:S(2)}, u32[]{:S(2)}) collective-permute-start(f32[2,4,128,512]{3,2,1,0:T(8,128)} %get-tuple-element.286.refs_0_), channel_id=1, source_target_pairs={{0,8},{1,9},{2,10},{3,11},{4,12},{5,13},{6,14},{7,15},{8,0},{9,1},... | collective-permute-start | bytes 6291464 | tf_op jit(solution)/shard_map/ppermute | solution.py:303
  22.6 47.7 %collective-permute-start.4 = (f32[2,4,128,512]{3,2,1,0:T(8,128)}, f32[2,4,128,512]{3,2,1,0:T(8,128)}, u32[]{:S(2)}, u32[]{:S(2)}) collective-permute-start(f32[2,4,128,512]{3,2,1,0:T(8,128)} %get-tuple-element.286.refs_0_), channel_id=1, source_target_pairs={{0,1},{1,0},{2,3},{3,2},{4,5},{5,4},{6,7},{7,6},{8,9},{9,8},{10,11... | collective-permute-start | bytes 6291464 | tf_op jit(solution)/shard_map/ppermute | solution.py:303
  24.9 47.5 %collective-permute-start.3 = (f32[2,4,128,512]{3,2,1,0:T(8,128)}, f32[2,4,128,512]{3,2,1,0:T(8,128)}, u32[]{:S(2)}, u32[]{:S(2)}) collective-permute-start(f32[2,4,128,512]{3,2,1,0:T(8,128)} %get-tuple-element.314.refs_0_), channel_id=1, source_target_pairs={{0,16},{1,17},{2,18},{3,19},{4,20},{5,21},{6,22},{7,23},{8,24},{9,... | collective-permute-start | bytes 6291464 | tf_op jit(solution)/shard_map/ppermute | solution.py:303
  72.4 50.6 %collective-permute-start.6 = (f32[2,4,128,512]{3,2,1,0:T(8,128)}, f32[2,4,128,512]{3,2,1,0:T(8,128)}, u32[]{:S(2)}, u32[]{:S(2)}) collective-permute-start(f32[2,4,128,512]{3,2,1,0:T(8,128)} %get-tuple-element.314.refs_0_), channel_id=1, source_target_pairs={{0,8},{1,9},{2,10},{3,11},{4,12},{5,13},{6,14},{7,15},{8,0},{9,1},... | collective-permute-start | bytes 6291464 | tf_op jit(solution)/shard_map/ppermute | solution.py:303
  179.1 59.9 %collective-permute-start.15 = (f32[2,4,128,512]{3,2,1,0:T(8,128)}, f32[2,4,128,512]{3,2,1,0:T(8,128)}, u32[]{:S(2)}, u32[]{:S(2)}) collective-permute-start(f32[2,4,128,512]{3,2,1,0:T(8,128)} %collective-permute-done.8), channel_id=1, source_target_pairs={{1,2},{2,1},{5,6},{6,5},{9,10},{10,9},{13,14},{14,13},{17,18},{18,... | collective-permute-start | bytes 6291464 | tf_op jit(solution)/shard_map/ppermute | solution.py:303
  186.3 52.8 %collective-permute-start.18 = (f32[2,4,128,512]{3,2,1,0:T(8,128)}, f32[2,4,128,512]{3,2,1,0:T(8,128)}, u32[]{:S(2)}, u32[]{:S(2)}) collective-permute-start(f32[2,4,128,512]{3,2,1,0:T(8,128)} %get-tuple-element.338.refs_0_), channel_id=1, source_target_pairs={{0,8},{1,9},{2,10},{3,11},{4,12},{5,13},{6,14},{7,15},{8,0},{9,1},... | collective-permute-start | bytes 6291464 | tf_op jit(solution)/shard_map/ppermute | solution.py:303
  187.8 51.3 %collective-permute-start.19 = (f32[2,4,128,512]{3,2,1,0:T(8,128)}, f32[2,4,128,512]{3,2,1,0:T(8,128)}, u32[]{:S(2)}, u32[]{:S(2)}) collective-permute-start(f32[2,4,128,512]{3,2,1,0:T(8,128)} %get-tuple-element.346.refs_0_), channel_id=1, source_target_pairs={{0,16},{1,17},{2,18},{3,19},{4,20},{5,21},{6,22},{7,23},{8,24},{9,... | collective-permute-start | bytes 6291464 | tf_op jit(solution)/shard_map/ppermute | solution.py:303
  190.4 48.7 %collective-permute-start.16 = (f32[2,4,128,512]{3,2,1,0:T(8,128)S(1)}, f32[2,4,128,512]{3,2,1,0:T(8,128)S(1)}, u32[]{:S(2)}, u32[]{:S(2)}) collective-permute-start(f32[2,4,128,512]{3,2,1,0:T(8,128)S(1)} %slice_select_fusion), channel_id=1, source_target_pairs={{0,1},{1,0},{2,3},{3,2},{4,5},{5,4},{6,7},{7,6},{8,9},{9,8},{10,11... | collective-permute-start | bytes 6291464 | tf_op jit(solution)/shard_map/ppermute | solution.py:303
  244.6 56.8 %collective-permute-start.23 = (f32[2,4,128,512]{3,2,1,0:T(8,128)}, f32[2,4,128,512]{3,2,1,0:T(8,128)}, u32[]{:S(2)}, u32[]{:S(2)}) collective-permute-start(f32[2,4,128,512]{3,2,1,0:T(8,128)} %collective-permute-done.2.refs_1_), channel_id=1, source_target_pairs={{1,2},{2,1},{5,6},{6,5},{9,10},{10,9},{13,14},{14,13},{17,18},{18,... | collective-permute-start | bytes 6291464 | tf_op jit(solution)/shard_map/ppermute | solution.py:303
  251.7 48.0 %collective-permute-start.22 = (f32[2,4,128,512]{3,2,1,0:T(8,128)}, f32[2,4,128,512]{3,2,1,0:T(8,128)}, u32[]{:S(2)}, u32[]{:S(2)}) collective-permute-start(f32[2,4,128,512]{3,2,1,0:T(8,128)} %get-tuple-element.411), channel_id=1, source_target_pairs={{0,1},{1,0},{2,3},{3,2},{4,5},{5,4},{6,7},{7,6},{8,9},{9,8},{10,11... | collective-permute-start | bytes 6291464 | tf_op jit(solution)/shard_map/ppermute | solution.py:303
  253.7 47.4 %collective-permute-start.20 = (f32[2,4,128,512]{3,2,1,0:T(8,128)}, f32[2,4,128,512]{3,2,1,0:T(8,128)}, u32[]{:S(2)}, u32[]{:S(2)}) collective-permute-start(f32[2,4,128,512]{3,2,1,0:T(8,128)} %get-tuple-element.346.refs_0_), channel_id=1, source_target_pairs={{0,8},{1,9},{2,10},{3,11},{4,12},{5,13},{6,14},{7,15},{8,0},{9,1},... | collective-permute-start | bytes 6291464 | tf_op jit(solution)/shard_map/ppermute | solution.py:303
  254.3 47.1 %collective-permute-start.21 = (f32[2,4,128,512]{3,2,1,0:T(8,128)}, f32[2,4,128,512]{3,2,1,0:T(8,128)}, u32[]{:S(2)}, u32[]{:S(2)}) collective-permute-start(f32[2,4,128,512]{3,2,1,0:T(8,128)} %get-tuple-element.338.refs_0_), channel_id=1, source_target_pairs={{0,16},{1,17},{2,18},{3,19},{4,20},{5,21},{6,22},{7,23},{8,24},{9,... | collective-permute-start | bytes 6291464 | tf_op jit(solution)/shard_map/ppermute | solution.py:303
  301.4 54.0 %collective-permute-start.28 = (f32[2,4,128,512]{3,2,1,0:T(8,128)S(1)}, f32[2,4,128,512]{3,2,1,0:T(8,128)}, u32[]{:S(2)}, u32[]{:S(2)}) collective-permute-start(f32[2,4,128,512]{3,2,1,0:T(8,128)S(1)} %copy-done.3), channel_id=1, source_target_pairs={{1,2},{2,1},{5,6},{6,5},{9,10},{10,9},{13,14},{14,13},{17,18},{18,... | collective-permute-start | bytes 6291464 | tf_op jit(solution)/shard_map/ppermute | solution.py:303
  305.2 47.7 %collective-permute-start.27 = (f32[2,4,128,512]{3,2,1,0:T(8,128)}, f32[2,4,128,512]{3,2,1,0:T(8,128)}, u32[]{:S(2)}, u32[]{:S(2)}) collective-permute-start(f32[2,4,128,512]{3,2,1,0:T(8,128)} %broadcast_select_fusion.1), channel_id=1, source_target_pairs={{0,1},{1,0},{2,3},{3,2},{4,5},{5,4},{6,7},{7,6},{8,9},{9,8},{10,11... | collective-permute-start | bytes 6291464 | tf_op jit(solution)/shard_map/ppermute | solution.py:303
  355.4 55.8 %collective-permute-start.31 = (f32[2,4,128,512]{3,2,1,0:T(8,128)}, f32[2,4,128,512]{3,2,1,0:T(8,128)}, u32[]{:S(2)}, u32[]{:S(2)}) collective-permute-start(f32[2,4,128,512]{3,2,1,0:T(8,128)} %collective-permute-done.11.refs_3_), channel_id=1, source_target_pairs={{1,2},{2,1},{5,6},{6,5},{9,10},{10,9},{13,14},{14,13},{17,18},{18,... | collective-permute-start | bytes 6291464 | tf_op jit(solution)/shard_map/ppermute | solution.py:303
  361.1 50.2 %collective-permute-start.30 = (f32[2,4,128,512]{3,2,1,0:T(8,128)}, f32[2,4,128,512]{3,2,1,0:T(8,128)S(1)}, u32[]{:S(2)}, u32[]{:S(2)}) collective-permute-start(f32[2,4,128,512]{3,2,1,0:T(8,128)} %broadcast_select_fusion), channel_id=1, source_target_pairs={{0,1},{1,0},{2,3},{3,2},{4,5},{5,4},{6,7},{7,6},{8,9},{9,8},{10,11... | collective-permute-start | bytes 6291464 | tf_op jit(solution)/shard_map/ppermute | solution.py:303
  362.1 49.2 %collective-permute-start.32 = (f32[2,4,128,512]{3,2,1,0:T(8,128)}, f32[2,4,128,512]{3,2,1,0:T(8,128)}, u32[]{:S(2)}, u32[]{:S(2)}) collective-permute-start(f32[2,4,128,512]{3,2,1,0:T(8,128)} %get-tuple-element.382.refs_0_), channel_id=1, source_target_pairs={{0,8},{1,9},{2,10},{3,11},{4,12},{5,13},{6,14},{7,15},{8,0},{9,1},... | collective-permute-start | bytes 6291464 | tf_op jit(solution)/shard_map/ppermute | solution.py:303
  362.7 48.6 %collective-permute-start.33 = (f32[2,4,128,512]{3,2,1,0:T(8,128)S(1)}, f32[2,4,128,512]{3,2,1,0:T(8,128)}, u32[]{:S(2)}, u32[]{:S(2)}) collective-permute-start(f32[2,4,128,512]{3,2,1,0:T(8,128)S(1)} %copy-done.6), channel_id=1, source_target_pairs={{0,16},{1,17},{2,18},{3,19},{4,20},{5,21},{6,22},{7,23},{8,24},{9,... | collective-permute-start | bytes 6291464 | tf_op jit(solution)/shard_map/ppermute | solution.py:303
  413.8 48.1 %collective-permute-start.38 = (f32[2,4,128,512]{3,2,1,0:T(8,128)}, f32[2,4,128,512]{3,2,1,0:T(8,128)}, u32[]{:S(2)}, u32[]{:S(2)}) collective-permute-start(f32[2,4,128,512]{3,2,1,0:T(8,128)} %get-tuple-element.363), channel_id=1, source_target_pairs={{0,5},{1,4},{2,7},{3,6},{4,1},{5,0},{6,3},{7,2},{8,13},{9,12},{10,... | collective-permute-start | bytes 6291464 | tf_op jit(solution)/shard_map/ppermute | solution.py:303
  461.8 47.9 %collective-permute-start.39 = (f32[2,4,128,512]{3,2,1,0:T(8,128)}, f32[2,4,128,512]{3,2,1,0:T(8,128)S(1)}, u32[]{:S(2)}, u32[]{:S(2)}) collective-permute-start(f32[2,4,128,512]{3,2,1,0:T(8,128)} %collective-permute-done.32.refs_1_), channel_id=1, source_target_pairs={{0,16},{1,17},{2,18},{3,19},{4,20},{5,21},{6,22},{7,23},{8,24},{9,... | collective-permute-start | bytes 6291464 | tf_op jit(solution)/shard_map/ppermute | solution.py:303
  463.4 47.7 %collective-permute-start.40 = (f32[2,4,128,512]{3,2,1,0:T(8,128)}, f32[2,4,128,512]{3,2,1,0:T(8,128)}, u32[]{:S(2)}, u32[]{:S(2)}) collective-permute-start(f32[2,4,128,512]{3,2,1,0:T(8,128)} %collective-permute-done.33.refs_2_), channel_id=1, source_target_pairs={{0,8},{1,9},{2,10},{3,11},{4,12},{5,13},{6,14},{7,15},{8,0},{9,1},... | collective-permute-start | bytes 6291464 | tf_op jit(solution)/shard_map/ppermute | solution.py:303
  464.0 47.1 %collective-permute-start.41 = (f32[2,4,128,512]{3,2,1,0:T(8,128)}, f32[2,4,128,512]{3,2,1,0:T(8,128)}, u32[]{:S(2)}, u32[]{:S(2)}) collective-permute-start(f32[2,4,128,512]{3,2,1,0:T(8,128)} %get-tuple-element.389), channel_id=1, source_target_pairs={{0,4},{1,5},{2,6},{3,7},{4,0},{5,1},{6,2},{7,3},{8,12},{9,13},{10,... | collective-permute-start | bytes 6291464 | tf_op jit(solution)/shard_map/ppermute | solution.py:303
  464.5 48.1 %collective-permute-start.43 = (f32[2,4,128,512]{3,2,1,0:T(8,128)}, f32[2,4,128,512]{3,2,1,0:T(8,128)}, u32[]{:S(2)}, u32[]{:S(2)}) collective-permute-start(f32[2,4,128,512]{3,2,1,0:T(8,128)} %get-tuple-element.391), channel_id=1, source_target_pairs={{0,5},{1,4},{2,7},{3,6},{4,1},{5,0},{6,3},{7,2},{8,13},{9,12},{10,... | collective-permute-start | bytes 6291464 | tf_op jit(solution)/shard_map/ppermute | solution.py:303
  (35 other events, 966.8 us)

commit v2 on v1

v2 whole, which is shorter than its diff:
```python
import functools

import jax
import jax.numpy as jnp
from jax import lax
from jax.experimental import pallas as pl
from jax.experimental.pallas import tpu as pltpu
from jax.sharding import PartitionSpec as P

AXES = ("row", "col")

HBM = pl.BlockSpec(memory_space=pl.ANY)
VMEM = 58 * 2**20


def streamed(amplitudes, integrals, occ_energy, vir_energy):
    planes = lax.axis_size("col")
    plane = lax.axis_index("col")
    rows_i, _, rows_a, _ = amplitudes.shape
    cols_j, cols_b = integrals.shape[2:]
    occ_i = lax.dynamic_slice_in_dim(occ_energy, lax.axis_index("row") * rows_i, rows_i, 0)
    vir_a = lax.dynamic_slice_in_dim(vir_energy, plane * rows_a, rows_a, 0)
    ring = [(z, (z + 1) % planes) for z in range(planes)]

    def step(s, carry):
        block, out = carry
        q = lax.rem(plane - s + planes, planes)
        panel = lax.all_gather(block, "row", axis=1, tiled=True)
        cycle = jnp.einsum("ikac,kcjb->ijab", amplitudes, panel, precision=lax.Precision.HIGHEST)
        occ_j = lax.dynamic_slice_in_dim(occ_energy, q * cols_j, cols_j, 0)
        denom = (
            occ_i[:, None, None, None]
            + occ_j[None, :, None, None]
            - vir_a[None, None, :, None]
            - vir_energy[None, None, None, :]
        )
        out = lax.dynamic_update_slice_in_dim(out, cycle / denom, q * cols_j, 1)
        return lax.ppermute(block, "col", ring), out

    out = jnp.zeros((rows_i, occ_energy.shape[0], rows_a, cols_b), jnp.float32)
    return lax.fori_loop(0, planes, step, (integrals, out))[1]


def split(value):
    high = value.astype(jnp.bfloat16)
    return high, (value - high.astype(jnp.float32)).astype(jnp.bfloat16)


def columns_kernel(pair, core_ref, block, mine, other):
    half = block.shape[2] // 2
    for which in range(2):

        @pl.when(core_ref[0] == which)
        def _(which=which):
            for t in range(2):
                mine[t, 0] = block[0, :, which * half + 2 * pair + t, :]
                other[t, 0] = block[0, :, (1 - which) * half + 2 * pair + t, :]


def columns(integrals, core, pair):
    ks, cs, js, width = integrals.shape
    return pl.pallas_call(
        functools.partial(columns_kernel, pair),
        grid_spec=pltpu.PrefetchScalarGridSpec(
            num_scalar_prefetch=1,
            grid=(ks,),
            in_specs=[pl.BlockSpec((1, cs, js, width), lambda k, _: (k, 0, 0, 0))],
            out_specs=[pl.BlockSpec((2, 1, cs, width), lambda k, _: (0, k, 0, 0))] * 2,
        ),
        out_shape=[jax.ShapeDtypeStruct((2, ks, cs, width), jnp.float32)] * 2,
        compiler_params=pltpu.CompilerParams(vmem_limit_bytes=VMEM),
    )(core.reshape(1), integrals)


def merge_kernel(core_ref, mine, other, out, *room):
    cs = mine.shape[2]
    for source, at in ((mine, core_ref[0]), (other, 1 - core_ref[0])):
        out[0, :, pl.ds(pl.multiple_of(at * cs, cs), cs), :] = source[0]


def merge(mine, other, core, room=None):
    _, ks, cs, width = other.shape
    block = (1, ks, cs, width)
    return pl.pallas_call(
        merge_kernel,
        grid_spec=pltpu.PrefetchScalarGridSpec(
            num_scalar_prefetch=1,
            grid=(2,),
            in_specs=[pl.BlockSpec(block, lambda t, _: (t, 0, 0, 0))] * 2,
            out_specs=[pl.BlockSpec((1, ks, 2 * cs, width), lambda t, _: (t, 0, 0, 0))] + [HBM] * (room is not None),
        ),
        out_shape=[jax.ShapeDtypeStruct((2, ks, 2 * cs, width), jnp.float32)]
        + [jax.ShapeDtypeStruct(r, jnp.float32) for r in [room] if r],
        compiler_params=pltpu.CompilerParams(vmem_limit_bytes=VMEM),
    )(core.reshape(1), mine, other)


def rows_kernel(starts, chip_ref, *refs):
    sources, (high, low) = refs[:-2], refs[-2:]
    step = pl.program_id(0)
    for source, (first, count) in zip(sources, starts):

        @pl.when((step >= first) & (step < first + count))
        def _(source=source):
            ks = source.shape[1]
            n = source.shape[3] // 4
            for m in range(4):
                at = pl.ds(pl.multiple_of((chip_ref[0] ^ m) * n, n), n)
                for k in range(ks):
                    to = pl.ds((m * ks + k) * n, n)
                    high[:, to], low[:, to] = split(source[0, k, :, at])


def rows(values, chip):
    starts, first = [], 0
    for v in values:
        starts.append((first, v.shape[0]))
        first += v.shape[0]
    _, ks, rows_a, depth = values[0].shape
    shape = jax.ShapeDtypeStruct((first * rows_a, ks * depth), jnp.bfloat16)
    return pl.pallas_call(
        functools.partial(rows_kernel, starts),
        grid_spec=pltpu.PrefetchScalarGridSpec(
            num_scalar_prefetch=1,
            grid=(first,),
            in_specs=[
                pl.BlockSpec((1, ks, rows_a, depth), lambda s, _, a=a, n=n: (jnp.clip(s - a, 0, n - 1), 0, 0, 0))
                for a, n in starts
            ],
            out_specs=[pl.BlockSpec((rows_a, ks * depth), lambda s, _: (s, 0))] * 2,
        ),
        out_shape=[shape, shape],
        compiler_params=pltpu.CompilerParams(vmem_limit_bytes=VMEM),
    )(chip.reshape(1), *values)


def each_place(act, gots, blocks, out, keys, at, block, sem):
    for n, got in enumerate(gots):

        @pl.when((keys[at] == 1) & (block < blocks[n]))
        def _(n=n, got=got, at=at):
            copy = pltpu.make_async_copy(got.at[0], out.at[:, keys[at + 1 + block]], sem.at[n])
            getattr(copy, act)()

        at += 1 + blocks[n]


def place_keys(gots):
    return [v for _, js, keep in gots for v in (keep, *js)]


def place_spec(got):
    last = got.shape[0] - 1
    return pl.BlockSpec((1, *got.shape[1:]), lambda b, *_: (jnp.minimum(b, last), 0, 0, 0))


def product_kernel(chunks, sets, blocks, mode, added, keys, occ, a_hi, a_lo, rowd, vir, *refs):
    pieces, refs = refs[: sets * len(chunks)], refs[sets * len(chunks) :]
    if added:
        start, refs = refs[0], refs[1:]
    places_here = mode in ("own", "mine")
    if places_here:
        gots, refs = refs[: len(blocks)], refs[len(blocks) + 1 :]
        out, *send, b_hi, b_lo, own, own_sem, got_sem = refs
        send = send[0] if send else None
    elif mode == "send":
        send, b_hi, b_lo = refs
    elif mode == "lent":
        own, send, b_hi, b_lo = refs
    else:
        part, b_hi, b_lo = refs
    block, step, tiles = pl.program_id(0), pl.program_id(1), pl.num_programs(1)
    own_at, send_at = {"mine": (0, None), "send": (None, 0)}.get(mode, (0, 1))
    ks, n = pieces[0].shape[1:3]
    tile_i = a_hi.shape[0] // 128
    column = keys[1 + block]

    def own_copy():
        return pltpu.make_async_copy(own, out.at[:, column], own_sem.at[0])

    def places(act):
        each_place(act, gots, blocks, out, keys, 1 + 2 * sets, block, got_sem)

    if places_here:
        pl.when(step == 0)(lambda: places("start"))

    @pl.when(keys[0] == 1)
    def _():
        for one in range(sets):

            @pl.when((step == 0) & (block >= 2 * one) & (block < 2 * one + 2))
            def _(one=one):
                for m in range(len(chunks)):
                    for k in range(ks):
                        at = pl.ds((m * ks + k) * n, n)
                        b_hi[at, :], b_lo[at, :] = split(pieces[one * len(chunks) + m][0, k])

        cols = slice(0, len(chunks) * ks * n)
        dot = functools.partial(jnp.dot, preferred_element_type=jnp.float32)
        high, low = a_hi[:, cols], a_lo[:, cols]
        value = dot(low, b_hi[...]) + dot(high, b_lo[...]) + dot(high, b_hi[...])
        if added:
            value = value + start[0]
        if mode == "part":
            part[0] = value
        else:
            wide = jnp.concatenate([rowd[...]] * (value.shape[1] // 128), axis=1)
            value = value / (wide + occ[column] - vir[...])
            value = value.reshape(tile_i, 128, value.shape[1])
            if own_at is not None:

                @pl.when(step == own_at)
                def _():
                    if mode == "lent":
                        own[0] = value
                    else:
                        own[...] = value
                        own_copy().start()

            if send_at is not None:

                @pl.when(step == send_at)
                def _():
                    send[0] = value

        if places_here:
            pl.when(step == tiles - 1)(lambda: own_copy().wait())

    if places_here:
        pl.when(step == tiles - 1)(lambda: places("wait"))


def product(rows_in, sets, run, js, occ, vir, mode="own", chunks=(0, 1, 2, 3), added=None, out=None, gots=()):
    a_hi, a_lo, rowd = rows_in
    size, whole = a_hi.shape
    _, ks, n, width = sets[0][0].shape
    depth = len(chunks) * ks * n
    count = 2 * len(sets)
    i_own = size // 256
    tall = size // 2
    first, tiles = {"mine": (0, 1), "send": (1, 1)}.get(mode, (0, 2))
    block = jax.ShapeDtypeStruct((count, i_own, 128, width), jnp.float32)
    block_spec = pl.BlockSpec((1, i_own, 128, width), lambda b, s, *_: (b, 0, 0, 0))
    part_spec = pl.BlockSpec((1, tall, width), lambda b, s, *_: (b, s + first, 0))
    keys = jnp.stack([jnp.asarray(v, jnp.int32) for v in (run, *js, *place_keys(gots))])
    args = [keys, occ, a_hi, a_lo, rowd, vir]
    if chunks[0] == 0:
        a_spec = pl.BlockSpec((tall, whole), lambda b, s, *_: (s + first, 0))
    else:
        a_spec = pl.BlockSpec((tall, depth), lambda b, s, *_: (s + first, chunks[0]))
    specs = [a_spec, a_spec, pl.BlockSpec((tall, 128), lambda b, s, *_: (s + first, 0))]
    specs += [pl.BlockSpec(vir.shape, lambda b, s, *_: (0, 0))]
    for one, pieces in enumerate(sets):
        args += pieces
        specs += [
            pl.BlockSpec((1, ks, n, width), lambda b, s, *_, one=one: (jnp.clip(b - 2 * one, 0, 1), 0, 0, 0))
        ] * len(pieces)
    if added is not None:
        args.append(added)
        specs.append(part_spec)
    scratch = [pltpu.VMEM((depth, width), jnp.bfloat16)] * 2
    alias = {}
    if mode in ("own", "mine"):
        args += [*[g for g, _, _ in gots], out]
        specs += [place_spec(g) for g, _, _ in gots] + [HBM]
        alias = {len(args) - 1: 0}
        scratch += [pltpu.VMEM(block.shape[1:], jnp.float32)]
        scratch += [pltpu.SemaphoreType.DMA((1,)), pltpu.SemaphoreType.DMA((max(len(gots), 1),))]
        out_specs, out_shape = [HBM], [jax.ShapeDtypeStruct(out.shape, out.dtype)]
        if mode == "own":
            out_specs, out_shape = out_specs + [block_spec], out_shape + [block]
    elif mode == "send":
        out_specs, out_shape = block_spec, block
    elif mode == "lent":
        out_specs, out_shape = [block_spec, block_spec], [block, block]
    else:
        out_specs, out_shape = part_spec, jax.ShapeDtypeStruct((count, size, width), jnp.float32)
    return pl.pallas_call(
        functools.partial(product_kernel, chunks, len(sets), [g.shape[0] for g, _, _ in gots], mode, added is not None),
        grid_spec=pltpu.PrefetchScalarGridSpec(
            num_scalar_prefetch=2, grid=(count, tiles), in_specs=specs, out_specs=out_specs, scratch_shapes=scratch
        ),
        out_shape=out_shape,
        input_output_aliases=alias,
        compiler_params=pltpu.CompilerParams(vmem_limit_bytes=VMEM),
        cost_estimate=pl.CostEstimate(
            flops=6 * count * size * depth * width // (2 // tiles),
            bytes_accessed=4 * count * (size * (depth + width) + depth * width),
            transcendentals=0,
        ),
    )(*args)


def place_kernel(blocks, keys, *refs):
    gots, out, sem = refs[: len(blocks)], refs[len(blocks) + 1], refs[len(blocks) + 2]
    for act in ("start", "wait"):
        each_place(act, gots, blocks, out, keys, 0, pl.program_id(0), sem)


def place(out, gots):
    keys = jnp.stack([jnp.asarray(v, jnp.int32) for v in place_keys(gots)])
    blocks = [g.shape[0] for g, _, _ in gots]
    return pl.pallas_call(
        functools.partial(place_kernel, blocks),
        grid_spec=pltpu.PrefetchScalarGridSpec(
            num_scalar_prefetch=1,
            grid=(max(blocks),),
            in_specs=[place_spec(g) for g, _, _ in gots] + [HBM],
            out_specs=HBM,
            scratch_shapes=[pltpu.SemaphoreType.DMA((len(gots),))],
        ),
        out_shape=jax.ShapeDtypeStruct(out.shape, out.dtype),
        input_output_aliases={len(gots) + 1: 0},
        compiler_params=pltpu.CompilerParams(vmem_limit_bytes=VMEM),
    )(keys, *[g for g, _, _ in gots], out)


def hop(value, mask=0, planes=None, core=0):
    planes = {z: z for z in range(4)} if planes is None else planes
    flip = 2 * mask + core
    pairs = [(r * 4 + z, (r ^ flip) * 4 + w) for r in range(8) for z, w in planes.items()]
    return lax.ppermute(value, AXES, pairs)


def hop_middle(value):
    pairs = [(r * 4 + z, r * 4 + 3 - z) for r in range(8) for z in (1, 2)]
    pairs += [(r * 4 + z, (r ^ 1) * 4 + z) for r in range(8) for z in (0, 3)]
    return lax.ppermute(value, AXES, pairs)


def together(values):
    return lax.optimization_barrier(values)


def body(amplitudes, integrals, occ_energy, vir_energy):
    row, plane = lax.axis_index("row"), lax.axis_index("col")
    core, chip = lax.rem(row, 2), lax.div(row, 2)
    rows_i, ks, rows_a, depth = amplitudes.shape
    cols_j, cols_b = integrals.shape[2:]
    parts = cols_j // 2
    swap = {0: 1, 1: 0, 2: 3, 3: 2}
    is_end = (plane == 0) | (plane == 3)
    is_mid = ~is_end
    vir = vir_energy.reshape(1, -1)

    def share(plane_of):
        occ = [lax.dynamic_slice_in_dim(occ_energy, r * rows_i, rows_i, 0) for r in (row, row ^ 1)]
        part = lax.dynamic_slice_in_dim(vir_energy, plane_of * rows_a, rows_a, 0)
        rowd = (jnp.concatenate(occ)[:, None] - part[None, :]).reshape(-1, 1)
        return jnp.broadcast_to(rowd, (rowd.shape[0], 128))

    def column(w, pair, of_core):
        return (plane ^ w) * cols_j + of_core * parts + 2 * pair

    def either(at_end, at_mid):
        return jnp.where(is_end, at_end, at_mid)

    def along(x, y, z, mid=None, flip=0):
        got = [hop_middle(mid)] if mid is not None else []
        return [hop(x, mask=1), hop(y, mask=2), hop(z, planes=swap, core=flip)] + got

    room = (rows_i, occ_energy.shape[0], rows_a, cols_b)
    mine, other = columns(integrals, core, 0)
    a0, out = merge(mine, hop(other, core=1), core, room)
    state = dict(out=out, gots=[], sends=[])

    def columns_of(w, pair, of_core):
        at = column(w, pair, of_core)
        return [at, at + 1]

    def work(rows_in, sets, where, run=1, **how):
        js = [j for w, pair in where for j in columns_of(w, pair, core)]
        state["out"], send = product(rows_in, sets, run, js, occ_energy, vir, out=state["out"], gots=state["gots"], **how)
        state["gots"] = []
        state["sends"].append((send, [j for w, pair in where for j in columns_of(w, pair, 1 - core)], run))

    def exchange():
        now, state["sends"] = state["sends"], []
        return [(hop(v, core=1), js, keep) for v, js, keep in now]

    def end_round(values, moved=()):
        gots, sends = state["gots"] + list(moved), state["sends"]
        values, new_gots, new_sends, state["out"] = together(
            (values, [g[0] for g in gots], [s[0] for s in sends], state["out"])
        )
        state["gots"] = [(v, *g[1:]) for v, g in zip(new_gots, gots)]
        state["sends"] = [(v, *s[1:]) for v, s in zip(new_sends, sends)]
        return values

    a0x, a0y, a1, a3m = along(a0, a0, a0, a0)
    mine, other = columns(integrals, core, 1)
    (b0,) = merge(mine, hop(other, core=1), core)
    z = either(b0, a3m)
    v = end_round((amplitudes, a0, b0, a0x, a0y, a1, a3m, z))
    amplitudes, a0, b0, a0x, a0y, a1, a3m, z = v
    a_other = hop(amplitudes, core=1)
    a0d, b0y, ab, a2m = along(a0y, b0, z, a1)
    z = either(amplitudes[:2], a2m)
    e3 = either(ab, a2m)
    v = end_round((amplitudes, a_other, a0, b0, a0x, a0y, a0d, a1, a3m, b0y, ab, e3, z))
    amplitudes, a_other, a0, b0, a0x, a0y, a0d, a1, a3m, b0y, ab, e3, z = v
    b0x, e3y, first, b3m = along(b0, e3, z, b0)
    here = (*rows([amplitudes, a_other], chip), share(plane))
    work(here, [(a0, a0x, a0y, a0d)], [(0, 0)])
    z = either(amplitudes[2:], b3m)
    first, state["out"] = together((first, state["out"]))
    first_other = hop(first, core=1)
    v = end_round((here, a0, b0, a0x, a0y, a0d, a1, a3m, b0x, b0y, ab, e3, e3y, first, first_other, b3m, z))
    here, a0, b0, a0x, a0y, a0d, a1, a3m, b0x, b0y, ab, e3, e3y, first, first_other, b3m, z = v
    moved = exchange()
    e3x, b0d, second, b2m = along(e3, b0x, z, ab)
    e6 = either(first, ab)
    z = either(a0x, b2m)
    v = (here, a0, b0, a0x, a0y, a0d, a1, a3m, b0x, b0y, b0d, b2m, e3, e3x, e3y, e6, first, first_other, second, b3m, z)
    v = end_round(v, moved)
    here, a0, b0, a0x, a0y, a0d, a1, a3m, b0x, b0y, b0d, b2m, e3, e3x, e3y, e6, first, first_other, second, b3m, z = v
    second_other = hop(second, core=1)
    e6x, e6y, third, g3x = along(e6, e6, z, a0x)
    e4, first = together((either(second, b2m), first))
    near = (*rows([first, second, first_other, second_other], chip), share(plane ^ 1))
    s_a, l_a = product(near, [(a0, a0x, a0y, a0d)], is_mid, columns_of(0, 0, core), occ_energy, vir, mode="lent")
    z = either(a0y, s_a)
    v = (here, near, a1, a3m, b0, b0x, b0y, b0d, a0y, a0d, b3m, e3, e3x, e3y, e4, e6, e6x, e6y, third, g3x, l_a, z)
    v = end_round(v)
    here, near, a1, a3m, b0, b0x, b0y, b0d, a0y, a0d, b3m, e3, e3x, e3y, e4, e6, e6x, e6y, third, g3x, l_a, z = v
    e3d, e6d, fourth, g3y = along(e3y, e6x, z, a0y)
    e5, near = together((either(third, b3m), near))
    s_b, l_b = product(near, [(b0, b0x, b0y, b0d)], is_mid, columns_of(0, 1, core), occ_energy, vir, mode="lent")
    z, here = together((either(a0d, s_b), here))
    work(here, [(b0, b0x, b0y, b0d)], [(0, 1)])
    v = (here, a1, a3m, a0d, e3, e3x, e3y, e3d, e4, e5, e6, e6x, e6y, e6d, third, fourth, g3x, g3y, l_a, l_b, z)
    v = end_round(v)
    here, a1, a3m, a0d, e3, e3x, e3y, e3d, e4, e5, e6, e6x, e6y, e6d, third, fourth, g3x, g3y, l_a, l_b, z = v
    state["gots"].append((fourth, columns_of(1, 0, core), is_end))
    moved = exchange()
    e4x, e4y, fifth, g3d = along(e4, e4, z, a0d)
    work(here, [(e3, e3x, e3y, e3d), (e6, e6x, e6y, e6d)], [(2, 0), (either(3, 1), either(0, 1))])
    v = end_round((here, a1, a3m, e4, e4x, e4y, e5, third, fourth, fifth, g3x, g3y, g3d, l_a, l_b), moved)
    here, a1, a3m, e4, e4x, e4y, e5, third, fourth, fifth, g3x, g3y, g3d, l_a, l_b = v
    state["gots"].append((fifth, columns_of(1, 1, core), is_end))
    moved = exchange()
    e5x, e5y, sixth = along(e5, e5, l_a, flip=1)
    work(here, [(a1, third, fourth, fifth), (a3m, g3x, g3y, g3d)], [(1, 0), (3, 0)], is_mid)
    moved.append((sixth, columns_of(1, 0, 1 - core), is_end))
    v = end_round((here, e4, e4x, e4y, e5, e5x, e5y, l_b), moved)
    here, e4, e4x, e4y, e5, e5x, e5y, l_b = v
    moved = exchange()
    e4d, e5d, seventh = along(e4y, e5x, l_b, flip=1)
    last = [(2, 1), (3, 1)]
    js = [j for w, pair in last for j in columns_of(w, pair, core)]
    sums = product(
        here, [(e4, e4x, e4y), (e5, e5x, e5y)], 1, js, occ_energy, vir, mode="part", chunks=(0, 1, 2)
    )
    sums, state["out"] = together((sums, state["out"]))
    state["out"], state["gots"] = place(state["out"], state["gots"] + moved), []
    here, e4d, e5d, sums = end_round((here, e4d, e5d, sums), [(seventh, columns_of(1, 1, 1 - core), is_end)])
    how = dict(chunks=(3,), added=sums)
    send = product(here, [(e4d,), (e5d,)], 1, js, occ_energy, vir, mode="send", **how)
    got = hop(send, core=1)
    (out,) = product(
        here, [(e4d,), (e5d,)], 1, js, occ_energy, vir, mode="mine", out=state["out"], gots=state["gots"], **how
    )
    return place(out, [(got, [j for w, pair in last for j in columns_of(w, pair, 1 - core)], 1)])


def solution(mesh):
    planned = mesh.shape["row"] == 8 and mesh.shape["col"] == 4
    return jax.shard_map(
        body if planned else streamed,
        mesh=mesh,
        in_specs=(P("row", None, "col", None), P(None, "row", "col", None), P(), P()),
        out_specs=P("row", None, "col", None),
        check_vma=False,
    )
```

time: 555 us -> 505 us (0.910)
  waiting for transfers between devices: 214 us -> 186 us
  starting transfers between devices: 54.6 us -> 42.1 us
  Pallas kernels: 244 us -> 233 us
    ppermute x46 -> x37, waiting for transfers between devices: 214 us -> 181 us  [hop(): return lax.ppermute(value, AXES, pairs)]
    ppermute x46 -> x37, starting transfers between devices: 54.6 us -> 41.1 us  [hop(): return lax.ppermute(value, AXES, pairs)]
    pallas_call x14 -> x13, Pallas kernels: 219 us -> 208 us  [the longest x9 184 us: product(): pl.pallas_call(functools.partial(product_kernel, chunks, len(sets), [g.sh...]
    select_n x8 -> x9, other arithmetic: 26.7 us -> 27 us  [either(): return jnp.where(is_end, at_end, at_mid)]
  transfers between devices with their start and end apart: 46 -> 44, of which waited for: 26 -> 27; matrix products, arithmetic and copies ran while one was open for 6% -> 6% of each run, Pallas kernels for 37% -> 42%
where the time goes in v2:
time: 505 us; the launch traced here: 504 us
  Pallas kernels  233 us (46%)
  waiting for transfers between devices  186 us (37%)
  starting transfers between devices  42.1 us (8%)
  other arithmetic  28.9 us (6%)
  local copies, waits for them, and re-layouts  13.7 us (3%)
    pallas_call x9, Pallas kernels, product(): pl.pallas_call(functools.partial(product_kernel, chunks, len(sets), [g.sh...  184 us
    ppermute x37, waiting for transfers between devices, hop(): return lax.ppermute(value, AXES, pairs)  181 us
    ppermute x37, starting transfers between devices, hop(): return lax.ppermute(value, AXES, pairs)  41.1 us
    select_n x9, other arithmetic, either(): return jnp.where(is_end, at_end, at_mid)  27 us
    pallas_call x2, Pallas kernels, rows(): pl.pallas_call(functools.partial(rows_kernel, starts), grid_spec=pltpu.Pr...  20.2 us
    pallas_call x2, Pallas kernels, place(): pl.pallas_call(functools.partial(place_kernel, blocks), grid_spec=pltpu.P...  14.5 us
  transfers between devices with their start and end apart: 44, of which 27 were waited for; matrix products, arithmetic and copies ran while one was open for 6% of the time, Pallas kernels for 42%

profile of v2, /device:TPU:0, one launch (start us, length us, event | category | flops | bytes accessed | tf_op | source)
XLA Modules:
  0.0 504.3 jit_solution(15719094935752966234)
XLA Ops:
  0.0 4.4 shard_map.46
  18.4 4.4 shard_map.48
  31.5 28.8 %collective-permute-done.2.refs_1_ = f32[2,4,128,512]{3,2,1,0:T(8,128)} collective-permute-done((f32[2,4,128,512]{3,2,1,0:T(8,128)}, f32[2,4,128,512]{3,2,1,0:T(8,128)}, u32[]{:S(2)}, u32[]{:S(2)}) %collective-permute-start.2) | collective-permute-done | bytes 2097184 | tf_op jit(solution)/shard_map/ppermute | solution.py:322
  68.7 5.2 %collective-permute-done.10 = f32[2,4,128,512]{3,2,1,0:T(8,128)S(1)} collective-permute-done((f32[2,4,128,512]{3,2,1,0:T(8,128)}, f32[2,4,128,512]{3,2,1,0:T(8,128)S(1)}, u32[]{:S(2)}, u32[]{:S(2)}) %collective-permute-start.10) | collective-permute-done | bytes 2097184 | tf_op jit(solution)/shard_map/ppermute | solution.py:328
  73.8 38.3 %collective-permute-done.9 = f32[2,4,128,512]{3,2,1,0:T(8,128)S(1)} collective-permute-done((f32[2,4,128,512]{3,2,1,0:T(8,128)S(1)}, f32[2,4,128,512]{3,2,1,0:T(8,128)S(1)}, u32[]{:S(2)}, u32[]{:S(2)}) %collective-permute-start.9) | collective-permute-done | bytes 2097184 | tf_op jit(solution)/shard_map/ppermute | solution.py:322
  123.5 9.6 %shard_map.50 = (bf16[1024,2048]{1,0:T(8,128)(2,1)}, bf16[1024,2048]{1,0:T(8,128)(2,1)}) custom-call(s32[1]{0:T(128)} %bitcast.8.chip_ref, f32[4,4,128,512]{3,2,1,0:T(8,128)} %refs_0_, f32[4,4,128,512]{3,2,1,0:T(8,128)} %copy-done.9), custom_call_target="tpu_custom_call" | custom-call | tf_op jit(solution)/shard_map/pallas_call | solution.py:121
  134.1 21.8 %shard_map.51 = (f32[4,32,128,512]{3,2,1,0:T(8,128)}, f32[2,4,128,512]{3,2,1,0:T(8,128)}) custom-call(s32[3]{0:T(128)} %add_add_fusion.keys, f32[32]{0:T(128)} %occ.17, bf16[1024,2048]{1,0:T(8,128)(2,1)} %get-tuple-element.397.a_hi, bf16[1024,2048]{1,0:T(8,128)(2,1)} %get-tuple-element.398.a_lo, ...), custom_call_target="tpu_custom_call", output_to_operand_aliasing={{0}: (10, {})} | custom-call | flops 12884901888 | bytes 29360128 | tf_op jit(solution)/shard_map/pallas_call | solution.py:278
  155.9 9.9 %collective-permute-done.13.refs_0_ = f32[2,4,128,512]{3,2,1,0:T(8,128)} collective-permute-done((f32[2,4,128,512]{3,2,1,0:T(8,128)}, f32[2,4,128,512]{3,2,1,0:T(8,128)}, u32[]{:S(2)}, u32[]{:S(2)}) %collective-permute-start.13) | collective-permute-done | bytes 2097184 | tf_op jit(solution)/shard_map/ppermute | solution.py:322
  181.7 36.8 %collective-permute-done.16.refs_3_ = f32[2,4,128,512]{3,2,1,0:T(8,128)} collective-permute-done((f32[2,4,128,512]{3,2,1,0:T(8,128)}, f32[2,4,128,512]{3,2,1,0:T(8,128)}, u32[]{:S(2)}, u32[]{:S(2)}) %collective-permute-start.16) | collective-permute-done | bytes 2097184 | tf_op jit(solution)/shard_map/ppermute | solution.py:322
  230.8 10.6 %shard_map.52 = (bf16[1024,2048]{1,0:T(8,128)(2,1)}, bf16[1024,2048]{1,0:T(8,128)(2,1)}) custom-call(s32[1]{0:T(128)} %bitcast.8.chip_ref, f32[2,4,128,512]{3,2,1,0:T(8,128)} %collective-permute-done.13.refs_0_, f32[2,4,128,512]{3,2,1,0:T(8,128)} %collective-permute-done.19.refs_1_, f32[2,4,128,512]{3,2,1,0:T(8,128)} %copy-done.14, ...), custom_call_target="tpu_custom_call" | custom-call | tf_op jit(solution)/shard_map/pallas_call | solution.py:121
  242.4 12.1 %shard_map.53 = (f32[2,4,128,512]{3,2,1,0:T(8,128)}, f32[2,4,128,512]{3,2,1,0:T(8,128)}) custom-call(s32[3]{0:T(128)} %add_add_fusion.1.keys, f32[32]{0:T(128)} %occ.17, bf16[1024,2048]{1,0:T(8,128)(2,1)} %get-tuple-element.298.a_hi, bf16[1024,2048]{1,0:T(8,128)(2,1)} %get-tuple-element.299.a_lo, f32[1024,128]{1,0:T(8,128)} %broadcast_in_dim.5.rowd, ...), custom_call_target="tpu_custom_call" | custom-call | flops 12884901888 | bytes 29360128 | tf_op jit(solution)/shard_map/pallas_call | solution.py:278
  258.1 10.9 %collective-permute-done.22.refs_5_ = f32[2,4,128,512]{3,2,1,0:T(8,128)} collective-permute-done((f32[2,4,128,512]{3,2,1,0:T(8,128)}, f32[2,4,128,512]{3,2,1,0:T(8,128)}, u32[]{:S(2)}, u32[]{:S(2)}) %collective-permute-start.22) | collective-permute-done | bytes 2097184 | tf_op jit(solution)/shard_map/ppermute | solution.py:322
  276.3 12.0 %shard_map.54 = (f32[2,4,128,512]{3,2,1,0:T(8,128)}, f32[2,4,128,512]{3,2,1,0:T(8,128)}) custom-call(s32[3]{0:T(128)} %pad_add_fusion.keys, f32[32]{0:T(128)} %occ.17, bf16[1024,2048]{1,0:T(8,128)(2,1)} %get-tuple-element.298.a_hi, bf16[1024,2048]{1,0:T(8,128)(2,1)} %get-tuple-element.299.a_lo, f32[1024,128]{1,0:T(8,128)} %broadcast_in_dim.5.rowd, ...), custom_call_target="tpu_custom_call" | custom-call | flops 12884901888 | bytes 29360128 | tf_op jit(solution)/shard_map/pallas_call | solution.py:278
  290.2 22.5 %shard_map.55 = (f32[4,32,128,512]{3,2,1,0:T(8,128)}, f32[2,4,128,512]{3,2,1,0:T(8,128)}) custom-call(s32[6]{0:T(128)} %stack.194.keys, f32[32]{0:T(128)} %occ.17, bf16[1024,2048]{1,0:T(8,128)(2,1)} %get-tuple-element.397.a_hi, bf16[1024,2048]{1,0:T(8,128)(2,1)} %get-tuple-element.398.a_lo, ...), custom_call_target="tpu_custom_call", output_to_operand_aliasing={{0}: (11, {})} | custom-call | flops 12884901888 | bytes 29360128 | tf_op jit(solution)/shard_map/pallas_call | solution.py:278
  312.7 8.9 %collective-permute-done.26.refs_3_ = f32[2,4,128,512]{3,2,1,0:T(8,128)} collective-permute-done((f32[2,4,128,512]{3,2,1,0:T(8,128)}, f32[2,4,128,512]{3,2,1,0:T(8,128)}, u32[]{:S(2)}, u32[]{:S(2)}) %collective-permute-start.26) | collective-permute-done | bytes 2097184 | tf_op jit(solution)/shard_map/ppermute | solution.py:322
  325.1 4.2 collective-permute-start.32
  329.8 39.8 %shard_map.56 = (f32[4,32,128,512]{3,2,1,0:T(8,128)}, f32[4,4,128,512]{3,2,1,0:T(8,128)}) custom-call(s32[8]{0:T(128)} %stack.203.keys, f32[32]{0:T(128)} %occ.17, bf16[1024,2048]{1,0:T(8,128)(2,1)} %get-tuple-element.397.a_hi, bf16[1024,2048]{1,0:T(8,128)(2,1)} %get-tuple-element.398.a_lo, ...), custom_call_target="tpu_custom_call", output_to_operand_aliasing={{0}: (15, {})} | custom-call | flops 25769803776 | bytes 58720256 | tf_op jit(solution)/shard_map/pallas_call | solution.py:278
  377.3 23.2 %shard_map.57 = (f32[4,32,128,512]{3,2,1,0:T(8,128)}, f32[4,4,128,512]{3,2,1,0:T(8,128)}) custom-call(s32[11]{0:T(128)} %stack.210.keys, f32[32]{0:T(128)} %occ.17, bf16[1024,2048]{1,0:T(8,128)(2,1)} %get-tuple-element.397.a_hi, bf16[1024,2048]{1,0:T(8,128)(2,1)} %get-tuple-element.398.a_lo, ...), custom_call_target="tpu_custom_call", output_to_operand_aliasing={{0}: (16, {})} | custom-call | flops 25769803776 | bytes 58720256 | tf_op jit(solution)/shard_map/pallas_call | solution.py:278
  400.5 21.5 %collective-permute-done.35.refs_4_ = f32[2,4,128,512]{3,2,1,0:T(8,128)S(1)} collective-permute-done((f32[2,4,128,512]{3,2,1,0:T(8,128)}, f32[2,4,128,512]{3,2,1,0:T(8,128)S(1)}, u32[]{:S(2)}, u32[]{:S(2)}) %collective-permute-start.35) | collective-permute-done | bytes 2097184 | tf_op jit(solution)/shard_map/ppermute | solution.py:322
  429.7 31.7 %shard_map.58.refs_2_ = f32[4,1024,512]{2,1,0:T(8,128)} custom-call(s32[5]{0:T(128)} %stack.182.keys, f32[32]{0:T(128)} %occ.17, bf16[1024,2048]{1,0:T(8,128)(2,1)} %get-tuple-element.397.a_hi, bf16[1024,2048]{1,0:T(8,128)(2,1)} %get-tuple-element.398.a_lo, f32[1024,128]{1,0:T(8,128)} %broadcast_in_dim.4.rowd, f32[1,512]{1,0:T(1,128)} %bitcast.51, ...), custom_call_target="tpu_custom_call" | custom-call | flops 19327352832 | bytes 46137344 | tf_op jit(solution)/shard_map/pallas_call | solution.py:278
  461.4 8.1 %shard_map.59.refs_4_ = f32[4,32,128,512]{3,2,1,0:T(8,128)} custom-call(s32[13]{0:T(128)} %stack.219.keys, f32[4,4,128,512]{3,2,1,0:T(8,128)} %collective-permute-done.37.refs_0_, f32[2,4,128,512]{3,2,1,0:T(8,128)} %copy-done.12, f32[4,4,128,512]{3,2,1,0:T(8,128)} %collective-permute-done.42.refs_2_, ...), custom_call_target="tpu_custom_call", output_to_operand_aliasing={{}: (4, {})} | custom-call | tf_op jit(solution)/shard_map/pallas_call | solution.py:303
  475.0 9.4 %shard_map.60 = f32[4,4,128,512]{3,2,1,0:T(8,128)} custom-call(s32[5]{0:T(128)} %stack.182.keys, f32[32]{0:T(128)} %occ.17, bf16[1024,2048]{1,0:T(8,128)(2,1)} %get-tuple-element.397.a_hi, bf16[1024,2048]{1,0:T(8,128)(2,1)} %get-tuple-element.398.a_lo, f32[1024,128]{1,0:T(8,128)} %broadcast_in_dim.4.rowd, f32[1,512]{1,0:T(1,128)} %bitcast.52, ...), custom_call_target="tpu_custom_call" | custom-call | flops 3221225472 | bytes 20971520 | tf_op jit(solution)/shard_map/pallas_call | solution.py:278
  485.9 11.7 %shard_map.61.refs_1_ = f32[4,32,128,512]{3,2,1,0:T(8,128)} custom-call(s32[8]{0:T(128)} %stack.222.keys, f32[32]{0:T(128)} %occ.17, bf16[1024,2048]{1,0:T(8,128)(2,1)} %get-tuple-element.397.a_hi, bf16[1024,2048]{1,0:T(8,128)(2,1)} %get-tuple-element.398.a_lo, f32[1024,128]{1,0:T(8,128)} %broadcast_in_dim.4.rowd, ...), custom_call_target="tpu_custom_call", output_to_operand_aliasing={{}: (10, {})} | custom-call | flops 3221225472 | bytes 20971520 | tf_op jit(solution)/shard_map/pallas_call | solution.py:278
  497.7 6.4 %shard_map.62 = f32[4,32,128,512]{3,2,1,0:T(8,128)} custom-call(s32[5]{0:T(128)} %stack.177.keys, f32[4,4,128,512]{3,2,1,0:T(8,128)} %collective-permute-done.43.refs_0_, f32[4,32,128,512]{3,2,1,0:T(8,128)} %shard_map.61.refs_1_), custom_call_target="tpu_custom_call", output_to_operand_aliasing={{}: (2, {})} | custom-call | tf_op jit(solution)/shard_map/pallas_call | solution.py:303
  (150 shorter events, 111.6 us)
Async XLA Ops:
  11.2 49.1 %collective-permute-start.2 = (f32[2,4,128,512]{3,2,1,0:T(8,128)}, f32[2,4,128,512]{3,2,1,0:T(8,128)}, u32[]{:S(2)}, u32[]{:S(2)}) collective-permute-start(f32[2,4,128,512]{3,2,1,0:T(8,128)} %get-tuple-element.287.refs_0_), channel_id=1, source_target_pairs={{0,8},{1,9},{2,10},{3,11},{4,12},{5,13},{6,14},{7,15},{8,0},{9,1},... | collective-permute-start | bytes 6291464 | tf_op jit(solution)/shard_map/ppermute | solution.py:322
  13.9 47.9 %collective-permute-start.3 = (f32[2,4,128,512]{3,2,1,0:T(8,128)}, f32[2,4,128,512]{3,2,1,0:T(8,128)}, u32[]{:S(2)}, u32[]{:S(2)}) collective-permute-start(f32[2,4,128,512]{3,2,1,0:T(8,128)} %get-tuple-element.287.refs_0_), channel_id=1, source_target_pairs={{0,16},{1,17},{2,18},{3,19},{4,20},{5,21},{6,22},{7,23},{8,24},{9,... | collective-permute-start | bytes 6291464 | tf_op jit(solution)/shard_map/ppermute | solution.py:322
  15.4 48.4 %collective-permute-start.4 = (f32[2,4,128,512]{3,2,1,0:T(8,128)}, f32[2,4,128,512]{3,2,1,0:T(8,128)}, u32[]{:S(2)}, u32[]{:S(2)}) collective-permute-start(f32[2,4,128,512]{3,2,1,0:T(8,128)} %get-tuple-element.287.refs_0_), channel_id=1, source_target_pairs={{0,1},{1,0},{2,3},{3,2},{4,5},{5,4},{6,7},{7,6},{8,9},{9,8},{10,11... | collective-permute-start | bytes 6291464 | tf_op jit(solution)/shard_map/ppermute | solution.py:322
  63.8 51.1 %collective-permute-start.6 = (f32[4,4,128,512]{3,2,1,0:T(8,128)S(1)}, f32[4,4,128,512]{3,2,1,0:T(8,128)S(1)}, u32[]{:S(2)}, u32[]{:S(2)}) collective-permute-start(f32[4,4,128,512]{3,2,1,0:T(8,128)S(1)} %copy-done.1), channel_id=1, source_target_pairs={{0,4},{1,5},{2,6},{3,7},{4,0},{5,1},{6,2},{7,3},{8,12},{9,13},{10,... | collective-permute-start | bytes 12582920 | tf_op jit(solution)/shard_map/ppermute | solution.py:322
  64.4 47.7 %collective-permute-start.9 = (f32[2,4,128,512]{3,2,1,0:T(8,128)S(1)}, f32[2,4,128,512]{3,2,1,0:T(8,128)S(1)}, u32[]{:S(2)}, u32[]{:S(2)}) collective-permute-start(f32[2,4,128,512]{3,2,1,0:T(8,128)S(1)} %broadcast_select_fusion.7), channel_id=1, source_target_pairs={{0,1},{1,0},{2,3},{3,2},{4,5},{5,4},{6,7},{7,6},{8,9},{9,8},{10,11... | collective-permute-start | bytes 6291464 | tf_op jit(solution)/shard_map/ppermute | solution.py:322
  66.1 48.8 %collective-permute-start.7 = (f32[2,4,128,512]{3,2,1,0:T(8,128)}, f32[2,4,128,512]{3,2,1,0:T(8,128)S(1)}, u32[]{:S(2)}, u32[]{:S(2)}) collective-permute-start(f32[2,4,128,512]{3,2,1,0:T(8,128)} %collective-permute-done.3.refs_2_), channel_id=1, source_target_pairs={{0,8},{1,9},{2,10},{3,11},{4,12},{5,13},{6,14},{7,15},{8,0},{9,1},... | collective-permute-start | bytes 6291464 | tf_op jit(solution)/shard_map/ppermute | solution.py:322
  67.2 47.8 %collective-permute-start.8 = (f32[2,4,128,512]{3,2,1,0:T(8,128)S(1)}, f32[2,4,128,512]{3,2,1,0:T(8,128)S(1)}, u32[]{:S(2)}, u32[]{:S(2)}) collective-permute-start(f32[2,4,128,512]{3,2,1,0:T(8,128)S(1)} %copy-done), channel_id=1, source_target_pairs={{0,16},{1,17},{2,18},{3,19},{4,20},{5,21},{6,22},{7,23},{8,24},{9,... | collective-permute-start | bytes 6291464 | tf_op jit(solution)/shard_map/ppermute | solution.py:322
  118.3 47.5 %collective-permute-start.13 = (f32[2,4,128,512]{3,2,1,0:T(8,128)}, f32[2,4,128,512]{3,2,1,0:T(8,128)}, u32[]{:S(2)}, u32[]{:S(2)}) collective-permute-start(f32[2,4,128,512]{3,2,1,0:T(8,128)} %get-tuple-element.234), channel_id=1, source_target_pairs={{0,1},{1,0},{2,3},{3,2},{4,5},{5,4},{6,7},{7,6},{8,9},{9,8},{10,11... | collective-permute-start | bytes 6291464 | tf_op jit(solution)/shard_map/ppermute | solution.py:322
  120.9 48.1 %collective-permute-start.11 = (f32[2,4,128,512]{3,2,1,0:T(8,128)S(1)}, f32[2,4,128,512]{3,2,1,0:T(8,128)}, u32[]{:S(2)}, u32[]{:S(2)}) collective-permute-start(f32[2,4,128,512]{3,2,1,0:T(8,128)S(1)} %copy-done), channel_id=1, source_target_pairs={{0,8},{1,9},{2,10},{3,11},{4,12},{5,13},{6,14},{7,15},{8,0},{9,1},... | collective-permute-start | bytes 6291464 | tf_op jit(solution)/shard_map/ppermute | solution.py:322
  122.0 48.1 %collective-permute-start.12 = (f32[2,4,128,512]{3,2,1,0:T(8,128)}, f32[2,4,128,512]{3,2,1,0:T(8,128)}, u32[]{:S(2)}, u32[]{:S(2)}) collective-permute-start(f32[2,4,128,512]{3,2,1,0:T(8,128)} %get-tuple-element.348.refs_0_), channel_id=1, source_target_pairs={{0,16},{1,17},{2,18},{3,19},{4,20},{5,21},{6,22},{7,23},{8,24},{9,... | collective-permute-start | bytes 6291464 | tf_op jit(solution)/shard_map/ppermute | solution.py:322
  170.3 48.2 %collective-permute-start.16 = (f32[2,4,128,512]{3,2,1,0:T(8,128)}, f32[2,4,128,512]{3,2,1,0:T(8,128)}, u32[]{:S(2)}, u32[]{:S(2)}) collective-permute-start(f32[2,4,128,512]{3,2,1,0:T(8,128)} %collective-permute-done.11.refs_1_), channel_id=1, source_target_pairs={{0,16},{1,17},{2,18},{3,19},{4,20},{5,21},{6,22},{7,23},{8,24},{9,... | collective-permute-start | bytes 6291464 | tf_op jit(solution)/shard_map/ppermute | solution.py:322
  171.7 47.7 %collective-permute-start.18 = (f32[2,4,128,512]{3,2,1,0:T(8,128)S(1)}, f32[2,4,128,512]{3,2,1,0:T(8,128)S(1)}, u32[]{:S(2)}, u32[]{:S(2)}) collective-permute-start(f32[2,4,128,512]{3,2,1,0:T(8,128)S(1)} %copy-done.13), channel_id=1, source_target_pairs={{0,8},{1,9},{2,10},{3,11},{4,12},{5,13},{6,14},{7,15},{8,0},{9,1},... | collective-permute-start | bytes 6291464 | tf_op jit(solution)/shard_map/ppermute | solution.py:322
  172.9 47.4 %collective-permute-start.19 = (f32[2,4,128,512]{3,2,1,0:T(8,128)S(1)}, f32[2,4,128,512]{3,2,1,0:T(8,128)}, u32[]{:S(2)}, u32[]{:S(2)}) collective-permute-start(f32[2,4,128,512]{3,2,1,0:T(8,128)S(1)} %slice_select_fusion), channel_id=1, source_target_pairs={{0,1},{1,0},{2,3},{3,2},{4,5},{5,4},{6,7},{7,6},{8,9},{9,8},{10,11... | collective-permute-start | bytes 6291464 | tf_op jit(solution)/shard_map/ppermute | solution.py:322
  220.7 48.4 %collective-permute-start.22 = (f32[2,4,128,512]{3,2,1,0:T(8,128)}, f32[2,4,128,512]{3,2,1,0:T(8,128)}, u32[]{:S(2)}, u32[]{:S(2)}) collective-permute-start(f32[2,4,128,512]{3,2,1,0:T(8,128)} %broadcast_select_fusion.5.refs_4_), channel_id=1, source_target_pairs={{0,8},{1,9},{2,10},{3,11},{4,12},{5,13},{6,14},{7,15},{8,0},{9,1},... | collective-permute-start | bytes 6291464 | tf_op jit(solution)/shard_map/ppermute | solution.py:322
  221.8 48.1 %collective-permute-start.23 = (f32[2,4,128,512]{3,2,1,0:T(8,128)}, f32[2,4,128,512]{3,2,1,0:T(8,128)}, u32[]{:S(2)}, u32[]{:S(2)}) collective-permute-start(f32[2,4,128,512]{3,2,1,0:T(8,128)} %broadcast_select_fusion.5.refs_4_), channel_id=1, source_target_pairs={{0,16},{1,17},{2,18},{3,19},{4,20},{5,21},{6,22},{7,23},{8,24},{9,... | collective-permute-start | bytes 6291464 | tf_op jit(solution)/shard_map/ppermute | solution.py:322
  222.4 48.5 %collective-permute-start.24 = (f32[2,4,128,512]{3,2,1,0:T(8,128)}, f32[2,4,128,512]{3,2,1,0:T(8,128)}, u32[]{:S(2)}, u32[]{:S(2)}) collective-permute-start(f32[2,4,128,512]{3,2,1,0:T(8,128)} %broadcast_select_fusion.4), channel_id=1, source_target_pairs={{0,1},{1,0},{2,3},{3,2},{4,5},{5,4},{6,7},{7,6},{8,9},{9,8},{10,11... | collective-permute-start | bytes 6291464 | tf_op jit(solution)/shard_map/ppermute | solution.py:322
  325.1 48.0 %collective-permute-start.32 = (f32[2,4,128,512]{3,2,1,0:T(8,128)}, f32[2,4,128,512]{3,2,1,0:T(8,128)}, u32[]{:S(2)}, u32[]{:S(2)}) collective-permute-start(f32[2,4,128,512]{3,2,1,0:T(8,128)} %broadcast_select_fusion), channel_id=1, source_target_pairs={{0,1},{1,0},{2,3},{3,2},{4,5},{5,4},{6,7},{7,6},{8,9},{9,8},{10,11... | collective-permute-start | bytes 6291464 | tf_op jit(solution)/shard_map/ppermute | solution.py:322
  373.1 50.8 %collective-permute-start.37 = (f32[4,4,128,512]{3,2,1,0:T(8,128)}, f32[4,4,128,512]{3,2,1,0:T(8,128)}, u32[]{:S(2)}, u32[]{:S(2)}) collective-permute-start(f32[4,4,128,512]{3,2,1,0:T(8,128)} %get-tuple-element.367), channel_id=1, source_target_pairs={{0,4},{1,5},{2,6},{3,7},{4,0},{5,1},{6,2},{7,3},{8,12},{9,13},{10,... | collective-permute-start | bytes 12582920 | tf_op jit(solution)/shard_map/ppermute | solution.py:322
  373.8 48.2 %collective-permute-start.35 = (f32[2,4,128,512]{3,2,1,0:T(8,128)}, f32[2,4,128,512]{3,2,1,0:T(8,128)S(1)}, u32[]{:S(2)}, u32[]{:S(2)}) collective-permute-start(f32[2,4,128,512]{3,2,1,0:T(8,128)} %broadcast_select_fusion.1.refs_3_), channel_id=1, source_target_pairs={{0,8},{1,9},{2,10},{3,11},{4,12},{5,13},{6,14},{7,15},{8,0},{9,1},... | collective-permute-start | bytes 6291464 | tf_op jit(solution)/shard_map/ppermute | solution.py:322
  374.3 48.1 %collective-permute-start.36 = (f32[2,4,128,512]{3,2,1,0:T(8,128)}, f32[2,4,128,512]{3,2,1,0:T(8,128)}, u32[]{:S(2)}, u32[]{:S(2)}) collective-permute-start(f32[2,4,128,512]{3,2,1,0:T(8,128)} %broadcast_select_fusion.1.refs_3_), channel_id=1, source_target_pairs={{0,16},{1,17},{2,18},{3,19},{4,20},{5,21},{6,22},{7,23},{8,24},{9,... | collective-permute-start | bytes 6291464 | tf_op jit(solution)/shard_map/ppermute | solution.py:322
  376.0 47.8 %collective-permute-start.38 = (f32[2,4,128,512]{3,2,1,0:T(8,128)}, f32[2,4,128,512]{3,2,1,0:T(8,128)S(1)}, u32[]{:S(2)}, u32[]{:S(2)}) collective-permute-start(f32[2,4,128,512]{3,2,1,0:T(8,128)} %get-tuple-element.368), channel_id=1, source_target_pairs={{0,5},{1,4},{2,7},{3,6},{4,1},{5,0},{6,3},{7,2},{8,13},{9,12},{10,... | collective-permute-start | bytes 6291464 | tf_op jit(solution)/shard_map/ppermute | solution.py:322
  425.3 48.1 %collective-permute-start.39 = (f32[2,4,128,512]{3,2,1,0:T(8,128)}, f32[2,4,128,512]{3,2,1,0:T(8,128)S(1)}, u32[]{:S(2)}, u32[]{:S(2)}) collective-permute-start(f32[2,4,128,512]{3,2,1,0:T(8,128)} %collective-permute-done.31.refs_2_), channel_id=1, source_target_pairs={{0,8},{1,9},{2,10},{3,11},{4,12},{5,13},{6,14},{7,15},{8,0},{9,1},... | collective-permute-start | bytes 6291464 | tf_op jit(solution)/shard_map/ppermute | solution.py:322
  426.0 47.9 %collective-permute-start.40 = (f32[2,4,128,512]{3,2,1,0:T(8,128)}, f32[2,4,128,512]{3,2,1,0:T(8,128)}, u32[]{:S(2)}, u32[]{:S(2)}) collective-permute-start(f32[2,4,128,512]{3,2,1,0:T(8,128)} %copy-done.20), channel_id=1, source_target_pairs={{0,16},{1,17},{2,18},{3,19},{4,20},{5,21},{6,22},{7,23},{8,24},{9,... | collective-permute-start | bytes 6291464 | tf_op jit(solution)/shard_map/ppermute | solution.py:322
  427.1 47.8 %collective-permute-start.41 = (f32[2,4,128,512]{3,2,1,0:T(8,128)}, f32[2,4,128,512]{3,2,1,0:T(8,128)}, u32[]{:S(2)}, u32[]{:S(2)}) collective-permute-start(f32[2,4,128,512]{3,2,1,0:T(8,128)} %get-tuple-element.392), channel_id=1, source_target_pairs={{0,5},{1,4},{2,7},{3,6},{4,1},{5,0},{6,3},{7,2},{8,13},{9,12},{10,... | collective-permute-start | bytes 6291464 | tf_op jit(solution)/shard_map/ppermute | solution.py:322
  (42 other events, 907.6 us)

commit v3 on v2

--- a/solution.py
+++ b/solution.py
@@ -10,7 +10,7 @@
 AXES = ("row", "col")
 
 HBM = pl.BlockSpec(memory_space=pl.ANY)
-VMEM = 58 * 2**20
+VMEM = 44 * 2**20
 
 
 def streamed(amplitudes, integrals, occ_energy, vir_energy):
@@ -154,15 +154,19 @@
     return pl.BlockSpec((1, *got.shape[1:]), lambda b, *_: (jnp.minimum(b, last), 0, 0, 0))
 
 
-def product_kernel(chunks, sets, blocks, mode, added, keys, occ, a_hi, a_lo, rowd, vir, *refs):
+def product_kernel(chunks, starts, blocks, mode, added, keys, occ, a_hi, a_lo, rowd, vir, *refs):
+    sets = len(starts) - 1
     pieces, refs = refs[: sets * len(chunks)], refs[sets * len(chunks) :]
     if added:
         start, refs = refs[0], refs[1:]
-    places_here = mode in ("own", "mine")
+    places_here = mode == "own" or len(blocks) > 0
     if places_here:
         gots, refs = refs[: len(blocks)], refs[len(blocks) + 1 :]
-        out, *send, b_hi, b_lo, own, own_sem, got_sem = refs
-        send = send[0] if send else None
+        out, *refs, got_sem = refs
+    if mode == "own":
+        send, b_hi, b_lo, own, own_sem = refs
+    elif mode == "mine":
+        _, own, b_hi, b_lo = refs
     elif mode == "send":
         send, b_hi, b_lo = refs
     elif mode == "lent":
@@ -179,7 +183,7 @@
         return pltpu.make_async_copy(own, out.at[:, column], own_sem.at[0])
 
     def places(act):
-        each_place(act, gots, blocks, out, keys, 1 + 2 * sets, block, got_sem)
+        each_place(act, gots, blocks, out, keys, 1 + starts[-1], block, got_sem)
 
     if places_here:
         pl.when(step == 0)(lambda: places("start"))
@@ -188,7 +192,7 @@
     def _():
         for one in range(sets):
 
-            @pl.when((step == 0) & (block >= 2 * one) & (block < 2 * one + 2))
+            @pl.when((step == 0) & (block >= starts[one]) & (block < starts[one + 1]))
             def _(one=one):
                 for m in range(len(chunks)):
                     for k in range(ks):
@@ -211,7 +215,9 @@
 
                 @pl.when(step == own_at)
                 def _():
-                    if mode == "lent":
+                    if mode == "mine":
+                        own[:, 0] = value
+                    elif mode == "lent":
                         own[0] = value
                     else:
                         own[...] = value
@@ -223,25 +229,29 @@
                 def _():
                     send[0] = value
 
-        if places_here:
+        if mode == "own":
             pl.when(step == tiles - 1)(lambda: own_copy().wait())
 
     if places_here:
         pl.when(step == tiles - 1)(lambda: places("wait"))
 
 
-def product(rows_in, sets, run, js, occ, vir, mode="own", chunks=(0, 1, 2, 3), added=None, out=None, gots=()):
+def product(rows_in, sets, run, js, occ, vir, mode="own", chunks=(0, 1, 2, 3), added=None, added_at=None, out=None, gots=()):
     a_hi, a_lo, rowd = rows_in
     size, whole = a_hi.shape
     _, ks, n, width = sets[0][0].shape
     depth = len(chunks) * ks * n
-    count = 2 * len(sets)
+    starts = [0]
+    for pieces in sets:
+        starts.append(starts[-1] + pieces[0].shape[0])
+    count = starts[-1]
     i_own = size // 256
     tall = size // 2
     first, tiles = {"mine": (0, 1), "send": (1, 1)}.get(mode, (0, 2))
     block = jax.ShapeDtypeStruct((count, i_own, 128, width), jnp.float32)
     block_spec = pl.BlockSpec((1, i_own, 128, width), lambda b, s, *_: (b, 0, 0, 0))
     part_spec = pl.BlockSpec((1, tall, width), lambda b, s, *_: (b, s + first, 0))
+    added_at = added_at or (lambda b: b)
     keys = jnp.stack([jnp.asarray(v, jnp.int32) for v in (run, *js, *place_keys(gots))])
     args = [keys, occ, a_hi, a_lo, rowd, vir]
     if chunks[0] == 0:
@@ -250,33 +260,40 @@
         a_spec = pl.BlockSpec((tall, depth), lambda b, s, *_: (s + first, chunks[0]))
     specs = [a_spec, a_spec, pl.BlockSpec((tall, 128), lambda b, s, *_: (s + first, 0))]
     specs += [pl.BlockSpec(vir.shape, lambda b, s, *_: (0, 0))]
-    for one, pieces in enumerate(sets):
+    for at, pieces in zip(starts, sets):
+        last = pieces[0].shape[0] - 1
         args += pieces
         specs += [
-            pl.BlockSpec((1, ks, n, width), lambda b, s, *_, one=one: (jnp.clip(b - 2 * one, 0, 1), 0, 0, 0))
+            pl.BlockSpec((1, ks, n, width), lambda b, s, *_, at=at, last=last: (jnp.clip(b - at, 0, last), 0, 0, 0))
         ] * len(pieces)
     if added is not None:
         args.append(added)
-        specs.append(part_spec)
+        specs.append(pl.BlockSpec((1, tall, width), lambda b, s, *_: (added_at(b), s + first, 0)))
     scratch = [pltpu.VMEM((depth, width), jnp.bfloat16)] * 2
     alias = {}
-    if mode in ("own", "mine"):
+    out_specs, out_shape = [], []
+    if mode == "own":
+        scratch += [pltpu.VMEM(block.shape[1:], jnp.float32), pltpu.SemaphoreType.DMA((1,))]
+    if mode == "mine":
+        args.append(out)
+        specs.append(HBM)
+        alias = {len(args) - 1: 0}
+        out_specs = [pl.BlockSpec((i_own, 1, 128, width), lambda b, s, keys, _: (0, keys[1 + b], 0, 0))]
+        out_shape = [jax.ShapeDtypeStruct(out.shape, out.dtype)]
+    elif mode == "own" or gots:
         args += [*[g for g, _, _ in gots], out]
         specs += [place_spec(g) for g, _, _ in gots] + [HBM]
         alias = {len(args) - 1: 0}
-        scratch += [pltpu.VMEM(block.shape[1:], jnp.float32)]
-        scratch += [pltpu.SemaphoreType.DMA((1,)), pltpu.SemaphoreType.DMA((max(len(gots), 1),))]
+        scratch.append(pltpu.SemaphoreType.DMA((max(len(gots), 1),)))
         out_specs, out_shape = [HBM], [jax.ShapeDtypeStruct(out.shape, out.dtype)]
-        if mode == "own":
-            out_specs, out_shape = out_specs + [block_spec], out_shape + [block]
-    elif mode == "send":
-        out_specs, out_shape = block_spec, block
+    if mode in ("own", "send"):
+        out_specs, out_shape = out_specs + [block_spec], out_shape + [block]
     elif mode == "lent":
         out_specs, out_shape = [block_spec, block_spec], [block, block]
-    else:
-        out_specs, out_shape = part_spec, jax.ShapeDtypeStruct((count, size, width), jnp.float32)
+    elif mode == "part":
+        out_specs, out_shape = out_specs + [part_spec], out_shape + [jax.ShapeDtypeStruct((count, size, width), jnp.float32)]
     return pl.pallas_call(
-        functools.partial(product_kernel, chunks, len(sets), [g.shape[0] for g, _, _ in gots], mode, added is not None),
+        functools.partial(product_kernel, chunks, starts, [g.shape[0] for g, _, _ in gots], mode, added is not None),
         grid_spec=pltpu.PrefetchScalarGridSpec(
             num_scalar_prefetch=2, grid=(count, tiles), in_specs=specs, out_specs=out_specs, scratch_shapes=scratch
         ),
@@ -315,6 +332,39 @@
     )(keys, *[g for g, _, _ in gots], out)
 
 
+def finish_kernel(starts, keys, *refs):
+    sources, out = refs[: len(starts) - 1], refs[-1]
+    for n, source in enumerate(sources):
+
+        @pl.when((pl.program_id(0) >= starts[n]) & (pl.program_id(0) < starts[n + 1]))
+        def _(source=source):
+            out[:, 0] = source[0]
+
+
+def finish(out, gots):
+    keys = jnp.stack([jnp.asarray(j, jnp.int32) for _, js in gots for j in js])
+    starts = [0]
+    for got, _ in gots:
+        starts.append(starts[-1] + got.shape[0])
+    rows_i, _, rows_a, width = out.shape
+    return pl.pallas_call(
+        functools.partial(finish_kernel, starts),
+        grid_spec=pltpu.PrefetchScalarGridSpec(
+            num_scalar_prefetch=1,
+            grid=(starts[-1],),
+            in_specs=[
+                pl.BlockSpec((1, *g.shape[1:]), lambda b, _, at=at, n=g.shape[0]: (jnp.clip(b - at, 0, n - 1), 0, 0, 0))
+                for at, (g, _) in zip(starts, gots)
+            ]
+            + [HBM],
+            out_specs=pl.BlockSpec((rows_i, 1, rows_a, width), lambda b, keys: (0, keys[b], 0, 0)),
+        ),
+        out_shape=jax.ShapeDtypeStruct(out.shape, out.dtype),
+        input_output_aliases={len(gots) + 1: 0},
+        compiler_params=pltpu.CompilerParams(vmem_limit_bytes=VMEM),
+    )(keys, *[g for g, _ in gots], out)
+
+
 def hop(value, mask=0, planes=None, core=0):
     planes = {z: z for z in range(4)} if planes is None else planes
     flip = 2 * mask + core
@@ -373,6 +423,18 @@
         state["out"], send = product(rows_in, sets, run, js, occ_energy, vir, out=state["out"], gots=state["gots"], **how)
         state["gots"] = []
         state["sends"].append((send, [j for w, pair in where for j in columns_of(w, pair, 1 - core)], run))
+
+    def begin(here, sets, where, chunks=(0, 1, 2)):
+        js = [j for w, pair in where for j in columns_of(w, pair, core)]
+        how = dict(mode="part", chunks=chunks)
+        if state["gots"]:
+            state["out"], sums = product(
+                here, sets, 1, js, occ_energy, vir, out=state["out"], gots=state["gots"], **how
+            )
+            state["gots"] = []
+            return sums
+        (sums,) = product(here, sets, 1, js, occ_energy, vir, **how)
+        return sums
 
     def exchange():
         now, state["sends"] = state["sends"], []
@@ -409,25 +471,26 @@
     here, a0, b0, a0x, a0y, a0d, a1, a3m, b0x, b0y, ab, e3, e3y, first, first_other, b3m, z = v
     moved = exchange()
     e3x, b0d, second, b2m = along(e3, b0x, z, ab)
-    e6 = either(first, ab)
+    e6, here = together((either(first, ab), here))
+    b_sum = begin(here, [(b0, b0x, b0y)], [(0, 1)])
     z = either(a0x, b2m)
-    v = (here, a0, b0, a0x, a0y, a0d, a1, a3m, b0x, b0y, b0d, b2m, e3, e3x, e3y, e6, first, first_other, second, b3m, z)
+    v = (here, a0, b0, a0x, a0y, a0d, a1, a3m, b0x, b0y, b0d, b2m, b_sum, e3, e3x, e3y, e6, first, first_other, second, b3m, z)
     v = end_round(v, moved)
-    here, a0, b0, a0x, a0y, a0d, a1, a3m, b0x, b0y, b0d, b2m, e3, e3x, e3y, e6, first, first_other, second, b3m, z = v
+    here, a0, b0, a0x, a0y, a0d, a1, a3m, b0x, b0y, b0d, b2m, b_sum, e3, e3x, e3y, e6, first, first_other, second, b3m, z = v
     second_other = hop(second, core=1)
     e6x, e6y, third, g3x = along(e6, e6, z, a0x)
     e4, first = together((either(second, b2m), first))
     near = (*rows([first, second, first_other, second_other], chip), share(plane ^ 1))
     s_a, l_a = product(near, [(a0, a0x, a0y, a0d)], is_mid, columns_of(0, 0, core), occ_energy, vir, mode="lent")
     z = either(a0y, s_a)
-    v = (here, near, a1, a3m, b0, b0x, b0y, b0d, a0y, a0d, b3m, e3, e3x, e3y, e4, e6, e6x, e6y, third, g3x, l_a, z)
+    v = (here, near, a1, a3m, b0, b0x, b0y, b0d, a0y, a0d, b3m, b_sum, e3, e3x, e3y, e4, e6, e6x, e6y, third, g3x, l_a, z)
     v = end_round(v)
-    here, near, a1, a3m, b0, b0x, b0y, b0d, a0y, a0d, b3m, e3, e3x, e3y, e4, e6, e6x, e6y, third, g3x, l_a, z = v
+    here, near, a1, a3m, b0, b0x, b0y, b0d, a0y, a0d, b3m, b_sum, e3, e3x, e3y, e4, e6, e6x, e6y, third, g3x, l_a, z = v
     e3d, e6d, fourth, g3y = along(e3y, e6x, z, a0y)
     e5, near = together((either(third, b3m), near))
     s_b, l_b = product(near, [(b0, b0x, b0y, b0d)], is_mid, columns_of(0, 1, core), occ_energy, vir, mode="lent")
     z, here = together((either(a0d, s_b), here))
-    work(here, [(b0, b0x, b0y, b0d)], [(0, 1)])
+    work(here, [(b0d,)], [(0, 1)], chunks=(3,), added=b_sum)
     v = (here, a1, a3m, a0d, e3, e3x, e3y, e3d, e4, e5, e6, e6x, e6y, e6d, third, fourth, g3x, g3y, l_a, l_b, z)
     v = end_round(v)
     here, a1, a3m, a0d, e3, e3x, e3y, e3d, e4, e5, e6, e6x, e6y, e6d, third, fourth, g3x, g3y, l_a, l_b, z = v
@@ -447,20 +510,17 @@
     moved = exchange()
     e4d, e5d, seventh = along(e4y, e5x, l_b, flip=1)
     last = [(2, 1), (3, 1)]
-    js = [j for w, pair in last for j in columns_of(w, pair, core)]
-    sums = product(
-        here, [(e4, e4x, e4y), (e5, e5x, e5y)], 1, js, occ_energy, vir, mode="part", chunks=(0, 1, 2)
-    )
+    js, js_other = ([j for w, pair in last for j in columns_of(w, pair, c)] for c in (core, 1 - core))
+    sums = begin(here, [(e4, e4x, e4y), (e5, e5x, e5y)], last)
     sums, state["out"] = together((sums, state["out"]))
-    state["out"], state["gots"] = place(state["out"], state["gots"] + moved), []
-    here, e4d, e5d, sums = end_round((here, e4d, e5d, sums), [(seventh, columns_of(1, 1, 1 - core), is_end)])
+    out = place(state["out"], moved)
+    here, e4d, e5d, sums, seventh, out = together((here, e4d, e5d, sums, seventh, out))
     how = dict(chunks=(3,), added=sums)
-    send = product(here, [(e4d,), (e5d,)], 1, js, occ_energy, vir, mode="send", **how)
+    (send,) = product(here, [(e4d,), (e5d,)], 1, js, occ_energy, vir, mode="send", **how)
     got = hop(send, core=1)
-    (out,) = product(
-        here, [(e4d,), (e5d,)], 1, js, occ_energy, vir, mode="mine", out=state["out"], gots=state["gots"], **how
-    )
-    return place(out, [(got, [j for w, pair in last for j in columns_of(w, pair, 1 - core)], 1)])
+    (out,) = product(here, [(e4d,), (e5d,)], 1, js, occ_energy, vir, mode="mine", out=out, **how)
+    js_seventh = [jnp.where(is_end, a, b) for a, b in zip(columns_of(1, 1, 1 - core), js_other)]
+    return finish(out, [(seventh, js_seventh), (got, js_other)])
 
 
 def solution(mesh):

time: 505 us -> 498 us (0.986)
  Pallas kernels: 233 us -> 203 us
  local copies, waits for them, and re-layouts: 13.7 us -> 33.3 us
  waiting for transfers between devices: 186 us -> 198 us
    unnamed x44 -> x82, local copies, waits for them, and re-layouts: 7 us -> 32.2 us
    ppermute x37, waiting for transfers between devices: 181 us -> 193 us  [hop(): return lax.ppermute(value, AXES, pairs)]
    pallas_call x2 -> x1, Pallas kernels: 14.5 us -> 3.39 us  [place(): pl.pallas_call(functools.partial(place_kernel, blocks), grid_spec=pltpu.P...]
    pallas_call x9 -> x11, Pallas kernels: 184 us -> 177 us  [the longest x10 169 us: product(): pl.pallas_call(functools.partial(product_kernel, chunks, starts, [g.shape...]
    pallas_call x2, Pallas kernels: 8.75 us -> 2.57 us  [columns(): pl.pallas_call(functools.partial(columns_kernel, pair), grid_spec=pltpu.P...]
  transfers between devices with their start and end apart: 44 -> 44, of which waited for: 27 -> 25; matrix products, arithmetic and copies ran while one was open for 6% -> 5% of each run, Pallas kernels for 42% -> 37%
where the time goes in v3:
time: 498 us; the launch traced here: 497 us
  Pallas kernels  203 us (41%)
  waiting for transfers between devices  198 us (40%)
  starting transfers between devices  37.2 us (7%)
  local copies, waits for them, and re-layouts  33.3 us (7%)
  other arithmetic  25.1 us (5%)
    ppermute x37, waiting for transfers between devices, hop(): return lax.ppermute(value, AXES, pairs)  193 us
    pallas_call x10, Pallas kernels, product(): pl.pallas_call(functools.partial(product_kernel, chunks, starts, [g.shape...  169 us
    ppermute x37, starting transfers between devices, hop(): return lax.ppermute(value, AXES, pairs)  36.1 us
    unnamed x82, local copies, waits for them, and re-layouts  32.2 us
    select_n x9, other arithmetic, either(): return jnp.where(is_end, at_end, at_mid)  24.6 us
    pallas_call x2, Pallas kernels, rows(): pl.pallas_call(functools.partial(rows_kernel, starts), grid_spec=pltpu.Pr...  16.6 us
  transfers between devices with their start and end apart: 44, of which 25 were waited for; matrix products, arithmetic and copies ran while one was open for 5% of the time, Pallas kernels for 37%

profile of v3, /device:TPU:0, one launch (start us, length us, event | category | flops | bytes accessed | tf_op | source)
XLA Modules:
  0.0 497.1 jit_solution(18147457787443061652)
XLA Ops:
  23.6 32.9 %collective-permute-done.2.refs_1_ = f32[2,4,128,512]{3,2,1,0:T(8,128)} collective-permute-done((f32[2,4,128,512]{3,2,1,0:T(8,128)}, f32[2,4,128,512]{3,2,1,0:T(8,128)}, u32[]{:S(2)}, u32[]{:S(2)}) %collective-permute-start.2) | collective-permute-done | bytes 2097184 | tf_op jit(solution)/shard_map/ppermute | solution.py:372
  64.9 5.1 %collective-permute-done.10 = f32[2,4,128,512]{3,2,1,0:T(8,128)S(1)} collective-permute-done((f32[2,4,128,512]{3,2,1,0:T(8,128)}, f32[2,4,128,512]{3,2,1,0:T(8,128)S(1)}, u32[]{:S(2)}, u32[]{:S(2)}) %collective-permute-start.10) | collective-permute-done | bytes 2097184 | tf_op jit(solution)/shard_map/ppermute | solution.py:378
  70.0 38.4 %collective-permute-done.9 = f32[2,4,128,512]{3,2,1,0:T(8,128)} collective-permute-done((f32[2,4,128,512]{3,2,1,0:T(8,128)S(1)}, f32[2,4,128,512]{3,2,1,0:T(8,128)}, u32[]{:S(2)}, u32[]{:S(2)}) %collective-permute-start.9) | collective-permute-done | bytes 2097184 | tf_op jit(solution)/shard_map/ppermute | solution.py:372
  108.4 4.4 slice_select_fusion.1
  120.0 6.8 %shard_map.50 = (bf16[1024,2048]{1,0:T(8,128)(2,1)S(1)}, bf16[1024,2048]{1,0:T(8,128)(2,1)S(1)}) custom-call(s32[1]{0:T(128)} %bitcast.6.chip_ref, f32[4,4,128,512]{3,2,1,0:T(8,128)} %refs_0_, f32[4,4,128,512]{3,2,1,0:T(8,128)} %copy-done.38), custom_call_target="tpu_custom_call" | custom-call | tf_op jit(solution)/shard_map/pallas_call | solution.py:121
  131.0 20.4 %shard_map.51 = (f32[4,32,128,512]{3,2,1,0:T(8,128)}, f32[2,4,128,512]{3,2,1,0:T(8,128)}) custom-call(s32[3]{0:T(128)S(1)} %fusion.keys, f32[32]{0:T(128)S(1)} %copy-done.18, bf16[1024,2048]{1,0:T(8,128)(2,1)} %copy-done, bf16[1024,2048]{1,0:T(8,128)(2,1)} %copy-done.2, f32[1024,128]{1,0:T(8,128)S(1)} %broadcast_in_dim.4.rowd, ...), custom_call_target="tpu_custom_call", output_to_operand_aliasing={{0}: (10, {})} | custom-call | flops 12884901888 | bytes 29360128 | tf_op jit(solution)/shard_map/pallas_call | solution.py:295
  151.5 12.6 %collective-permute-done.13.refs_0_ = f32[2,4,128,512]{3,2,1,0:T(8,128)} collective-permute-done((f32[2,4,128,512]{3,2,1,0:T(8,128)}, f32[2,4,128,512]{3,2,1,0:T(8,128)}, u32[]{:S(2)}, u32[]{:S(2)}) %collective-permute-start.13) | collective-permute-done | bytes 2097184 | tf_op jit(solution)/shard_map/ppermute | solution.py:372
  173.9 3.6 broadcast_select_fusion.5.refs_4_
  177.5 15.8 %shard_map.52.refs_1_ = f32[2,1024,512]{2,1,0:T(8,128)} custom-call(s32[3]{0:T(128)S(1)} %fusion.1.keys, f32[32]{0:T(128)S(1)} %copy-done.18, bf16[1024,2048]{1,0:T(8,128)(2,1)} %copy-done, bf16[1024,2048]{1,0:T(8,128)(2,1)} %copy-done.2, f32[1024,128]{1,0:T(8,128)S(1)} %broadcast_in_dim.4.rowd, f32[1,512]{1,0:T(1,128)S(1)} %bitcast.46, ...), custom_call_target="tpu_custom_call" | custom-call | flops 9663676416 | bytes 23068672 | tf_op jit(solution)/shard_map/pallas_call | solution.py:295
  196.7 21.4 %collective-permute-done.16.refs_3_.refs_0_ = f32[2,4,128,512]{3,2,1,0:T(8,128)} collective-permute-done((f32[2,4,128,512]{3,2,1,0:T(8,128)}, f32[2,4,128,512]{3,2,1,0:T(8,128)}, u32[]{:S(2)}, u32[]{:S(2)}) %collective-permute-start.16) | collective-permute-done | bytes 2097184 | tf_op jit(solution)/shard_map/ppermute | solution.py:372
  227.0 9.8 %shard_map.53 = (bf16[1024,2048]{1,0:T(8,128)(2,1)}, bf16[1024,2048]{1,0:T(8,128)(2,1)}) custom-call(s32[1]{0:T(128)} %bitcast.6.chip_ref, f32[2,4,128,512]{3,2,1,0:T(8,128)} %collective-permute-done.13.refs_0_, f32[2,4,128,512]{3,2,1,0:T(8,128)} %collective-permute-done.19.refs_1_, f32[2,4,128,512]{3,2,1,0:T(8,128)S(1)} %copy-done.14, ...), custom_call_target="tpu_custom_call" | custom-call | tf_op jit(solution)/shard_map/pallas_call | solution.py:121
  237.1 9.6 %shard_map.54 = (f32[2,4,128,512]{3,2,1,0:T(8,128)S(1)}, f32[2,4,128,512]{3,2,1,0:T(8,128)S(1)}) custom-call(s32[3]{0:T(128)S(1)} %add_add_fusion.keys, f32[32]{0:T(128)S(1)} %copy-done.18, bf16[1024,2048]{1,0:T(8,128)(2,1)} %get-tuple-element.311.a_hi, bf16[1024,2048]{1,0:T(8,128)(2,1)} %get-tuple-element.312.a_lo, f32[1024,128]{1,0:T(8,128)S(1)} %broadcast_in_dim.5.rowd, ...), custom_call_target="tpu_custom_call" | custom-call | flops 12884901888 | bytes 29360128 | tf_op jit(solution)/shard_map/pallas_call | solution.py:295
  248.8 20.0 %collective-permute-done.22.refs_5_ = f32[2,4,128,512]{3,2,1,0:T(8,128)} collective-permute-done((f32[2,4,128,512]{3,2,1,0:T(8,128)}, f32[2,4,128,512]{3,2,1,0:T(8,128)}, u32[]{:S(2)}, u32[]{:S(2)}) %collective-permute-start.22) | collective-permute-done | bytes 2097184 | tf_op jit(solution)/shard_map/ppermute | solution.py:372
  277.3 9.8 %shard_map.55 = (f32[2,4,128,512]{3,2,1,0:T(8,128)S(1)}, f32[2,4,128,512]{3,2,1,0:T(8,128)}) custom-call(s32[3]{0:T(128)S(1)} %add_add_fusion.1.keys, f32[32]{0:T(128)S(1)} %copy-done.18, bf16[1024,2048]{1,0:T(8,128)(2,1)} %get-tuple-element.311.a_hi, bf16[1024,2048]{1,0:T(8,128)(2,1)} %get-tuple-element.312.a_lo, f32[1024,128]{1,0:T(8,128)S(1)} %broadcast_in_dim.5.rowd, ...), custom_call_target="tpu_custom_call" | custom-call | flops 12884901888 | bytes 29360128 | tf_op jit(solution)/shard_map/pallas_call | solution.py:295
  290.4 9.0 %shard_map.56 = (f32[4,32,128,512]{3,2,1,0:T(8,128)}, f32[2,4,128,512]{3,2,1,0:T(8,128)S(1)}) custom-call(s32[6]{0:T(128)S(1)} %stack.196.keys, f32[32]{0:T(128)S(1)} %copy-done.18, bf16[1024,2048]{1,0:T(8,128)(2,1)} %copy-done, bf16[1024,2048]{1,0:T(8,128)(2,1)} %copy-done.2, ...), custom_call_target="tpu_custom_call", output_to_operand_aliasing={{0}: (9, {})} | custom-call | flops 3221225472 | bytes 10485760 | tf_op jit(solution)/shard_map/pallas_call | solution.py:295
  300.7 16.6 %collective-permute-done.26.refs_3_ = f32[2,4,128,512]{3,2,1,0:T(8,128)S(1)} collective-permute-done((f32[2,4,128,512]{3,2,1,0:T(8,128)S(1)}, f32[2,4,128,512]{3,2,1,0:T(8,128)S(1)}, u32[]{:S(2)}, u32[]{:S(2)}) %collective-permute-start.26) | collective-permute-done | bytes 2097184 | tf_op jit(solution)/shard_map/ppermute | solution.py:372
  324.8 37.5 %shard_map.57 = (f32[4,32,128,512]{3,2,1,0:T(8,128)}, f32[4,4,128,512]{3,2,1,0:T(8,128)}) custom-call(s32[8]{0:T(128)S(1)} %stack.205.keys, f32[32]{0:T(128)S(1)} %copy-done.18, bf16[1024,2048]{1,0:T(8,128)(2,1)} %copy-done, bf16[1024,2048]{1,0:T(8,128)(2,1)} %copy-done.2, f32[1024,128]{1,0:T(8,128)S(1)} %broadcast_in_dim.4.rowd, ...), custom_call_target="tpu_custom_call", output_to_operand_aliasing={{0}: (15, {})} | custom-call | flops 25769803776 | bytes 58720256 | tf_op jit(solution)/shard_map/pallas_call | solution.py:295
  373.9 19.3 %shard_map.58 = (f32[4,32,128,512]{3,2,1,0:T(8,128)}, f32[4,4,128,512]{3,2,1,0:T(8,128)}) custom-call(s32[11]{0:T(128)S(1)} %stack.212.keys, f32[32]{0:T(128)S(1)} %copy-done.18, bf16[1024,2048]{1,0:T(8,128)(2,1)} %copy-done, bf16[1024,2048]{1,0:T(8,128)(2,1)} %copy-done.2, f32[1024,128]{1,0:T(8,128)S(1)} %broadcast_in_dim.4.rowd, ...), custom_call_target="tpu_custom_call", output_to_operand_aliasing={{0}: (16, {})} | custom-call | flops 25769803776 | bytes 58720256 | tf_op jit(solution)/shard_map/pallas_call | solution.py:295
  393.2 22.7 %collective-permute-done.35.refs_4_ = f32[2,4,128,512]{3,2,1,0:T(8,128)} collective-permute-done((f32[2,4,128,512]{3,2,1,0:T(8,128)S(1)}, f32[2,4,128,512]{3,2,1,0:T(8,128)}, u32[]{:S(2)}, u32[]{:S(2)}) %collective-permute-start.35) | collective-permute-done | bytes 2097184 | tf_op jit(solution)/shard_map/ppermute | solution.py:372
  426.6 30.3 %shard_map.59 = (f32[4,32,128,512]{3,2,1,0:T(8,128)}, f32[4,1024,512]{2,1,0:T(8,128)}) custom-call(s32[13]{0:T(128)S(1)} %stack.223.keys, f32[32]{0:T(128)S(1)} %copy-done.18, bf16[1024,2048]{1,0:T(8,128)(2,1)} %copy-done, bf16[1024,2048]{1,0:T(8,128)(2,1)} %copy-done.2, f32[1024,128]{1,0:T(8,128)S(1)} %broadcast_in_dim.4.rowd, ...), custom_call_target="tpu_custom_call", output_to_operand_aliasing={{0}: (14, {})} | custom-call | flops 19327352832 | bytes 46137344 | tf_op jit(solution)/shard_map/pallas_call | solution.py:295
  460.3 6.9 %collective-permute-done.39.refs_0_ = f32[2,4,128,512]{3,2,1,0:T(8,128)S(1)} collective-permute-done((f32[2,4,128,512]{3,2,1,0:T(8,128)}, f32[2,4,128,512]{3,2,1,0:T(8,128)S(1)}, u32[]{:S(2)}, u32[]{:S(2)}) %collective-permute-start.39) | collective-permute-done | bytes 2097184 | tf_op jit(solution)/shard_map/ppermute | solution.py:372
  469.2 8.9 %shard_map.61 = f32[4,4,128,512]{3,2,1,0:T(8,128)} custom-call(s32[5]{0:T(128)S(1)} %stack.227.keys, f32[32]{0:T(128)S(1)} %copy-done.18, bf16[1024,2048]{1,0:T(8,128)(2,1)} %copy-done, bf16[1024,2048]{1,0:T(8,128)(2,1)} %copy-done.2, f32[1024,128]{1,0:T(8,128)S(1)} %broadcast_in_dim.4.rowd, f32[1,512]{1,0:T(1,128)S(1)} %bitcast.53, ...), custom_call_target="tpu_custom_call" | custom-call | flops 3221225472 | bytes 20971520 | tf_op jit(solution)/shard_map/pallas_call | solution.py:295
  480.4 8.8 %shard_map.62.refs_2_ = f32[4,32,128,512]{3,2,1,0:T(8,128)} custom-call(s32[5]{0:T(128)S(1)} %stack.227.keys, f32[32]{0:T(128)S(1)} %copy-done.18, bf16[1024,2048]{1,0:T(8,128)(2,1)S(1)} %copy-done.1, bf16[1024,2048]{1,0:T(8,128)(2,1)} %copy-done.2, f32[1024,128]{1,0:T(8,128)S(1)} %broadcast_in_dim.4.rowd, ...), custom_call_target="tpu_custom_call", output_to_operand_aliasing={{}: (9, {})} | custom-call | flops 3221225472 | bytes 20971520 | tf_op jit(solution)/shard_map/pallas_call | solution.py:295
  489.2 7.9 %shard_map.63 = f32[4,32,128,512]{3,2,1,0:T(8,128)} custom-call(s32[6]{0:T(128)S(1)} %stack.183.keys, f32[2,4,128,512]{3,2,1,0:T(8,128)} %collective-permute-done.41.refs_0_, f32[4,4,128,512]{3,2,1,0:T(8,128)} %collective-permute-done.43.refs_1_, f32[4,32,128,512]{3,2,1,0:T(8,128)} %shard_map.62.refs_2_), custom_call_target="tpu_custom_call", output_to_operand_aliasing={{}: (3, {})} | custom-call | tf_op jit(solution)/shard_map/pallas_call | solution.py:350
  (190 shorter events, 118.0 us)
Async XLA Ops:
  7.4 49.1 %collective-permute-start.2 = (f32[2,4,128,512]{3,2,1,0:T(8,128)}, f32[2,4,128,512]{3,2,1,0:T(8,128)}, u32[]{:S(2)}, u32[]{:S(2)}) collective-permute-start(f32[2,4,128,512]{3,2,1,0:T(8,128)} %get-tuple-element.300.refs_0_), channel_id=1, source_target_pairs={{0,8},{1,9},{2,10},{3,11},{4,12},{5,13},{6,14},{7,15},{8,0},{9,1},... | collective-permute-start | bytes 6291464 | tf_op jit(solution)/shard_map/ppermute | solution.py:372
  10.1 47.8 %collective-permute-start.3 = (f32[2,4,128,512]{3,2,1,0:T(8,128)}, f32[2,4,128,512]{3,2,1,0:T(8,128)S(1)}, u32[]{:S(2)}, u32[]{:S(2)}) collective-permute-start(f32[2,4,128,512]{3,2,1,0:T(8,128)} %get-tuple-element.300.refs_0_), channel_id=1, source_target_pairs={{0,16},{1,17},{2,18},{3,19},{4,20},{5,21},{6,22},{7,23},{8,24},{9,... | collective-permute-start | bytes 6291464 | tf_op jit(solution)/shard_map/ppermute | solution.py:372
  11.6 48.4 %collective-permute-start.4 = (f32[2,4,128,512]{3,2,1,0:T(8,128)}, f32[2,4,128,512]{3,2,1,0:T(8,128)}, u32[]{:S(2)}, u32[]{:S(2)}) collective-permute-start(f32[2,4,128,512]{3,2,1,0:T(8,128)} %get-tuple-element.300.refs_0_), channel_id=1, source_target_pairs={{0,1},{1,0},{2,3},{3,2},{4,5},{5,4},{6,7},{7,6},{8,9},{9,8},{10,11... | collective-permute-start | bytes 6291464 | tf_op jit(solution)/shard_map/ppermute | solution.py:372
  60.0 54.2 %collective-permute-start.6 = (f32[4,4,128,512]{3,2,1,0:T(8,128)S(1)}, f32[4,4,128,512]{3,2,1,0:T(8,128)S(1)}, u32[]{:S(2)}, u32[]{:S(2)}) collective-permute-start(f32[4,4,128,512]{3,2,1,0:T(8,128)S(1)} %copy-done.33), channel_id=1, source_target_pairs={{0,4},{1,5},{2,6},{3,7},{4,0},{5,1},{6,2},{7,3},{8,12},{9,13},{10,... | collective-permute-start | bytes 12582920 | tf_op jit(solution)/shard_map/ppermute | solution.py:372
  60.6 47.8 %collective-permute-start.9 = (f32[2,4,128,512]{3,2,1,0:T(8,128)S(1)}, f32[2,4,128,512]{3,2,1,0:T(8,128)}, u32[]{:S(2)}, u32[]{:S(2)}) collective-permute-start(f32[2,4,128,512]{3,2,1,0:T(8,128)S(1)} %broadcast_select_fusion.7), channel_id=1, source_target_pairs={{0,1},{1,0},{2,3},{3,2},{4,5},{5,4},{6,7},{7,6},{8,9},{9,8},{10,11... | collective-permute-start | bytes 6291464 | tf_op jit(solution)/shard_map/ppermute | solution.py:372
  62.3 50.5 %collective-permute-start.7 = (f32[2,4,128,512]{3,2,1,0:T(8,128)S(1)}, f32[2,4,128,512]{3,2,1,0:T(8,128)S(1)}, u32[]{:S(2)}, u32[]{:S(2)}) collective-permute-start(f32[2,4,128,512]{3,2,1,0:T(8,128)S(1)} %collective-permute-done.3.refs_2_), channel_id=1, source_target_pairs={{0,8},{1,9},{2,10},{3,11},{4,12},{5,13},{6,14},{7,15},{8,0},{9,1},... | collective-permute-start | bytes 6291464 | tf_op jit(solution)/shard_map/ppermute | solution.py:372
  63.4 49.4 %collective-permute-start.8 = (f32[2,4,128,512]{3,2,1,0:T(8,128)S(1)}, f32[2,4,128,512]{3,2,1,0:T(8,128)S(1)}, u32[]{:S(2)}, u32[]{:S(2)}) collective-permute-start(f32[2,4,128,512]{3,2,1,0:T(8,128)S(1)} %shard_map.49.refs_0_), channel_id=1, source_target_pairs={{0,16},{1,17},{2,18},{3,19},{4,20},{5,21},{6,22},{7,23},{8,24},{9,... | collective-permute-start | bytes 6291464 | tf_op jit(solution)/shard_map/ppermute | solution.py:372
  116.8 47.2 %collective-permute-start.13 = (f32[2,4,128,512]{3,2,1,0:T(8,128)}, f32[2,4,128,512]{3,2,1,0:T(8,128)}, u32[]{:S(2)}, u32[]{:S(2)}) collective-permute-start(f32[2,4,128,512]{3,2,1,0:T(8,128)} %get-tuple-element.242), channel_id=1, source_target_pairs={{0,1},{1,0},{2,3},{3,2},{4,5},{5,4},{6,7},{7,6},{8,9},{9,8},{10,11... | collective-permute-start | bytes 6291464 | tf_op jit(solution)/shard_map/ppermute | solution.py:372
  117.4 48.7 %collective-permute-start.11 = (f32[2,4,128,512]{3,2,1,0:T(8,128)}, f32[2,4,128,512]{3,2,1,0:T(8,128)}, u32[]{:S(2)}, u32[]{:S(2)}) collective-permute-start(f32[2,4,128,512]{3,2,1,0:T(8,128)} %copy-done.7), channel_id=1, source_target_pairs={{0,8},{1,9},{2,10},{3,11},{4,12},{5,13},{6,14},{7,15},{8,0},{9,1},... | collective-permute-start | bytes 6291464 | tf_op jit(solution)/shard_map/ppermute | solution.py:372
  118.5 48.0 %collective-permute-start.12 = (f32[2,4,128,512]{3,2,1,0:T(8,128)}, f32[2,4,128,512]{3,2,1,0:T(8,128)S(1)}, u32[]{:S(2)}, u32[]{:S(2)}) collective-permute-start(f32[2,4,128,512]{3,2,1,0:T(8,128)} %get-tuple-element.362.refs_0_), channel_id=1, source_target_pairs={{0,16},{1,17},{2,18},{3,19},{4,20},{5,21},{6,22},{7,23},{8,24},{9,... | collective-permute-start | bytes 6291464 | tf_op jit(solution)/shard_map/ppermute | solution.py:372
  169.9 48.2 %collective-permute-start.16 = (f32[2,4,128,512]{3,2,1,0:T(8,128)}, f32[2,4,128,512]{3,2,1,0:T(8,128)}, u32[]{:S(2)}, u32[]{:S(2)}) collective-permute-start(f32[2,4,128,512]{3,2,1,0:T(8,128)} %collective-permute-done.11.refs_1_), channel_id=1, source_target_pairs={{0,16},{1,17},{2,18},{3,19},{4,20},{5,21},{6,22},{7,23},{8,24},{9,... | collective-permute-start | bytes 6291464 | tf_op jit(solution)/shard_map/ppermute | solution.py:372
  171.3 47.9 %collective-permute-start.18 = (f32[2,4,128,512]{3,2,1,0:T(8,128)}, f32[2,4,128,512]{3,2,1,0:T(8,128)}, u32[]{:S(2)}, u32[]{:S(2)}) collective-permute-start(f32[2,4,128,512]{3,2,1,0:T(8,128)} %get-tuple-element.362.refs_0_), channel_id=1, source_target_pairs={{0,8},{1,9},{2,10},{3,11},{4,12},{5,13},{6,14},{7,15},{8,0},{9,1},... | collective-permute-start | bytes 6291464 | tf_op jit(solution)/shard_map/ppermute | solution.py:372
  172.8 47.6 %collective-permute-start.19 = (f32[2,4,128,512]{3,2,1,0:T(8,128)}, f32[2,4,128,512]{3,2,1,0:T(8,128)}, u32[]{:S(2)}, u32[]{:S(2)}) collective-permute-start(f32[2,4,128,512]{3,2,1,0:T(8,128)} %slice_select_fusion), channel_id=1, source_target_pairs={{0,1},{1,0},{2,3},{3,2},{4,5},{5,4},{6,7},{7,6},{8,9},{9,8},{10,11... | collective-permute-start | bytes 6291464 | tf_op jit(solution)/shard_map/ppermute | solution.py:372
  220.4 48.4 %collective-permute-start.22 = (f32[2,4,128,512]{3,2,1,0:T(8,128)}, f32[2,4,128,512]{3,2,1,0:T(8,128)}, u32[]{:S(2)}, u32[]{:S(2)}) collective-permute-start(f32[2,4,128,512]{3,2,1,0:T(8,128)} %broadcast_select_fusion.5.refs_4_), channel_id=1, source_target_pairs={{0,8},{1,9},{2,10},{3,11},{4,12},{5,13},{6,14},{7,15},{8,0},{9,1},... | collective-permute-start | bytes 6291464 | tf_op jit(solution)/shard_map/ppermute | solution.py:372
  221.0 48.1 %collective-permute-start.23 = (f32[2,4,128,512]{3,2,1,0:T(8,128)}, f32[2,4,128,512]{3,2,1,0:T(8,128)}, u32[]{:S(2)}, u32[]{:S(2)}) collective-permute-start(f32[2,4,128,512]{3,2,1,0:T(8,128)} %broadcast_select_fusion.5.refs_4_), channel_id=1, source_target_pairs={{0,16},{1,17},{2,18},{3,19},{4,20},{5,21},{6,22},{7,23},{8,24},{9,... | collective-permute-start | bytes 6291464 | tf_op jit(solution)/shard_map/ppermute | solution.py:372
  221.6 48.8 %collective-permute-start.24 = (f32[2,4,128,512]{3,2,1,0:T(8,128)}, f32[2,4,128,512]{3,2,1,0:T(8,128)}, u32[]{:S(2)}, u32[]{:S(2)}) collective-permute-start(f32[2,4,128,512]{3,2,1,0:T(8,128)} %broadcast_select_fusion.4), channel_id=1, source_target_pairs={{0,1},{1,0},{2,3},{3,2},{4,5},{5,4},{6,7},{7,6},{8,9},{9,8},{10,11... | collective-permute-start | bytes 6291464 | tf_op jit(solution)/shard_map/ppermute | solution.py:372
  271.0 47.6 %collective-permute-start.27 = (f32[2,4,128,512]{3,2,1,0:T(8,128)}, f32[2,4,128,512]{3,2,1,0:T(8,128)}, u32[]{:S(2)}, u32[]{:S(2)}) collective-permute-start(f32[2,4,128,512]{3,2,1,0:T(8,128)} %collective-permute-done.22.refs_5_), channel_id=1, source_target_pairs={{0,16},{1,17},{2,18},{3,19},{4,20},{5,21},{6,22},{7,23},{8,24},{9,... | collective-permute-start | bytes 6291464 | tf_op jit(solution)/shard_map/ppermute | solution.py:372
  367.6 50.5 %collective-permute-start.37 = (f32[4,4,128,512]{3,2,1,0:T(8,128)}, f32[4,4,128,512]{3,2,1,0:T(8,128)}, u32[]{:S(2)}, u32[]{:S(2)}) collective-permute-start(f32[4,4,128,512]{3,2,1,0:T(8,128)} %get-tuple-element.381), channel_id=1, source_target_pairs={{0,4},{1,5},{2,6},{3,7},{4,0},{5,1},{6,2},{7,3},{8,12},{9,13},{10,... | collective-permute-start | bytes 12582920 | tf_op jit(solution)/shard_map/ppermute | solution.py:372
  367.7 48.2 %collective-permute-start.35 = (f32[2,4,128,512]{3,2,1,0:T(8,128)S(1)}, f32[2,4,128,512]{3,2,1,0:T(8,128)}, u32[]{:S(2)}, u32[]{:S(2)}) collective-permute-start(f32[2,4,128,512]{3,2,1,0:T(8,128)S(1)} %copy-done.11), channel_id=1, source_target_pairs={{0,8},{1,9},{2,10},{3,11},{4,12},{5,13},{6,14},{7,15},{8,0},{9,1},... | collective-permute-start | bytes 6291464 | tf_op jit(solution)/shard_map/ppermute | solution.py:372
  368.4 47.7 %collective-permute-start.36 = (f32[2,4,128,512]{3,2,1,0:T(8,128)S(1)}, f32[2,4,128,512]{3,2,1,0:T(8,128)S(1)}, u32[]{:S(2)}, u32[]{:S(2)}) collective-permute-start(f32[2,4,128,512]{3,2,1,0:T(8,128)S(1)} %copy-done.11), channel_id=1, source_target_pairs={{0,16},{1,17},{2,18},{3,19},{4,20},{5,21},{6,22},{7,23},{8,24},{9,... | collective-permute-start | bytes 6291464 | tf_op jit(solution)/shard_map/ppermute | solution.py:372
  370.1 48.0 %collective-permute-start.38 = (f32[2,4,128,512]{3,2,1,0:T(8,128)}, f32[2,4,128,512]{3,2,1,0:T(8,128)S(1)}, u32[]{:S(2)}, u32[]{:S(2)}) collective-permute-start(f32[2,4,128,512]{3,2,1,0:T(8,128)} %copy-done.23), channel_id=1, source_target_pairs={{0,5},{1,4},{2,7},{3,6},{4,1},{5,0},{6,3},{7,2},{8,13},{9,12},{10,... | collective-permute-start | bytes 6291464 | tf_op jit(solution)/shard_map/ppermute | solution.py:372
  419.4 47.9 %collective-permute-start.39 = (f32[2,4,128,512]{3,2,1,0:T(8,128)}, f32[2,4,128,512]{3,2,1,0:T(8,128)S(1)}, u32[]{:S(2)}, u32[]{:S(2)}) collective-permute-start(f32[2,4,128,512]{3,2,1,0:T(8,128)} %collective-permute-done.31.refs_2_), channel_id=1, source_target_pairs={{0,8},{1,9},{2,10},{3,11},{4,12},{5,13},{6,14},{7,15},{8,0},{9,1},... | collective-permute-start | bytes 6291464 | tf_op jit(solution)/shard_map/ppermute | solution.py:372
  419.9 47.7 %collective-permute-start.40 = (f32[2,4,128,512]{3,2,1,0:T(8,128)}, f32[2,4,128,512]{3,2,1,0:T(8,128)}, u32[]{:S(2)}, u32[]{:S(2)}) collective-permute-start(f32[2,4,128,512]{3,2,1,0:T(8,128)} %collective-permute-done.35.refs_4_), channel_id=1, source_target_pairs={{0,16},{1,17},{2,18},{3,19},{4,20},{5,21},{6,22},{7,23},{8,24},{9,... | collective-permute-start | bytes 6291464 | tf_op jit(solution)/shard_map/ppermute | solution.py:372
  421.2 48.0 %collective-permute-start.41 = (f32[2,4,128,512]{3,2,1,0:T(8,128)}, f32[2,4,128,512]{3,2,1,0:T(8,128)}, u32[]{:S(2)}, u32[]{:S(2)}) collective-permute-start(f32[2,4,128,512]{3,2,1,0:T(8,128)} %get-tuple-element.410), channel_id=1, source_target_pairs={{0,5},{1,4},{2,7},{3,6},{4,1},{5,0},{6,3},{7,2},{8,13},{9,12},{10,... | collective-permute-start | bytes 6291464 | tf_op jit(solution)/shard_map/ppermute | solution.py:372
  (61 other events, 1189.1 us)

commit v4 on v3

--- a/solution.py
+++ b/solution.py
@@ -68,7 +68,7 @@
             out_specs=[pl.BlockSpec((2, 1, cs, width), lambda k, _: (0, k, 0, 0))] * 2,
         ),
         out_shape=[jax.ShapeDtypeStruct((2, ks, cs, width), jnp.float32)] * 2,
-        compiler_params=pltpu.CompilerParams(vmem_limit_bytes=VMEM),
+        compiler_params=pltpu.CompilerParams(vmem_limit_bytes=VMEM // 2),
     )(core.reshape(1), integrals)
 
 
@@ -91,7 +91,7 @@
         ),
         out_shape=[jax.ShapeDtypeStruct((2, ks, 2 * cs, width), jnp.float32)]
         + [jax.ShapeDtypeStruct(r, jnp.float32) for r in [room] if r],
-        compiler_params=pltpu.CompilerParams(vmem_limit_bytes=VMEM),
+        compiler_params=pltpu.CompilerParams(vmem_limit_bytes=VMEM // 2),
     )(core.reshape(1), mine, other)
 
 
@@ -130,7 +130,7 @@
             out_specs=[pl.BlockSpec((rows_a, ks * depth), lambda s, _: (s, 0))] * 2,
         ),
         out_shape=[shape, shape],
-        compiler_params=pltpu.CompilerParams(vmem_limit_bytes=VMEM),
+        compiler_params=pltpu.CompilerParams(vmem_limit_bytes=VMEM // 2),
     )(chip.reshape(1), *values)
 
 
@@ -299,7 +299,7 @@
         ),
         out_shape=out_shape,
         input_output_aliases=alias,
-        compiler_params=pltpu.CompilerParams(vmem_limit_bytes=VMEM),
+        compiler_params=pltpu.CompilerParams(vmem_limit_bytes=VMEM if len(sets) > 1 else 3 * VMEM // 4),
         cost_estimate=pl.CostEstimate(
             flops=6 * count * size * depth * width // (2 // tiles),
             bytes_accessed=4 * count * (size * (depth + width) + depth * width),
@@ -328,41 +328,28 @@
         ),
         out_shape=jax.ShapeDtypeStruct(out.shape, out.dtype),
         input_output_aliases={len(gots) + 1: 0},
-        compiler_params=pltpu.CompilerParams(vmem_limit_bytes=VMEM),
+        compiler_params=pltpu.CompilerParams(vmem_limit_bytes=VMEM // 2),
     )(keys, *[g for g, _, _ in gots], out)
 
 
-def finish_kernel(starts, keys, *refs):
-    sources, out = refs[: len(starts) - 1], refs[-1]
-    for n, source in enumerate(sources):
-
-        @pl.when((pl.program_id(0) >= starts[n]) & (pl.program_id(0) < starts[n + 1]))
-        def _(source=source):
-            out[:, 0] = source[0]
-
-
-def finish(out, gots):
-    keys = jnp.stack([jnp.asarray(j, jnp.int32) for _, js in gots for j in js])
-    starts = [0]
-    for got, _ in gots:
-        starts.append(starts[-1] + got.shape[0])
+def finish_kernel(keys, got, _, out):
+    out[:, 0] = got[0]
+
+
+def finish(out, got, js):
     rows_i, _, rows_a, width = out.shape
     return pl.pallas_call(
-        functools.partial(finish_kernel, starts),
+        finish_kernel,
         grid_spec=pltpu.PrefetchScalarGridSpec(
             num_scalar_prefetch=1,
-            grid=(starts[-1],),
-            in_specs=[
-                pl.BlockSpec((1, *g.shape[1:]), lambda b, _, at=at, n=g.shape[0]: (jnp.clip(b - at, 0, n - 1), 0, 0, 0))
-                for at, (g, _) in zip(starts, gots)
-            ]
-            + [HBM],
+            grid=(got.shape[0],),
+            in_specs=[pl.BlockSpec((1, *got.shape[1:]), lambda b, _: (b, 0, 0, 0)), HBM],
             out_specs=pl.BlockSpec((rows_i, 1, rows_a, width), lambda b, keys: (0, keys[b], 0, 0)),
         ),
         out_shape=jax.ShapeDtypeStruct(out.shape, out.dtype),
-        input_output_aliases={len(gots) + 1: 0},
-        compiler_params=pltpu.CompilerParams(vmem_limit_bytes=VMEM),
-    )(keys, *[g for g, _ in gots], out)
+        input_output_aliases={2: 0},
+        compiler_params=pltpu.CompilerParams(vmem_limit_bytes=VMEM // 2),
+    )(jnp.stack(js), got, out)
 
 
 def hop(value, mask=0, planes=None, core=0):
@@ -516,11 +503,11 @@
     out = place(state["out"], moved)
     here, e4d, e5d, sums, seventh, out = together((here, e4d, e5d, sums, seventh, out))
     how = dict(chunks=(3,), added=sums)
-    (send,) = product(here, [(e4d,), (e5d,)], 1, js, occ_energy, vir, mode="send", **how)
+    gots = [(seventh, columns_of(1, 1, 1 - core), is_end)]
+    out, send = product(here, [(e4d,), (e5d,)], 1, js, occ_energy, vir, mode="send", out=out, gots=gots, **how)
     got = hop(send, core=1)
     (out,) = product(here, [(e4d,), (e5d,)], 1, js, occ_energy, vir, mode="mine", out=out, **how)
-    js_seventh = [jnp.where(is_end, a, b) for a, b in zip(columns_of(1, 1, 1 - core), js_other)]
-    return finish(out, [(seventh, js_seventh), (got, js_other)])
+    return finish(out, got, js_other)
 
 
 def solution(mesh):

time: 498 us -> 496 us (level)
  Pallas kernels: 203 us -> 183 us
  waiting for transfers between devices: 198 us -> 208 us
  local copies, waits for them, and re-layouts: 33.3 us -> 42.1 us
    pallas_call x10, Pallas kernels: 169 us -> 160 us  [product(): pl.pallas_call(functools.partial(product_kernel, chunks, starts, [g.shape...]
    ppermute x37, waiting for transfers between devices: 193 us -> 202 us  [hop(): return lax.ppermute(value, AXES, pairs)]
    unnamed x82 -> x90, local copies, waits for them, and re-layouts: 32.2 us -> 41 us
    pallas_call x2, Pallas kernels: 16.6 us -> 9.24 us  [rows(): pl.pallas_call(functools.partial(rows_kernel, starts), grid_spec=pltpu.Pr...]
  transfers between devices with their start and end apart: 44 -> 44, of which waited for: 25 -> 27; matrix products, arithmetic and copies ran while one was open for 5% -> 5% of each run, Pallas kernels for 37% -> 34%
where the time goes in v4:
time: 496 us; the launch traced here: 494 us
  waiting for transfers between devices  208 us (42%)
  Pallas kernels  183 us (37%)
  local copies, waits for them, and re-layouts  42.1 us (8%)
  starting transfers between devices  36.1 us (7%)
  other arithmetic  25 us (5%)
    ppermute x37, waiting for transfers between devices, hop(): return lax.ppermute(value, AXES, pairs)  202 us
    pallas_call x10, Pallas kernels, product(): pl.pallas_call(functools.partial(product_kernel, chunks, starts, [g.shape...  160 us
    unnamed x90, local copies, waits for them, and re-layouts  41 us
    ppermute x37, starting transfers between devices, hop(): return lax.ppermute(value, AXES, pairs)  35.1 us
    select_n x9, other arithmetic, either(): return jnp.where(is_end, at_end, at_mid)  24.5 us
  transfers between devices with their start and end apart: 44, of which 27 were waited for; matrix products, arithmetic and copies ran while one was open for 5% of the time, Pallas kernels for 34%

profile of v4, /device:TPU:0, one launch (start us, length us, event | category | flops | bytes accessed | tf_op | source)
XLA Modules:
  0.0 494.3 jit_solution(11638354120240667835)
XLA Ops:
  23.3 33.2 %collective-permute-done.2.refs_1_ = f32[2,4,128,512]{3,2,1,0:T(8,128)} collective-permute-done((f32[2,4,128,512]{3,2,1,0:T(8,128)}, f32[2,4,128,512]{3,2,1,0:T(8,128)}, u32[]{:S(2)}, u32[]{:S(2)}) %collective-permute-start.2) | collective-permute-done | bytes 2097184 | tf_op jit(solution)/shard_map/ppermute | solution.py:359
  64.7 5.4 %collective-permute-done.10 = f32[2,4,128,512]{3,2,1,0:T(8,128)S(1)} collective-permute-done((f32[2,4,128,512]{3,2,1,0:T(8,128)}, f32[2,4,128,512]{3,2,1,0:T(8,128)S(1)}, u32[]{:S(2)}, u32[]{:S(2)}) %collective-permute-start.10) | collective-permute-done | bytes 2097184 | tf_op jit(solution)/shard_map/ppermute | solution.py:365
  70.1 38.4 %collective-permute-done.9 = f32[2,4,128,512]{3,2,1,0:T(8,128)} collective-permute-done((f32[2,4,128,512]{3,2,1,0:T(8,128)S(1)}, f32[2,4,128,512]{3,2,1,0:T(8,128)}, u32[]{:S(2)}, u32[]{:S(2)}) %collective-permute-start.9) | collective-permute-done | bytes 2097184 | tf_op jit(solution)/shard_map/ppermute | solution.py:359
  108.4 4.4 slice_select_fusion.1
  125.9 22.0 %shard_map.51 = (f32[4,32,128,512]{3,2,1,0:T(8,128)}, f32[2,4,128,512]{3,2,1,0:T(8,128)}) custom-call(s32[3]{0:T(128)S(1)} %fusion.keys, f32[32]{0:T(128)S(1)} %copy-done.27, bf16[1024,2048]{1,0:T(8,128)(2,1)S(1)} %get-tuple-element.415.a_hi, bf16[1024,2048]{1,0:T(8,128)(2,1)S(1)} %get-tuple-element.416.a_lo, ...), custom_call_target="tpu_custom_call", output_to_operand_aliasing={{0}: (10, {})} | custom-call | flops 12884901888 | bytes 29360128 | tf_op jit(solution)/shard_map/pallas_call | solution.py:295
  147.9 15.4 %collective-permute-done.13.refs_0_ = f32[2,4,128,512]{3,2,1,0:T(8,128)} collective-permute-done((f32[2,4,128,512]{3,2,1,0:T(8,128)}, f32[2,4,128,512]{3,2,1,0:T(8,128)}, u32[]{:S(2)}, u32[]{:S(2)}) %collective-permute-start.13) | collective-permute-done | bytes 2097184 | tf_op jit(solution)/shard_map/ppermute | solution.py:359
  172.4 3.6 broadcast_select_fusion.5.refs_4_
  180.2 13.4 %shard_map.52.refs_1_ = f32[2,1024,512]{2,1,0:T(8,128)S(1)} custom-call(s32[3]{0:T(128)S(1)} %fusion.1.keys, f32[32]{0:T(128)S(1)} %copy-done.27, bf16[1024,2048]{1,0:T(8,128)(2,1)S(1)} %copy-done.1, bf16[1024,2048]{1,0:T(8,128)(2,1)S(1)} %copy-done.5, f32[1024,128]{1,0:T(8,128)S(1)} %broadcast_in_dim.4.rowd, f32[1,512]{1,0:T(1,128)S(1)} %bitcast.46, ...), custom_call_target="tpu_custom_call" | custom-call | flops 9663676416 | bytes 23068672 | tf_op jit(solution)/shard_map/pallas_call | solution.py:295
  193.7 4.9 broadcast_select_fusion.4
  198.6 18.8 %collective-permute-done.16.refs_3_.refs_0_ = f32[2,4,128,512]{3,2,1,0:T(8,128)} collective-permute-done((f32[2,4,128,512]{3,2,1,0:T(8,128)}, f32[2,4,128,512]{3,2,1,0:T(8,128)}, u32[]{:S(2)}, u32[]{:S(2)}) %collective-permute-start.16) | collective-permute-done | bytes 2097184 | tf_op jit(solution)/shard_map/ppermute | solution.py:359
  226.1 6.9 %shard_map.53 = (bf16[1024,2048]{1,0:T(8,128)(2,1)S(1)}, bf16[1024,2048]{1,0:T(8,128)(2,1)S(1)}) custom-call(s32[1]{0:T(128)} %bitcast.11.chip_ref, f32[2,4,128,512]{3,2,1,0:T(8,128)} %collective-permute-done.13.refs_0_, f32[2,4,128,512]{3,2,1,0:T(8,128)} %collective-permute-done.19.refs_1_, f32[2,4,128,512]{3,2,1,0:T(8,128)S(1)} %copy-done.23, ...), custom_call_target="tpu_custom_call" | custom-call | tf_op jit(solution)/shard_map/pallas_call | solution.py:121
  238.8 4.3 shard_map.54
  245.2 22.6 %collective-permute-done.22.refs_5_ = f32[2,4,128,512]{3,2,1,0:T(8,128)} collective-permute-done((f32[2,4,128,512]{3,2,1,0:T(8,128)}, f32[2,4,128,512]{3,2,1,0:T(8,128)}, u32[]{:S(2)}, u32[]{:S(2)}) %collective-permute-start.22) | collective-permute-done | bytes 2097184 | tf_op jit(solution)/shard_map/ppermute | solution.py:359
  278.6 5.3 %shard_map.55 = (f32[2,4,128,512]{3,2,1,0:T(8,128)S(1)}, f32[2,4,128,512]{3,2,1,0:T(8,128)}) custom-call(s32[3]{0:T(128)S(1)} %add_add_fusion.1.keys, f32[32]{0:T(128)S(1)} %copy-done.27, bf16[1024,2048]{1,0:T(8,128)(2,1)S(1)} %copy-done.29, bf16[1024,2048]{1,0:T(8,128)(2,1)S(1)} %copy-done.32, f32[1024,128]{1,0:T(8,128)S(1)} %broadcast_in_dim.5.rowd, ...), custom_call_target="tpu_custom_call" | custom-call | flops 12884901888 | bytes 29360128 | tf_op jit(solution)/shard_map/pallas_call | solution.py:295
  288.8 7.7 %shard_map.56 = (f32[4,32,128,512]{3,2,1,0:T(8,128)}, f32[2,4,128,512]{3,2,1,0:T(8,128)S(1)}) custom-call(s32[6]{0:T(128)S(1)} %stack.206.keys, f32[32]{0:T(128)S(1)} %copy-done.27, bf16[1024,2048]{1,0:T(8,128)(2,1)S(1)} %copy-done.2, bf16[1024,2048]{1,0:T(8,128)(2,1)S(1)} %copy-done.6, ...), custom_call_target="tpu_custom_call", output_to_operand_aliasing={{0}: (9, {})} | custom-call | flops 3221225472 | bytes 10485760 | tf_op jit(solution)/shard_map/pallas_call | solution.py:295
  296.6 20.2 %collective-permute-done.26.refs_3_ = f32[2,4,128,512]{3,2,1,0:T(8,128)} collective-permute-done((f32[2,4,128,512]{3,2,1,0:T(8,128)}, f32[2,4,128,512]{3,2,1,0:T(8,128)}, u32[]{:S(2)}, u32[]{:S(2)}) %collective-permute-start.26) | collective-permute-done | bytes 2097184 | tf_op jit(solution)/shard_map/ppermute | solution.py:359
  322.3 38.4 %shard_map.57 = (f32[4,32,128,512]{3,2,1,0:T(8,128)}, f32[4,4,128,512]{3,2,1,0:T(8,128)}) custom-call(s32[8]{0:T(128)S(1)} %stack.213.keys, f32[32]{0:T(128)S(1)} %copy-done.27, bf16[1024,2048]{1,0:T(8,128)(2,1)} %copy-done, bf16[1024,2048]{1,0:T(8,128)(2,1)} %copy-done.4, f32[1024,128]{1,0:T(8,128)S(1)} %broadcast_in_dim.4.rowd, ...), custom_call_target="tpu_custom_call", output_to_operand_aliasing={{0}: (15, {})} | custom-call | flops 25769803776 | bytes 58720256 | tf_op jit(solution)/shard_map/pallas_call | solution.py:295
  370.9 19.9 %shard_map.58 = (f32[4,32,128,512]{3,2,1,0:T(8,128)}, f32[4,4,128,512]{3,2,1,0:T(8,128)}) custom-call(s32[11]{0:T(128)S(1)} %stack.220.keys, f32[32]{0:T(128)S(1)} %copy-done.27, bf16[1024,2048]{1,0:T(8,128)(2,1)} %copy-done, bf16[1024,2048]{1,0:T(8,128)(2,1)} %copy-done.4, f32[1024,128]{1,0:T(8,128)S(1)} %broadcast_in_dim.4.rowd, ...), custom_call_target="tpu_custom_call", output_to_operand_aliasing={{0}: (16, {})} | custom-call | flops 25769803776 | bytes 58720256 | tf_op jit(solution)/shard_map/pallas_call | solution.py:295
  390.8 24.2 %collective-permute-done.35.refs_4_ = f32[2,4,128,512]{3,2,1,0:T(8,128)} collective-permute-done((f32[2,4,128,512]{3,2,1,0:T(8,128)}, f32[2,4,128,512]{3,2,1,0:T(8,128)}, u32[]{:S(2)}, u32[]{:S(2)}) %collective-permute-start.35) | collective-permute-done | bytes 2097184 | tf_op jit(solution)/shard_map/ppermute | solution.py:359
  425.5 30.3 %shard_map.59 = (f32[4,32,128,512]{3,2,1,0:T(8,128)}, f32[4,1024,512]{2,1,0:T(8,128)}) custom-call(s32[13]{0:T(128)S(1)} %stack.227.keys, f32[32]{0:T(128)S(1)} %copy-done.27, bf16[1024,2048]{1,0:T(8,128)(2,1)} %copy-done, bf16[1024,2048]{1,0:T(8,128)(2,1)} %copy-done.4, f32[1024,128]{1,0:T(8,128)S(1)} %broadcast_in_dim.4.rowd, ...), custom_call_target="tpu_custom_call", output_to_operand_aliasing={{0}: (14, {})} | custom-call | flops 19327352832 | bytes 46137344 | tf_op jit(solution)/shard_map/pallas_call | solution.py:295
  459.2 6.5 %collective-permute-done.39.refs_0_ = f32[2,4,128,512]{3,2,1,0:T(8,128)S(1)} collective-permute-done((f32[2,4,128,512]{3,2,1,0:T(8,128)}, f32[2,4,128,512]{3,2,1,0:T(8,128)S(1)}, u32[]{:S(2)}, u32[]{:S(2)}) %collective-permute-start.39) | collective-permute-done | bytes 2097184 | tf_op jit(solution)/shard_map/ppermute | solution.py:359
  468.1 9.7 %shard_map.61 = (f32[4,32,128,512]{3,2,1,0:T(8,128)}, f32[4,4,128,512]{3,2,1,0:T(8,128)}) custom-call(s32[8]{0:T(128)S(1)} %stack.193.keys, f32[32]{0:T(128)S(1)} %copy-done.27, bf16[1024,2048]{1,0:T(8,128)(2,1)} %copy-done, bf16[1024,2048]{1,0:T(8,128)(2,1)} %copy-done.4, f32[1024,128]{1,0:T(8,128)S(1)} %broadcast_in_dim.4.rowd, ...), custom_call_target="tpu_custom_call", output_to_operand_aliasing={{0}: (10, {})} | custom-call | flops 3221225472 | bytes 20971520 | tf_op jit(solution)/shard_map/pallas_call | solution.py:295
  480.2 8.8 %shard_map.62._ = f32[4,32,128,512]{3,2,1,0:T(8,128)} custom-call(s32[5]{0:T(128)S(1)} %stack.231.keys, f32[32]{0:T(128)S(1)} %copy-done.27, bf16[1024,2048]{1,0:T(8,128)(2,1)S(1)} %copy-done.3, bf16[1024,2048]{1,0:T(8,128)(2,1)} %copy-done.4, f32[1024,128]{1,0:T(8,128)S(1)} %broadcast_in_dim.4.rowd, ...), custom_call_target="tpu_custom_call", output_to_operand_aliasing={{}: (9, {})} | custom-call | flops 3221225472 | bytes 20971520 | tf_op jit(solution)/shard_map/pallas_call | solution.py:295
  489.0 5.3 %shard_map.63 = f32[4,32,128,512]{3,2,1,0:T(8,128)} custom-call(s32[4]{0:T(128)S(1)} %pad_add_fusion.2.keys, f32[4,4,128,512]{3,2,1,0:T(8,128)} %collective-permute-done.43.got, f32[4,32,128,512]{3,2,1,0:T(8,128)} %shard_map.62._), custom_call_target="tpu_custom_call", output_to_operand_aliasing={{}: (2, {})} | custom-call | tf_op jit(solution)/shard_map/pallas_call | solution.py:341
  (199 shorter events, 124.3 us)
Async XLA Ops:
  7.4 49.1 %collective-permute-start.2 = (f32[2,4,128,512]{3,2,1,0:T(8,128)}, f32[2,4,128,512]{3,2,1,0:T(8,128)}, u32[]{:S(2)}, u32[]{:S(2)}) collective-permute-start(f32[2,4,128,512]{3,2,1,0:T(8,128)} %get-tuple-element.302.refs_0_), channel_id=1, source_target_pairs={{0,8},{1,9},{2,10},{3,11},{4,12},{5,13},{6,14},{7,15},{8,0},{9,1},... | collective-permute-start | bytes 6291464 | tf_op jit(solution)/shard_map/ppermute | solution.py:359
  10.1 47.8 %collective-permute-start.3 = (f32[2,4,128,512]{3,2,1,0:T(8,128)}, f32[2,4,128,512]{3,2,1,0:T(8,128)S(1)}, u32[]{:S(2)}, u32[]{:S(2)}) collective-permute-start(f32[2,4,128,512]{3,2,1,0:T(8,128)} %get-tuple-element.302.refs_0_), channel_id=1, source_target_pairs={{0,16},{1,17},{2,18},{3,19},{4,20},{5,21},{6,22},{7,23},{8,24},{9,... | collective-permute-start | bytes 6291464 | tf_op jit(solution)/shard_map/ppermute | solution.py:359
  11.6 48.4 %collective-permute-start.4 = (f32[2,4,128,512]{3,2,1,0:T(8,128)}, f32[2,4,128,512]{3,2,1,0:T(8,128)}, u32[]{:S(2)}, u32[]{:S(2)}) collective-permute-start(f32[2,4,128,512]{3,2,1,0:T(8,128)} %get-tuple-element.302.refs_0_), channel_id=1, source_target_pairs={{0,1},{1,0},{2,3},{3,2},{4,5},{5,4},{6,7},{7,6},{8,9},{9,8},{10,11... | collective-permute-start | bytes 6291464 | tf_op jit(solution)/shard_map/ppermute | solution.py:359
  60.1 54.1 %collective-permute-start.6 = (f32[4,4,128,512]{3,2,1,0:T(8,128)S(1)}, f32[4,4,128,512]{3,2,1,0:T(8,128)S(1)}, u32[]{:S(2)}, u32[]{:S(2)}) collective-permute-start(f32[4,4,128,512]{3,2,1,0:T(8,128)S(1)} %copy-done.9), channel_id=1, source_target_pairs={{0,4},{1,5},{2,6},{3,7},{4,0},{5,1},{6,2},{7,3},{8,12},{9,13},{10,... | collective-permute-start | bytes 12582920 | tf_op jit(solution)/shard_map/ppermute | solution.py:359
  60.6 47.8 %collective-permute-start.9 = (f32[2,4,128,512]{3,2,1,0:T(8,128)S(1)}, f32[2,4,128,512]{3,2,1,0:T(8,128)}, u32[]{:S(2)}, u32[]{:S(2)}) collective-permute-start(f32[2,4,128,512]{3,2,1,0:T(8,128)S(1)} %broadcast_select_fusion.7), channel_id=1, source_target_pairs={{0,1},{1,0},{2,3},{3,2},{4,5},{5,4},{6,7},{7,6},{8,9},{9,8},{10,11... | collective-permute-start | bytes 6291464 | tf_op jit(solution)/shard_map/ppermute | solution.py:359
  62.4 50.4 %collective-permute-start.7 = (f32[2,4,128,512]{3,2,1,0:T(8,128)S(1)}, f32[2,4,128,512]{3,2,1,0:T(8,128)}, u32[]{:S(2)}, u32[]{:S(2)}) collective-permute-start(f32[2,4,128,512]{3,2,1,0:T(8,128)S(1)} %collective-permute-done.3.refs_2_), channel_id=1, source_target_pairs={{0,8},{1,9},{2,10},{3,11},{4,12},{5,13},{6,14},{7,15},{8,0},{9,1},... | collective-permute-start | bytes 6291464 | tf_op jit(solution)/shard_map/ppermute | solution.py:359
  63.2 49.6 %collective-permute-start.8 = (f32[2,4,128,512]{3,2,1,0:T(8,128)S(1)}, f32[2,4,128,512]{3,2,1,0:T(8,128)S(1)}, u32[]{:S(2)}, u32[]{:S(2)}) collective-permute-start(f32[2,4,128,512]{3,2,1,0:T(8,128)S(1)} %shard_map.49.refs_0_), channel_id=1, source_target_pairs={{0,16},{1,17},{2,18},{3,19},{4,20},{5,21},{6,22},{7,23},{8,24},{9,... | collective-permute-start | bytes 6291464 | tf_op jit(solution)/shard_map/ppermute | solution.py:359
  116.1 47.2 %collective-permute-start.13 = (f32[2,4,128,512]{3,2,1,0:T(8,128)}, f32[2,4,128,512]{3,2,1,0:T(8,128)}, u32[]{:S(2)}, u32[]{:S(2)}) collective-permute-start(f32[2,4,128,512]{3,2,1,0:T(8,128)} %get-tuple-element.244), channel_id=1, source_target_pairs={{0,1},{1,0},{2,3},{3,2},{4,5},{5,4},{6,7},{7,6},{8,9},{9,8},{10,11... | collective-permute-start | bytes 6291464 | tf_op jit(solution)/shard_map/ppermute | solution.py:359
  116.7 48.7 %collective-permute-start.11 = (f32[2,4,128,512]{3,2,1,0:T(8,128)}, f32[2,4,128,512]{3,2,1,0:T(8,128)}, u32[]{:S(2)}, u32[]{:S(2)}) collective-permute-start(f32[2,4,128,512]{3,2,1,0:T(8,128)} %copy-done.12), channel_id=1, source_target_pairs={{0,8},{1,9},{2,10},{3,11},{4,12},{5,13},{6,14},{7,15},{8,0},{9,1},... | collective-permute-start | bytes 6291464 | tf_op jit(solution)/shard_map/ppermute | solution.py:359
  117.5 48.1 %collective-permute-start.12 = (f32[2,4,128,512]{3,2,1,0:T(8,128)}, f32[2,4,128,512]{3,2,1,0:T(8,128)}, u32[]{:S(2)}, u32[]{:S(2)}) collective-permute-start(f32[2,4,128,512]{3,2,1,0:T(8,128)} %get-tuple-element.364.refs_0_), channel_id=1, source_target_pairs={{0,16},{1,17},{2,18},{3,19},{4,20},{5,21},{6,22},{7,23},{8,24},{9,... | collective-permute-start | bytes 6291464 | tf_op jit(solution)/shard_map/ppermute | solution.py:359
  169.2 48.2 %collective-permute-start.16 = (f32[2,4,128,512]{3,2,1,0:T(8,128)}, f32[2,4,128,512]{3,2,1,0:T(8,128)}, u32[]{:S(2)}, u32[]{:S(2)}) collective-permute-start(f32[2,4,128,512]{3,2,1,0:T(8,128)} %collective-permute-done.11.refs_1_), channel_id=1, source_target_pairs={{0,16},{1,17},{2,18},{3,19},{4,20},{5,21},{6,22},{7,23},{8,24},{9,... | collective-permute-start | bytes 6291464 | tf_op jit(solution)/shard_map/ppermute | solution.py:359
  170.3 47.9 %collective-permute-start.18 = (f32[2,4,128,512]{3,2,1,0:T(8,128)}, f32[2,4,128,512]{3,2,1,0:T(8,128)}, u32[]{:S(2)}, u32[]{:S(2)}) collective-permute-start(f32[2,4,128,512]{3,2,1,0:T(8,128)} %get-tuple-element.364.refs_0_), channel_id=1, source_target_pairs={{0,8},{1,9},{2,10},{3,11},{4,12},{5,13},{6,14},{7,15},{8,0},{9,1},... | collective-permute-start | bytes 6291464 | tf_op jit(solution)/shard_map/ppermute | solution.py:359
  171.8 47.6 %collective-permute-start.19 = (f32[2,4,128,512]{3,2,1,0:T(8,128)}, f32[2,4,128,512]{3,2,1,0:T(8,128)}, u32[]{:S(2)}, u32[]{:S(2)}) collective-permute-start(f32[2,4,128,512]{3,2,1,0:T(8,128)} %slice_select_fusion), channel_id=1, source_target_pairs={{0,1},{1,0},{2,3},{3,2},{4,5},{5,4},{6,7},{7,6},{8,9},{9,8},{10,11... | collective-permute-start | bytes 6291464 | tf_op jit(solution)/shard_map/ppermute | solution.py:359
  219.5 48.4 %collective-permute-start.22 = (f32[2,4,128,512]{3,2,1,0:T(8,128)}, f32[2,4,128,512]{3,2,1,0:T(8,128)}, u32[]{:S(2)}, u32[]{:S(2)}) collective-permute-start(f32[2,4,128,512]{3,2,1,0:T(8,128)} %broadcast_select_fusion.5.refs_4_), channel_id=1, source_target_pairs={{0,8},{1,9},{2,10},{3,11},{4,12},{5,13},{6,14},{7,15},{8,0},{9,1},... | collective-permute-start | bytes 6291464 | tf_op jit(solution)/shard_map/ppermute | solution.py:359
  220.0 48.1 %collective-permute-start.23 = (f32[2,4,128,512]{3,2,1,0:T(8,128)}, f32[2,4,128,512]{3,2,1,0:T(8,128)}, u32[]{:S(2)}, u32[]{:S(2)}) collective-permute-start(f32[2,4,128,512]{3,2,1,0:T(8,128)} %broadcast_select_fusion.5.refs_4_), channel_id=1, source_target_pairs={{0,16},{1,17},{2,18},{3,19},{4,20},{5,21},{6,22},{7,23},{8,24},{9,... | collective-permute-start | bytes 6291464 | tf_op jit(solution)/shard_map/ppermute | solution.py:359
  220.9 48.6 %collective-permute-start.24 = (f32[2,4,128,512]{3,2,1,0:T(8,128)}, f32[2,4,128,512]{3,2,1,0:T(8,128)}, u32[]{:S(2)}, u32[]{:S(2)}) collective-permute-start(f32[2,4,128,512]{3,2,1,0:T(8,128)} %broadcast_select_fusion.4), channel_id=1, source_target_pairs={{0,1},{1,0},{2,3},{3,2},{4,5},{5,4},{6,7},{7,6},{8,9},{9,8},{10,11... | collective-permute-start | bytes 6291464 | tf_op jit(solution)/shard_map/ppermute | solution.py:359
  269.5 47.2 %collective-permute-start.26 = (f32[2,4,128,512]{3,2,1,0:T(8,128)}, f32[2,4,128,512]{3,2,1,0:T(8,128)}, u32[]{:S(2)}, u32[]{:S(2)}) collective-permute-start(f32[2,4,128,512]{3,2,1,0:T(8,128)} %collective-permute-done.12.refs_2_), channel_id=1, source_target_pairs={{0,8},{1,9},{2,10},{3,11},{4,12},{5,13},{6,14},{7,15},{8,0},{9,1},... | collective-permute-start | bytes 6291464 | tf_op jit(solution)/shard_map/ppermute | solution.py:359
  366.5 50.1 %collective-permute-start.37 = (f32[4,4,128,512]{3,2,1,0:T(8,128)}, f32[4,4,128,512]{3,2,1,0:T(8,128)}, u32[]{:S(2)}, u32[]{:S(2)}) collective-permute-start(f32[4,4,128,512]{3,2,1,0:T(8,128)} %get-tuple-element.383), channel_id=1, source_target_pairs={{0,4},{1,5},{2,6},{3,7},{4,0},{5,1},{6,2},{7,3},{8,12},{9,13},{10,... | collective-permute-start | bytes 12582920 | tf_op jit(solution)/shard_map/ppermute | solution.py:359
  366.6 48.4 %collective-permute-start.35 = (f32[2,4,128,512]{3,2,1,0:T(8,128)}, f32[2,4,128,512]{3,2,1,0:T(8,128)}, u32[]{:S(2)}, u32[]{:S(2)}) collective-permute-start(f32[2,4,128,512]{3,2,1,0:T(8,128)} %broadcast_select_fusion.1.refs_3_), channel_id=1, source_target_pairs={{0,8},{1,9},{2,10},{3,11},{4,12},{5,13},{6,14},{7,15},{8,0},{9,1},... | collective-permute-start | bytes 6291464 | tf_op jit(solution)/shard_map/ppermute | solution.py:359
  367.2 47.9 %collective-permute-start.36 = (f32[2,4,128,512]{3,2,1,0:T(8,128)}, f32[2,4,128,512]{3,2,1,0:T(8,128)S(1)}, u32[]{:S(2)}, u32[]{:S(2)}) collective-permute-start(f32[2,4,128,512]{3,2,1,0:T(8,128)} %broadcast_select_fusion.1.refs_3_), channel_id=1, source_target_pairs={{0,16},{1,17},{2,18},{3,19},{4,20},{5,21},{6,22},{7,23},{8,24},{9,... | collective-permute-start | bytes 6291464 | tf_op jit(solution)/shard_map/ppermute | solution.py:359
  368.5 48.0 %collective-permute-start.38 = (f32[2,4,128,512]{3,2,1,0:T(8,128)}, f32[2,4,128,512]{3,2,1,0:T(8,128)S(1)}, u32[]{:S(2)}, u32[]{:S(2)}) collective-permute-start(f32[2,4,128,512]{3,2,1,0:T(8,128)} %copy-done.36), channel_id=1, source_target_pairs={{0,5},{1,4},{2,7},{3,6},{4,1},{5,0},{6,3},{7,2},{8,13},{9,12},{10,... | collective-permute-start | bytes 6291464 | tf_op jit(solution)/shard_map/ppermute | solution.py:359
  417.9 47.9 %collective-permute-start.39 = (f32[2,4,128,512]{3,2,1,0:T(8,128)}, f32[2,4,128,512]{3,2,1,0:T(8,128)S(1)}, u32[]{:S(2)}, u32[]{:S(2)}) collective-permute-start(f32[2,4,128,512]{3,2,1,0:T(8,128)} %collective-permute-done.31.refs_2_), channel_id=1, source_target_pairs={{0,8},{1,9},{2,10},{3,11},{4,12},{5,13},{6,14},{7,15},{8,0},{9,1},... | collective-permute-start | bytes 6291464 | tf_op jit(solution)/shard_map/ppermute | solution.py:359
  418.6 47.7 %collective-permute-start.40 = (f32[2,4,128,512]{3,2,1,0:T(8,128)}, f32[2,4,128,512]{3,2,1,0:T(8,128)}, u32[]{:S(2)}, u32[]{:S(2)}) collective-permute-start(f32[2,4,128,512]{3,2,1,0:T(8,128)} %collective-permute-done.35.refs_4_), channel_id=1, source_target_pairs={{0,16},{1,17},{2,18},{3,19},{4,20},{5,21},{6,22},{7,23},{8,24},{9,... | collective-permute-start | bytes 6291464 | tf_op jit(solution)/shard_map/ppermute | solution.py:359
  420.0 48.0 %collective-permute-start.41 = (f32[2,4,128,512]{3,2,1,0:T(8,128)}, f32[2,4,128,512]{3,2,1,0:T(8,128)}, u32[]{:S(2)}, u32[]{:S(2)}) collective-permute-start(f32[2,4,128,512]{3,2,1,0:T(8,128)} %get-tuple-element.412), channel_id=1, source_target_pairs={{0,5},{1,4},{2,7},{3,6},{4,1},{5,0},{6,3},{7,2},{8,13},{9,12},{10,... | collective-permute-start | bytes 6291464 | tf_op jit(solution)/shard_map/ppermute | solution.py:359
  (65 other events, 1152.5 us)

commit v5 on v4

--- a/solution.py
+++ b/solution.py
@@ -299,7 +299,7 @@
         ),
         out_shape=out_shape,
         input_output_aliases=alias,
-        compiler_params=pltpu.CompilerParams(vmem_limit_bytes=VMEM if len(sets) > 1 else 3 * VMEM // 4),
+        compiler_params=pltpu.CompilerParams(vmem_limit_bytes=VMEM + 12 * 2**20 if mode in ("mine", "send") else VMEM if len(sets) > 1 else 3 * VMEM // 4),
         cost_estimate=pl.CostEstimate(
             flops=6 * count * size * depth * width // (2 // tiles),
             bytes_accessed=4 * count * (size * (depth + width) + depth * width),

time: 496 us -> 494 us (level)
    unnamed x90 -> x86, local copies, waits for them, and re-layouts: 41 us -> 37.7 us
  transfers between devices with their start and end apart: 44 -> 44, of which waited for: 27 -> 27; matrix products, arithmetic and copies ran while one was open for 5% -> 6% of each run, Pallas kernels for 34% -> 34%
where the time goes in v5:
time: 494 us; the launch traced here: 493 us
  waiting for transfers between devices  207 us (42%)
  Pallas kernels  184 us (37%)
  local copies, waits for them, and re-layouts  40 us (8%)
  starting transfers between devices  36.4 us (7%)
  other arithmetic  25 us (5%)
    ppermute x37, waiting for transfers between devices, hop(): return lax.ppermute(value, AXES, pairs)  202 us
    pallas_call x10, Pallas kernels, product(): pl.pallas_call(functools.partial(product_kernel, chunks, starts, [g.shape...  161 us
    unnamed x86, local copies, waits for them, and re-layouts  37.7 us
    ppermute x37, starting transfers between devices, hop(): return lax.ppermute(value, AXES, pairs)  35.4 us
    select_n x9, other arithmetic, either(): return jnp.where(is_end, at_end, at_mid)  24.5 us
  transfers between devices with their start and end apart: 44, of which 27 were waited for; matrix products, arithmetic and copies ran while one was open for 6% of the time, Pallas kernels for 34%

profile of v5, /device:TPU:0, one launch (start us, length us, event | category | flops | bytes accessed | tf_op | source)
XLA Modules:
  0.0 492.8 jit_solution(10866623726878946750)
XLA Ops:
  23.3 33.3 %collective-permute-done.2.refs_1_ = f32[2,4,128,512]{3,2,1,0:T(8,128)} collective-permute-done((f32[2,4,128,512]{3,2,1,0:T(8,128)}, f32[2,4,128,512]{3,2,1,0:T(8,128)}, u32[]{:S(2)}, u32[]{:S(2)}) %collective-permute-start.2) | collective-permute-done | bytes 2097184 | tf_op jit(solution)/shard_map/ppermute | solution.py:359
  64.7 5.4 %collective-permute-done.10 = f32[2,4,128,512]{3,2,1,0:T(8,128)S(1)} collective-permute-done((f32[2,4,128,512]{3,2,1,0:T(8,128)}, f32[2,4,128,512]{3,2,1,0:T(8,128)S(1)}, u32[]{:S(2)}, u32[]{:S(2)}) %collective-permute-start.10) | collective-permute-done | bytes 2097184 | tf_op jit(solution)/shard_map/ppermute | solution.py:365
  70.1 38.4 %collective-permute-done.9 = f32[2,4,128,512]{3,2,1,0:T(8,128)} collective-permute-done((f32[2,4,128,512]{3,2,1,0:T(8,128)S(1)}, f32[2,4,128,512]{3,2,1,0:T(8,128)}, u32[]{:S(2)}, u32[]{:S(2)}) %collective-permute-start.9) | collective-permute-done | bytes 2097184 | tf_op jit(solution)/shard_map/ppermute | solution.py:359
  108.4 4.4 slice_select_fusion.1
  126.0 22.1 %shard_map.51 = (f32[4,32,128,512]{3,2,1,0:T(8,128)}, f32[2,4,128,512]{3,2,1,0:T(8,128)}) custom-call(s32[3]{0:T(128)S(1)} %fusion.keys, f32[32]{0:T(128)S(1)} %copy-done.27, bf16[1024,2048]{1,0:T(8,128)(2,1)S(1)} %get-tuple-element.415.a_hi, bf16[1024,2048]{1,0:T(8,128)(2,1)S(1)} %get-tuple-element.416.a_lo, ...), custom_call_target="tpu_custom_call", output_to_operand_aliasing={{0}: (10, {})} | custom-call | flops 12884901888 | bytes 29360128 | tf_op jit(solution)/shard_map/pallas_call | solution.py:295
  148.1 15.3 %collective-permute-done.13.refs_0_ = f32[2,4,128,512]{3,2,1,0:T(8,128)} collective-permute-done((f32[2,4,128,512]{3,2,1,0:T(8,128)}, f32[2,4,128,512]{3,2,1,0:T(8,128)}, u32[]{:S(2)}, u32[]{:S(2)}) %collective-permute-start.13) | collective-permute-done | bytes 2097184 | tf_op jit(solution)/shard_map/ppermute | solution.py:359
  172.4 3.6 broadcast_select_fusion.5.refs_4_
  180.3 13.4 %shard_map.52.refs_1_ = f32[2,1024,512]{2,1,0:T(8,128)S(1)} custom-call(s32[3]{0:T(128)S(1)} %fusion.1.keys, f32[32]{0:T(128)S(1)} %copy-done.27, bf16[1024,2048]{1,0:T(8,128)(2,1)S(1)} %copy-done.1, bf16[1024,2048]{1,0:T(8,128)(2,1)S(1)} %copy-done.4, f32[1024,128]{1,0:T(8,128)S(1)} %broadcast_in_dim.4.rowd, f32[1,512]{1,0:T(1,128)S(1)} %bitcast.48, ...), custom_call_target="tpu_custom_call" | custom-call | flops 9663676416 | bytes 23068672 | tf_op jit(solution)/shard_map/pallas_call | solution.py:295
  193.7 4.9 %broadcast_select_fusion.4 = f32[2,4,128,512]{3,2,1,0:T(8,128)} fusion(f32[2,4,128,512]{3,2,1,0:T(8,128)} %collective-permute-done.2.refs_1_, f32[2,4,128,512]{3,2,1,0:T(8,128)} %collective-permute-done.17, pred[]{:T(512)S(6)} %or.3), kind=kLoop, calls=%fused_computation.6 | loop fusion | flops 524288 | bytes 6291457 | tf_op jit(solution)/shard_map/jit(_where)/select_n | solution.py:393
  198.6 18.8 %collective-permute-done.16.refs_3_.refs_0_ = f32[2,4,128,512]{3,2,1,0:T(8,128)} collective-permute-done((f32[2,4,128,512]{3,2,1,0:T(8,128)}, f32[2,4,128,512]{3,2,1,0:T(8,128)}, u32[]{:S(2)}, u32[]{:S(2)}) %collective-permute-start.16) | collective-permute-done | bytes 2097184 | tf_op jit(solution)/shard_map/ppermute | solution.py:359
  226.1 6.9 %shard_map.53 = (bf16[1024,2048]{1,0:T(8,128)(2,1)S(1)}, bf16[1024,2048]{1,0:T(8,128)(2,1)S(1)}) custom-call(s32[1]{0:T(128)} %bitcast.11.chip_ref, f32[2,4,128,512]{3,2,1,0:T(8,128)} %collective-permute-done.13.refs_0_, f32[2,4,128,512]{3,2,1,0:T(8,128)} %collective-permute-done.19.refs_1_, f32[2,4,128,512]{3,2,1,0:T(8,128)S(1)} %copy-done.23, ...), custom_call_target="tpu_custom_call" | custom-call | tf_op jit(solution)/shard_map/pallas_call | solution.py:121
  238.8 4.3 shard_map.54
  245.2 22.6 %collective-permute-done.22.refs_5_ = f32[2,4,128,512]{3,2,1,0:T(8,128)} collective-permute-done((f32[2,4,128,512]{3,2,1,0:T(8,128)}, f32[2,4,128,512]{3,2,1,0:T(8,128)}, u32[]{:S(2)}, u32[]{:S(2)}) %collective-permute-start.22) | collective-permute-done | bytes 2097184 | tf_op jit(solution)/shard_map/ppermute | solution.py:359
  278.6 5.3 %shard_map.55 = (f32[2,4,128,512]{3,2,1,0:T(8,128)S(1)}, f32[2,4,128,512]{3,2,1,0:T(8,128)}) custom-call(s32[3]{0:T(128)S(1)} %add_add_fusion.1.keys, f32[32]{0:T(128)S(1)} %copy-done.27, bf16[1024,2048]{1,0:T(8,128)(2,1)S(1)} %copy-done.29, bf16[1024,2048]{1,0:T(8,128)(2,1)S(1)} %copy-done.32, f32[1024,128]{1,0:T(8,128)S(1)} %broadcast_in_dim.5.rowd, ...), custom_call_target="tpu_custom_call" | custom-call | flops 12884901888 | bytes 29360128 | tf_op jit(solution)/shard_map/pallas_call | solution.py:295
  288.9 7.7 %shard_map.56 = (f32[4,32,128,512]{3,2,1,0:T(8,128)}, f32[2,4,128,512]{3,2,1,0:T(8,128)S(1)}) custom-call(s32[6]{0:T(128)S(1)} %stack.206.keys, f32[32]{0:T(128)S(1)} %copy-done.27, bf16[1024,2048]{1,0:T(8,128)(2,1)S(1)} %copy-done.2, bf16[1024,2048]{1,0:T(8,128)(2,1)S(1)} %copy-done.5, ...), custom_call_target="tpu_custom_call", output_to_operand_aliasing={{0}: (9, {})} | custom-call | flops 3221225472 | bytes 10485760 | tf_op jit(solution)/shard_map/pallas_call | solution.py:295
  296.6 20.2 %collective-permute-done.26.refs_3_ = f32[2,4,128,512]{3,2,1,0:T(8,128)} collective-permute-done((f32[2,4,128,512]{3,2,1,0:T(8,128)}, f32[2,4,128,512]{3,2,1,0:T(8,128)}, u32[]{:S(2)}, u32[]{:S(2)}) %collective-permute-start.26) | collective-permute-done | bytes 2097184 | tf_op jit(solution)/shard_map/ppermute | solution.py:359
  322.3 38.4 %shard_map.57 = (f32[4,32,128,512]{3,2,1,0:T(8,128)}, f32[4,4,128,512]{3,2,1,0:T(8,128)}) custom-call(s32[8]{0:T(128)S(1)} %stack.213.keys, f32[32]{0:T(128)S(1)} %copy-done.27, bf16[1024,2048]{1,0:T(8,128)(2,1)} %copy-done, bf16[1024,2048]{1,0:T(8,128)(2,1)} %copy-done.3, f32[1024,128]{1,0:T(8,128)S(1)} %broadcast_in_dim.4.rowd, ...), custom_call_target="tpu_custom_call", output_to_operand_aliasing={{0}: (15, {})} | custom-call | flops 25769803776 | bytes 58720256 | tf_op jit(solution)/shard_map/pallas_call | solution.py:295
  370.9 19.9 %shard_map.58 = (f32[4,32,128,512]{3,2,1,0:T(8,128)}, f32[4,4,128,512]{3,2,1,0:T(8,128)}) custom-call(s32[11]{0:T(128)S(1)} %stack.220.keys, f32[32]{0:T(128)S(1)} %copy-done.27, bf16[1024,2048]{1,0:T(8,128)(2,1)} %copy-done, bf16[1024,2048]{1,0:T(8,128)(2,1)} %copy-done.3, f32[1024,128]{1,0:T(8,128)S(1)} %broadcast_in_dim.4.rowd, ...), custom_call_target="tpu_custom_call", output_to_operand_aliasing={{0}: (16, {})} | custom-call | flops 25769803776 | bytes 58720256 | tf_op jit(solution)/shard_map/pallas_call | solution.py:295
  390.8 24.2 %collective-permute-done.35.refs_4_ = f32[2,4,128,512]{3,2,1,0:T(8,128)} collective-permute-done((f32[2,4,128,512]{3,2,1,0:T(8,128)}, f32[2,4,128,512]{3,2,1,0:T(8,128)}, u32[]{:S(2)}, u32[]{:S(2)}) %collective-permute-start.35) | collective-permute-done | bytes 2097184 | tf_op jit(solution)/shard_map/ppermute | solution.py:359
  425.3 30.3 %shard_map.59 = (f32[4,32,128,512]{3,2,1,0:T(8,128)}, f32[4,1024,512]{2,1,0:T(8,128)}) custom-call(s32[13]{0:T(128)S(1)} %stack.227.keys, f32[32]{0:T(128)S(1)} %copy-done.27, bf16[1024,2048]{1,0:T(8,128)(2,1)} %copy-done, bf16[1024,2048]{1,0:T(8,128)(2,1)} %copy-done.3, f32[1024,128]{1,0:T(8,128)S(1)} %broadcast_in_dim.4.rowd, ...), custom_call_target="tpu_custom_call", output_to_operand_aliasing={{0}: (14, {})} | custom-call | flops 19327352832 | bytes 46137344 | tf_op jit(solution)/shard_map/pallas_call | solution.py:295
  459.0 6.0 %collective-permute-done.39.refs_0_ = f32[2,4,128,512]{3,2,1,0:T(8,128)} collective-permute-done((f32[2,4,128,512]{3,2,1,0:T(8,128)}, f32[2,4,128,512]{3,2,1,0:T(8,128)}, u32[]{:S(2)}, u32[]{:S(2)}) %collective-permute-start.39) | collective-permute-done | bytes 2097184 | tf_op jit(solution)/shard_map/ppermute | solution.py:359
  467.3 9.9 %shard_map.61 = (f32[4,32,128,512]{3,2,1,0:T(8,128)}, f32[4,4,128,512]{3,2,1,0:T(8,128)}) custom-call(s32[8]{0:T(128)} %stack.193.keys, f32[32]{0:T(128)} %occ.19, bf16[1024,2048]{1,0:T(8,128)(2,1)} %copy-done, bf16[1024,2048]{1,0:T(8,128)(2,1)} %copy-done.3, f32[1024,128]{1,0:T(8,128)} %copy-done.11, ...), custom_call_target="tpu_custom_call", output_to_operand_aliasing={{0}: (10, {})} | custom-call | flops 3221225472 | bytes 20971520 | tf_op jit(solution)/shard_map/pallas_call | solution.py:295
  478.0 9.4 %shard_map.62._ = f32[4,32,128,512]{3,2,1,0:T(8,128)} custom-call(s32[5]{0:T(128)} %stack.231.keys, f32[32]{0:T(128)} %occ.19, bf16[1024,2048]{1,0:T(8,128)(2,1)} %copy-done, bf16[1024,2048]{1,0:T(8,128)(2,1)} %copy-done.3, f32[1024,128]{1,0:T(8,128)} %copy-done.11, f32[1,512]{1,0:T(1,128)} %bitcast.46, ...), custom_call_target="tpu_custom_call", output_to_operand_aliasing={{}: (9, {})} | custom-call | flops 3221225472 | bytes 20971520 | tf_op jit(solution)/shard_map/pallas_call | solution.py:295
  487.5 5.3 %shard_map.63 = f32[4,32,128,512]{3,2,1,0:T(8,128)} custom-call(s32[4]{0:T(128)S(1)} %pad_add_fusion.2.keys, f32[4,4,128,512]{3,2,1,0:T(8,128)} %collective-permute-done.43.got, f32[4,32,128,512]{3,2,1,0:T(8,128)} %shard_map.62._), custom_call_target="tpu_custom_call", output_to_operand_aliasing={{}: (2, {})} | custom-call | tf_op jit(solution)/shard_map/pallas_call | solution.py:341
  (195 shorter events, 122.4 us)
Async XLA Ops:
  7.5 49.1 %collective-permute-start.2 = (f32[2,4,128,512]{3,2,1,0:T(8,128)}, f32[2,4,128,512]{3,2,1,0:T(8,128)}, u32[]{:S(2)}, u32[]{:S(2)}) collective-permute-start(f32[2,4,128,512]{3,2,1,0:T(8,128)} %get-tuple-element.302.refs_0_), channel_id=1, source_target_pairs={{0,8},{1,9},{2,10},{3,11},{4,12},{5,13},{6,14},{7,15},{8,0},{9,1},... | collective-permute-start | bytes 6291464 | tf_op jit(solution)/shard_map/ppermute | solution.py:359
  10.1 47.8 %collective-permute-start.3 = (f32[2,4,128,512]{3,2,1,0:T(8,128)}, f32[2,4,128,512]{3,2,1,0:T(8,128)S(1)}, u32[]{:S(2)}, u32[]{:S(2)}) collective-permute-start(f32[2,4,128,512]{3,2,1,0:T(8,128)} %get-tuple-element.302.refs_0_), channel_id=1, source_target_pairs={{0,16},{1,17},{2,18},{3,19},{4,20},{5,21},{6,22},{7,23},{8,24},{9,... | collective-permute-start | bytes 6291464 | tf_op jit(solution)/shard_map/ppermute | solution.py:359
  11.6 48.4 %collective-permute-start.4 = (f32[2,4,128,512]{3,2,1,0:T(8,128)}, f32[2,4,128,512]{3,2,1,0:T(8,128)}, u32[]{:S(2)}, u32[]{:S(2)}) collective-permute-start(f32[2,4,128,512]{3,2,1,0:T(8,128)} %get-tuple-element.302.refs_0_), channel_id=1, source_target_pairs={{0,1},{1,0},{2,3},{3,2},{4,5},{5,4},{6,7},{7,6},{8,9},{9,8},{10,11... | collective-permute-start | bytes 6291464 | tf_op jit(solution)/shard_map/ppermute | solution.py:359
  60.1 54.1 %collective-permute-start.6 = (f32[4,4,128,512]{3,2,1,0:T(8,128)S(1)}, f32[4,4,128,512]{3,2,1,0:T(8,128)S(1)}, u32[]{:S(2)}, u32[]{:S(2)}) collective-permute-start(f32[4,4,128,512]{3,2,1,0:T(8,128)S(1)} %copy-done.8), channel_id=1, source_target_pairs={{0,4},{1,5},{2,6},{3,7},{4,0},{5,1},{6,2},{7,3},{8,12},{9,13},{10,... | collective-permute-start | bytes 12582920 | tf_op jit(solution)/shard_map/ppermute | solution.py:359
  60.6 47.8 %collective-permute-start.9 = (f32[2,4,128,512]{3,2,1,0:T(8,128)S(1)}, f32[2,4,128,512]{3,2,1,0:T(8,128)}, u32[]{:S(2)}, u32[]{:S(2)}) collective-permute-start(f32[2,4,128,512]{3,2,1,0:T(8,128)S(1)} %broadcast_select_fusion.7), channel_id=1, source_target_pairs={{0,1},{1,0},{2,3},{3,2},{4,5},{5,4},{6,7},{7,6},{8,9},{9,8},{10,11... | collective-permute-start | bytes 6291464 | tf_op jit(solution)/shard_map/ppermute | solution.py:359
  62.4 50.4 %collective-permute-start.7 = (f32[2,4,128,512]{3,2,1,0:T(8,128)S(1)}, f32[2,4,128,512]{3,2,1,0:T(8,128)}, u32[]{:S(2)}, u32[]{:S(2)}) collective-permute-start(f32[2,4,128,512]{3,2,1,0:T(8,128)S(1)} %collective-permute-done.3.refs_2_), channel_id=1, source_target_pairs={{0,8},{1,9},{2,10},{3,11},{4,12},{5,13},{6,14},{7,15},{8,0},{9,1},... | collective-permute-start | bytes 6291464 | tf_op jit(solution)/shard_map/ppermute | solution.py:359
  63.2 49.6 %collective-permute-start.8 = (f32[2,4,128,512]{3,2,1,0:T(8,128)S(1)}, f32[2,4,128,512]{3,2,1,0:T(8,128)S(1)}, u32[]{:S(2)}, u32[]{:S(2)}) collective-permute-start(f32[2,4,128,512]{3,2,1,0:T(8,128)S(1)} %shard_map.49.refs_0_), channel_id=1, source_target_pairs={{0,16},{1,17},{2,18},{3,19},{4,20},{5,21},{6,22},{7,23},{8,24},{9,... | collective-permute-start | bytes 6291464 | tf_op jit(solution)/shard_map/ppermute | solution.py:359
  116.2 47.2 %collective-permute-start.13 = (f32[2,4,128,512]{3,2,1,0:T(8,128)}, f32[2,4,128,512]{3,2,1,0:T(8,128)}, u32[]{:S(2)}, u32[]{:S(2)}) collective-permute-start(f32[2,4,128,512]{3,2,1,0:T(8,128)} %get-tuple-element.244), channel_id=1, source_target_pairs={{0,1},{1,0},{2,3},{3,2},{4,5},{5,4},{6,7},{7,6},{8,9},{9,8},{10,11... | collective-permute-start | bytes 6291464 | tf_op jit(solution)/shard_map/ppermute | solution.py:359
  116.7 48.6 %collective-permute-start.11 = (f32[2,4,128,512]{3,2,1,0:T(8,128)}, f32[2,4,128,512]{3,2,1,0:T(8,128)}, u32[]{:S(2)}, u32[]{:S(2)}) collective-permute-start(f32[2,4,128,512]{3,2,1,0:T(8,128)} %copy-done.12), channel_id=1, source_target_pairs={{0,8},{1,9},{2,10},{3,11},{4,12},{5,13},{6,14},{7,15},{8,0},{9,1},... | collective-permute-start | bytes 6291464 | tf_op jit(solution)/shard_map/ppermute | solution.py:359
  117.5 48.1 %collective-permute-start.12 = (f32[2,4,128,512]{3,2,1,0:T(8,128)}, f32[2,4,128,512]{3,2,1,0:T(8,128)}, u32[]{:S(2)}, u32[]{:S(2)}) collective-permute-start(f32[2,4,128,512]{3,2,1,0:T(8,128)} %get-tuple-element.364.refs_0_), channel_id=1, source_target_pairs={{0,16},{1,17},{2,18},{3,19},{4,20},{5,21},{6,22},{7,23},{8,24},{9,... | collective-permute-start | bytes 6291464 | tf_op jit(solution)/shard_map/ppermute | solution.py:359
  169.2 48.2 %collective-permute-start.16 = (f32[2,4,128,512]{3,2,1,0:T(8,128)}, f32[2,4,128,512]{3,2,1,0:T(8,128)}, u32[]{:S(2)}, u32[]{:S(2)}) collective-permute-start(f32[2,4,128,512]{3,2,1,0:T(8,128)} %collective-permute-done.11.refs_1_), channel_id=1, source_target_pairs={{0,16},{1,17},{2,18},{3,19},{4,20},{5,21},{6,22},{7,23},{8,24},{9,... | collective-permute-start | bytes 6291464 | tf_op jit(solution)/shard_map/ppermute | solution.py:359
  170.3 47.9 %collective-permute-start.18 = (f32[2,4,128,512]{3,2,1,0:T(8,128)}, f32[2,4,128,512]{3,2,1,0:T(8,128)}, u32[]{:S(2)}, u32[]{:S(2)}) collective-permute-start(f32[2,4,128,512]{3,2,1,0:T(8,128)} %get-tuple-element.364.refs_0_), channel_id=1, source_target_pairs={{0,8},{1,9},{2,10},{3,11},{4,12},{5,13},{6,14},{7,15},{8,0},{9,1},... | collective-permute-start | bytes 6291464 | tf_op jit(solution)/shard_map/ppermute | solution.py:359
  171.8 47.6 %collective-permute-start.19 = (f32[2,4,128,512]{3,2,1,0:T(8,128)}, f32[2,4,128,512]{3,2,1,0:T(8,128)}, u32[]{:S(2)}, u32[]{:S(2)}) collective-permute-start(f32[2,4,128,512]{3,2,1,0:T(8,128)} %slice_select_fusion), channel_id=1, source_target_pairs={{0,1},{1,0},{2,3},{3,2},{4,5},{5,4},{6,7},{7,6},{8,9},{9,8},{10,11... | collective-permute-start | bytes 6291464 | tf_op jit(solution)/shard_map/ppermute | solution.py:359
  219.5 48.4 %collective-permute-start.22 = (f32[2,4,128,512]{3,2,1,0:T(8,128)}, f32[2,4,128,512]{3,2,1,0:T(8,128)}, u32[]{:S(2)}, u32[]{:S(2)}) collective-permute-start(f32[2,4,128,512]{3,2,1,0:T(8,128)} %broadcast_select_fusion.5.refs_4_), channel_id=1, source_target_pairs={{0,8},{1,9},{2,10},{3,11},{4,12},{5,13},{6,14},{7,15},{8,0},{9,1},... | collective-permute-start | bytes 6291464 | tf_op jit(solution)/shard_map/ppermute | solution.py:359
  220.0 48.1 %collective-permute-start.23 = (f32[2,4,128,512]{3,2,1,0:T(8,128)}, f32[2,4,128,512]{3,2,1,0:T(8,128)}, u32[]{:S(2)}, u32[]{:S(2)}) collective-permute-start(f32[2,4,128,512]{3,2,1,0:T(8,128)} %broadcast_select_fusion.5.refs_4_), channel_id=1, source_target_pairs={{0,16},{1,17},{2,18},{3,19},{4,20},{5,21},{6,22},{7,23},{8,24},{9,... | collective-permute-start | bytes 6291464 | tf_op jit(solution)/shard_map/ppermute | solution.py:359
  220.9 48.6 %collective-permute-start.24 = (f32[2,4,128,512]{3,2,1,0:T(8,128)}, f32[2,4,128,512]{3,2,1,0:T(8,128)}, u32[]{:S(2)}, u32[]{:S(2)}) collective-permute-start(f32[2,4,128,512]{3,2,1,0:T(8,128)} %broadcast_select_fusion.4), channel_id=1, source_target_pairs={{0,1},{1,0},{2,3},{3,2},{4,5},{5,4},{6,7},{7,6},{8,9},{9,8},{10,11... | collective-permute-start | bytes 6291464 | tf_op jit(solution)/shard_map/ppermute | solution.py:359
  269.5 47.2 %collective-permute-start.26 = (f32[2,4,128,512]{3,2,1,0:T(8,128)}, f32[2,4,128,512]{3,2,1,0:T(8,128)}, u32[]{:S(2)}, u32[]{:S(2)}) collective-permute-start(f32[2,4,128,512]{3,2,1,0:T(8,128)} %collective-permute-done.12.refs_2_), channel_id=1, source_target_pairs={{0,8},{1,9},{2,10},{3,11},{4,12},{5,13},{6,14},{7,15},{8,0},{9,1},... | collective-permute-start | bytes 6291464 | tf_op jit(solution)/shard_map/ppermute | solution.py:359
  366.5 50.2 %collective-permute-start.37 = (f32[4,4,128,512]{3,2,1,0:T(8,128)}, f32[4,4,128,512]{3,2,1,0:T(8,128)}, u32[]{:S(2)}, u32[]{:S(2)}) collective-permute-start(f32[4,4,128,512]{3,2,1,0:T(8,128)} %get-tuple-element.383), channel_id=1, source_target_pairs={{0,4},{1,5},{2,6},{3,7},{4,0},{5,1},{6,2},{7,3},{8,12},{9,13},{10,... | collective-permute-start | bytes 12582920 | tf_op jit(solution)/shard_map/ppermute | solution.py:359
  366.6 48.4 %collective-permute-start.35 = (f32[2,4,128,512]{3,2,1,0:T(8,128)}, f32[2,4,128,512]{3,2,1,0:T(8,128)}, u32[]{:S(2)}, u32[]{:S(2)}) collective-permute-start(f32[2,4,128,512]{3,2,1,0:T(8,128)} %broadcast_select_fusion.1.refs_3_), channel_id=1, source_target_pairs={{0,8},{1,9},{2,10},{3,11},{4,12},{5,13},{6,14},{7,15},{8,0},{9,1},... | collective-permute-start | bytes 6291464 | tf_op jit(solution)/shard_map/ppermute | solution.py:359
  367.2 48.0 %collective-permute-start.36 = (f32[2,4,128,512]{3,2,1,0:T(8,128)}, f32[2,4,128,512]{3,2,1,0:T(8,128)}, u32[]{:S(2)}, u32[]{:S(2)}) collective-permute-start(f32[2,4,128,512]{3,2,1,0:T(8,128)} %broadcast_select_fusion.1.refs_3_), channel_id=1, source_target_pairs={{0,16},{1,17},{2,18},{3,19},{4,20},{5,21},{6,22},{7,23},{8,24},{9,... | collective-permute-start | bytes 6291464 | tf_op jit(solution)/shard_map/ppermute | solution.py:359
  368.6 48.1 %collective-permute-start.38 = (f32[2,4,128,512]{3,2,1,0:T(8,128)}, f32[2,4,128,512]{3,2,1,0:T(8,128)}, u32[]{:S(2)}, u32[]{:S(2)}) collective-permute-start(f32[2,4,128,512]{3,2,1,0:T(8,128)} %copy-done.36), channel_id=1, source_target_pairs={{0,5},{1,4},{2,7},{3,6},{4,1},{5,0},{6,3},{7,2},{8,13},{9,12},{10,... | collective-permute-start | bytes 6291464 | tf_op jit(solution)/shard_map/ppermute | solution.py:359
  416.8 48.2 %collective-permute-start.39 = (f32[2,4,128,512]{3,2,1,0:T(8,128)}, f32[2,4,128,512]{3,2,1,0:T(8,128)}, u32[]{:S(2)}, u32[]{:S(2)}) collective-permute-start(f32[2,4,128,512]{3,2,1,0:T(8,128)} %collective-permute-done.31.refs_2_), channel_id=1, source_target_pairs={{0,8},{1,9},{2,10},{3,11},{4,12},{5,13},{6,14},{7,15},{8,0},{9,1},... | collective-permute-start | bytes 6291464 | tf_op jit(solution)/shard_map/ppermute | solution.py:359
  417.6 47.9 %collective-permute-start.40 = (f32[2,4,128,512]{3,2,1,0:T(8,128)}, f32[2,4,128,512]{3,2,1,0:T(8,128)}, u32[]{:S(2)}, u32[]{:S(2)}) collective-permute-start(f32[2,4,128,512]{3,2,1,0:T(8,128)} %collective-permute-done.35.refs_4_), channel_id=1, source_target_pairs={{0,16},{1,17},{2,18},{3,19},{4,20},{5,21},{6,22},{7,23},{8,24},{9,... | collective-permute-start | bytes 6291464 | tf_op jit(solution)/shard_map/ppermute | solution.py:359
  419.0 48.2 %collective-permute-start.41 = (f32[2,4,128,512]{3,2,1,0:T(8,128)}, f32[2,4,128,512]{3,2,1,0:T(8,128)}, u32[]{:S(2)}, u32[]{:S(2)}) collective-permute-start(f32[2,4,128,512]{3,2,1,0:T(8,128)} %get-tuple-element.412), channel_id=1, source_target_pairs={{0,5},{1,4},{2,7},{3,6},{4,1},{5,0},{6,3},{7,2},{8,13},{9,12},{10,... | collective-permute-start | bytes 6291464 | tf_op jit(solution)/shard_map/ppermute | solution.py:359
  (63 other events, 1441.3 us)
